TPU v7x, 128 devices: a whole 4x4x4 slice. The times are simulated.
128 devices in a mesh: section: 2 (over core), dp: 16 (over y, z), mp: 4 (over x).
Axes of the slice: x: 4, y: 4, z: 4, core: 2. Of those that a mesh axis runs over, the one named last changes fastest.
Arguments:
- inputs: bfloat16 [2, 2048, 768], P(None, 'dp'), may hold values from -6 to 6
- cotangent: bfloat16 [2, 2048, 768], P(None, 'dp'), may hold values from -6 to 6
- segments: int32 [2, 2048], P(None, 'dp'), may hold values from 0 to 2047, as said below
- buckets: int32 [128], replicated, may hold values from 0 to 31
- routes: int32 [2, 2, 2048, 2], P('section', None, 'dp'), may hold values from 0 to 31, all different within a row; in each aligned block of 128 rows (0 to 127, 128 to 255, ..., all dimensions but the last counted through in order) at most 16 rows name the same one
- gates: float32 [2, 2, 2048, 2], P('section', None, 'dp'), may hold values from 0.2 to 0.8
- attn_gain: bfloat16 [2, 768], P('section', 'dp'), may hold values from 0.5 to 1.5
- qkv_weight: bfloat16 [2, 768, 3, 768], P('section', 'dp', None, 'mp'), may hold values from -0.21875 to 0.21875
- out_weight: bfloat16 [2, 768, 768], P('section', 'dp', 'mp'), may hold values from -0.4375 to 0.4375
- rel_bias: bfloat16 [2, 32, 12], P('section', 'dp', 'mp'), may hold values from -4 to 4
- ffn_gain: bfloat16 [2, 768], P('section', 'dp'), may hold values from 0.5 to 1.5
- w_in: bfloat16 [2, 32, 768, 3072], P('section', 'dp', None, 'mp'), may hold values from -0.21875 to 0.21875
- w_out: bfloat16 [2, 32, 3072, 768], P('section', 'dp', 'mp'), may hold values from -0.15625 to 0.15625
Outputs:
- states: bfloat16 [2, 2, 2048, 768], P('section', None, 'dp')
- input_grads: bfloat16 [2, 2, 2048, 768], P('section', None, 'dp')
- attn_gain_grad: float32 [2, 768], P('section', 'dp')
- qkv_grad: float32 [2, 768, 3, 768], P('section', 'dp', None, 'mp')
- out_grad: float32 [2, 768, 768], P('section', 'dp', 'mp')
- rel_bias_grad: float32 [2, 32, 12], P('section', 'dp', 'mp')
- ffn_gain_grad: float32 [2, 768], P('section', 'dp')
- w_in_grad: float32 [2, 32, 768, 3072], P('section', 'dp', None, 'mp')
- w_out_grad: float32 [2, 32, 3072, 768], P('section', 'dp', 'mp')
Inputs may be any that keep to these rules, and one draw needn't show every extreme that they name: `segments`: A token's id is the place of its sequence's first token in the row, so ids never fall along a row; a new sequence begins at every multiple of 128 and at the row's last token. `routes`: A row names two different experts; in each aligned block of 128 rows (one layer, one micro-batch, one index of dp) no expert is named by more than 16 rows.
All inputs are finite; a program needn't handle non-finite values.
Results may differ from a plain program's by a relative error of at most 0.039.
Values may be sent and summed in bfloat16 or wider, within the bound.
No kernel may reach another device: no remote copies, remote signals or barrier semaphores. Data moves between devices by JAX's collectives and lax.ppermute only.
A program may use at most 128 MiB of HBM per device.

v0:
```python
import jax
import jax.numpy as jnp
from jax import lax
from jax.sharding import PartitionSpec as P

epsilon = 1e-06
highest = lax.Precision.HIGHEST
negative = -1e30


def passed_along(x, axis, by):
    size = lax.axis_size(axis)
    pairs = [(i, i + by) for i in range(size) if 0 <= i + by < size]
    return lax.ppermute(x, axis, pairs)


def norm_scale(values):
    return lax.rsqrt(jnp.mean(values * values, axis=-1, keepdims=True) + epsilon)


def norm_back(values, scale, gain, grad):
    inner = jnp.mean(values * gain * grad, axis=-1, keepdims=True)
    return scale * gain * grad - values * scale * scale * scale * inner


def slot_index(route, experts_total, per_device, groups, capacity):
    flat = route.reshape(-1)
    onehot = (flat[:, None] == jnp.arange(experts_total, dtype=jnp.int32)[None, :]).astype(
        jnp.int32
    )
    earlier = jnp.cumsum(onehot, axis=0) - onehot
    position = jnp.sum(earlier * onehot, axis=1)
    target = flat // per_device
    local = flat % per_device
    return (local * groups + target) * capacity + position


def attention_scores(split, bias, mask):
    raw = (
        jnp.einsum("qhe,khe->hqk", split[0], split[1], preferred_element_type=jnp.float32) * 0.125
        + bias
    )
    return jnp.where(mask[None], raw, negative)


def forward_layer(hidden, segment, route, gate, grid, bias, causal, expert_in, expert_out, sizes):
    qkv_full, out_full, gain_one, gain_two = grid
    experts_total, per_device, groups, capacity, heads = sizes
    tokens = hidden.shape[0]
    width = hidden.shape[1]
    scale_one = norm_scale(hidden)
    normed = (hidden * scale_one * gain_one.astype(jnp.float32)).astype(jnp.bfloat16)
    proj = jnp.einsum("td,dcf->ctf", normed, qkv_full, preferred_element_type=jnp.float32).astype(
        jnp.bfloat16
    )
    split = proj.reshape(3, tokens, heads, -1)
    mask = causal & (segment[:, None] == segment[None, :])
    scores = attention_scores(split, bias, mask)
    peak = jnp.max(scores, axis=-1, keepdims=True)
    logsum = peak + jnp.log(jnp.sum(jnp.exp(scores - peak), axis=-1, keepdims=True))
    probs = jnp.exp(scores - logsum).astype(jnp.bfloat16)
    context = jnp.einsum("hqk,khe->qhe", probs, split[2], preferred_element_type=jnp.float32)
    context = context.astype(jnp.bfloat16).reshape(tokens, -1)
    partial_value = jnp.einsum("tf,df->td", context, out_full, preferred_element_type=jnp.float32)
    middle = hidden + lax.psum(partial_value, "mp")
    scale_two = norm_scale(middle)
    normed_two = (middle * scale_two * gain_two.astype(jnp.float32)).astype(jnp.bfloat16)
    slots = slot_index(route, experts_total, per_device, groups, capacity)
    buffer = (
        jnp.zeros((per_device * groups * capacity, width), jnp.bfloat16)
        .at[slots]
        .set(jnp.repeat(normed_two, 2, axis=0))
    )
    received = lax.all_to_all(
        buffer.reshape(per_device, groups, capacity, width),
        "dp",
        split_axis=1,
        concat_axis=1,
        tiled=True,
    )
    received = received.reshape(per_device, groups * capacity, width)
    before = jnp.einsum("erd,edf->erf", received, expert_in, preferred_element_type=jnp.float32)
    active = jax.nn.gelu(before).astype(jnp.bfloat16)
    partial_rows = jnp.einsum(
        "erf,efd->erd", active, expert_out, preferred_element_type=jnp.float32
    )
    partial_rows = partial_rows.reshape(per_device, groups, capacity, width)
    summed = lax.psum(partial_rows, "mp").astype(jnp.bfloat16)
    returned = lax.all_to_all(summed, "dp", split_axis=1, concat_axis=1, tiled=True)
    picked = returned.reshape(-1, width)[slots].reshape(tokens, 2, width).astype(jnp.float32)
    output = middle + jnp.sum(gate[:, :, None] * picked, axis=1)
    kept = (
        hidden,
        scale_one,
        normed,
        proj,
        logsum,
        context,
        middle,
        scale_two,
        received,
        before,
        slots,
    )
    return (output.astype(jnp.bfloat16), kept)


def backward_layer(
    grad_out, kept, segment, gate, grid, bias, causal, onehot_grid, expert_in, expert_out, sizes
):
    hidden, scale_one, normed, proj, logsum, context, middle, scale_two, received, before, slots = (
        kept
    )
    qkv_full, out_full, gain_one, gain_two = grid
    experts_total, per_device, groups, capacity, heads = sizes
    tokens = hidden.shape[0]
    width = hidden.shape[1]
    rows_grad = (gate[:, :, None] * grad_out[:, None, :]).reshape(-1, width)
    buffer = (
        jnp.zeros((per_device * groups * capacity, width), jnp.float32).at[slots].set(rows_grad)
    )
    buffer = buffer.astype(jnp.bfloat16).reshape(per_device, groups, capacity, width)
    arrived = lax.all_to_all(buffer, "dp", split_axis=1, concat_axis=1, tiled=True).reshape(
        per_device, groups * capacity, width
    )
    active, gelu_pull = jax.vjp(jax.nn.gelu, before)
    active_low = active.astype(jnp.bfloat16)
    active_grad = jnp.einsum(
        "erd,efd->erf", arrived, expert_out, preferred_element_type=jnp.float32
    )
    out_expert_grad = jnp.einsum(
        "erf,erd->efd", active_low, arrived, preferred_element_type=jnp.float32
    )
    before_grad = gelu_pull(active_grad)[0].astype(jnp.bfloat16)
    in_expert_grad = jnp.einsum(
        "erd,erf->edf", received, before_grad, preferred_element_type=jnp.float32
    )
    rows_part = jnp.einsum(
        "erf,edf->erd", before_grad, expert_in, preferred_element_type=jnp.float32
    )
    rows_part = rows_part.reshape(per_device, groups, capacity, width)
    rows_back = lax.psum(rows_part, "mp").astype(jnp.bfloat16)
    returned = lax.all_to_all(rows_back, "dp", split_axis=1, concat_axis=1, tiled=True)
    returned = returned.reshape(-1, width)
    normed_two_grad = jnp.sum(returned[slots].reshape(tokens, 2, width).astype(jnp.float32), axis=1)
    gain_two_value = gain_two.astype(jnp.float32)
    gain_two_grad = jnp.sum(normed_two_grad * middle * scale_two, axis=0)
    middle_grad = grad_out + norm_back(middle, scale_two, gain_two_value, normed_two_grad)
    attn_low = middle_grad.astype(jnp.bfloat16)
    out_proj_grad = jnp.einsum("td,tf->df", attn_low, context, preferred_element_type=jnp.float32)
    context_grad = jnp.einsum("td,df->tf", attn_low, out_full, preferred_element_type=jnp.float32)
    context_grad = context_grad.astype(jnp.bfloat16).reshape(tokens, heads, -1)
    split = proj.reshape(3, tokens, heads, -1)
    mask = causal & (segment[:, None] == segment[None, :])
    scores = attention_scores(split, bias, mask)
    probs = jnp.exp(scores - logsum)
    probs_low = probs.astype(jnp.bfloat16)
    value_grad = jnp.einsum(
        "hqk,qhe->khe", probs_low, context_grad, preferred_element_type=jnp.float32
    )
    prob_grad = jnp.einsum(
        "qhe,khe->hqk", context_grad, split[2], preferred_element_type=jnp.float32
    )
    score_grad = (probs * (prob_grad - jnp.sum(probs * prob_grad, axis=-1, keepdims=True))).astype(
        jnp.bfloat16
    )
    table_grad = jnp.einsum(
        "hqk,nqk->nh", score_grad.astype(jnp.float32), onehot_grid, precision=highest
    )
    query_grad = (
        jnp.einsum("hqk,khe->qhe", score_grad, split[1], preferred_element_type=jnp.float32) * 0.125
    )
    key_grad = (
        jnp.einsum("hqk,qhe->khe", score_grad, split[0], preferred_element_type=jnp.float32) * 0.125
    )
    proj_grad = (
        jnp.stack([query_grad, key_grad, value_grad]).reshape(3, tokens, -1).astype(jnp.bfloat16)
    )
    qkv_part_grad = jnp.einsum("td,ctf->dcf", normed, proj_grad, preferred_element_type=jnp.float32)
    normed_part = jnp.einsum("ctf,dcf->td", proj_grad, qkv_full, preferred_element_type=jnp.float32)
    normed_grad = lax.psum(normed_part, "mp")
    gain_one_grad = jnp.sum(normed_grad * hidden * scale_one, axis=0)
    hidden_grad = middle_grad + norm_back(
        hidden, scale_one, gain_one.astype(jnp.float32), normed_grad
    )
    parts = (
        qkv_part_grad,
        out_proj_grad,
        gain_one_grad,
        gain_two_grad,
        table_grad,
        in_expert_grad,
        out_expert_grad,
    )
    return (hidden_grad, parts)


def body(
    inputs,
    cotangent,
    segments,
    buckets,
    routes,
    gates,
    attn_gain,
    qkv_weight,
    out_weight,
    rel_bias,
    ffn_gain,
    w_in,
    w_out,
):
    gathered = (
        lax.all_gather(qkv_weight, "dp", axis=1, tiled=True),
        lax.all_gather(out_weight, "dp", axis=1, tiled=True),
        lax.all_gather(attn_gain, "dp", axis=1, tiled=True),
        lax.all_gather(ffn_gain, "dp", axis=1, tiled=True),
        lax.all_gather(rel_bias, "dp", axis=1, tiled=True),
    )
    grid = (gathered[0][0], gathered[1][0], gathered[2][0], gathered[3][0])
    table = gathered[4][0]
    section = lax.axis_index("section")
    sections = lax.axis_size("section")
    batches = inputs.shape[0]
    tokens = inputs.shape[1]
    width = inputs.shape[2]
    groups = lax.axis_size("dp")
    per_device = w_in.shape[1]
    experts_total = per_device * groups
    capacity = 4 * tokens // experts_total
    sizes = (experts_total, per_device, groups, capacity, table.shape[1])
    expert_in = w_in[0]
    expert_out = w_out[0]
    places = jnp.arange(tokens, dtype=jnp.int32)
    distance = places[:, None] - places[None, :]
    causal = distance >= 0
    bucket_grid = buckets[jnp.clip(distance, 0, tokens - 1)]
    onehot_grid = (
        bucket_grid[None] == jnp.arange(table.shape[0], dtype=jnp.int32)[:, None, None]
    ).astype(jnp.float32)
    bias = jnp.einsum("nqk,nh->hqk", onehot_grid, table.astype(jnp.float32), precision=highest)
    ticks = batches + sections - 1
    arriving = jnp.zeros((tokens, width), jnp.bfloat16)
    results = []
    keeps = []
    for tick in range(ticks):
        batch = jnp.clip(tick - section, 0, batches - 1)
        value = jnp.where(section == 0, inputs[min(tick, batches - 1)], arriving)
        output, kept = forward_layer(
            value.astype(jnp.float32),
            segments[batch],
            routes[0, batch],
            gates[0, batch],
            grid,
            bias,
            causal,
            expert_in,
            expert_out,
            sizes,
        )
        results.append(output)
        keeps.append(kept)
        if tick + 1 < ticks:
            arriving = passed_along(output, "section", 1)
    stacked = jax.tree.map(lambda *items: jnp.stack(items), *keeps)
    result_stack = jnp.stack(results)
    states = jnp.stack([result_stack[number + section] for number in range(batches)])[None]
    last = sections - 1
    coming = jnp.zeros((tokens, width), jnp.bfloat16)
    totals = None
    grads_in = []
    for tick in range(ticks):
        batch = tick - (last - section)
        valid = (batch >= 0) & (batch < batches)
        safe = jnp.clip(batch, 0, batches - 1)
        start = jnp.where(section == last, cotangent[min(tick, batches - 1)], coming)
        start = jnp.where(valid, start, jnp.zeros_like(start)).astype(jnp.float32)
        kept = jax.tree.map(lambda stack: stack[safe + section], stacked)
        hidden_grad, parts = backward_layer(
            start,
            kept,
            segments[safe],
            gates[0, safe],
            grid,
            bias,
            causal,
            onehot_grid,
            expert_in,
            expert_out,
            sizes,
        )
        totals = parts if totals is None else jax.tree.map(jnp.add, totals, parts)
        low_grad = hidden_grad.astype(jnp.bfloat16)
        grads_in.append(low_grad)
        if tick + 1 < ticks:
            coming = passed_along(low_grad, "section", -1)
    grad_stack = jnp.stack(grads_in)
    input_grads = jnp.stack([grad_stack[number + last - section] for number in range(batches)])[
        None
    ]
    (
        qkv_total,
        out_total,
        gain_one_total,
        gain_two_total,
        table_total,
        in_total,
        out_expert_total,
    ) = totals
    reduced = (
        lax.psum_scatter(qkv_total[None], "dp", scatter_dimension=1, tiled=True),
        lax.psum_scatter(out_total[None], "dp", scatter_dimension=1, tiled=True),
        lax.psum_scatter(gain_one_total[None], "dp", scatter_dimension=1, tiled=True),
        lax.psum_scatter(gain_two_total[None], "dp", scatter_dimension=1, tiled=True),
        lax.psum_scatter(table_total[None], "dp", scatter_dimension=1, tiled=True),
    )
    return (
        states,
        input_grads,
        reduced[2],
        reduced[0],
        reduced[1],
        reduced[4],
        reduced[3],
        in_total[None],
        out_expert_total[None],
    )


def solution(mesh):
    return jax.shard_map(
        body,
        mesh=mesh,
        in_specs=(
            P(None, "dp", None),
            P(None, "dp", None),
            P(None, "dp"),
            P(),
            P("section", None, "dp", None),
            P("section", None, "dp", None),
            P("section", "dp"),
            P("section", "dp", None, "mp"),
            P("section", "dp", "mp"),
            P("section", "dp", "mp"),
            P("section", "dp"),
            P("section", "dp", None, "mp"),
            P("section", "dp", "mp", None),
        ),
        out_specs=(
            P("section", None, "dp", None),
            P("section", None, "dp", None),
            P("section", "dp"),
            P("section", "dp", None, "mp"),
            P("section", "dp", "mp"),
            P("section", "dp", "mp"),
            P("section", "dp"),
            P("section", "dp", None, "mp"),
            P("section", "dp", "mp", None),
        ),
        check_vma=False,
    )
```

profile of v0, /device:TPU:1, one launch (start us, length us, event | category | flops | bytes accessed | tf_op | source)
XLA Modules:
  0.0 1208.3 jit_solution(3092323139175706059)
XLA Ops:
  13.4 36.2 %all-reduce.10 = (bf16[768]{0:T(1024)(128)(2,1)}, bf16[768]{0:T(1024)(128)(2,1)S(1)}) all-reduce(bf16[768]{0:T(1024)(128)(2,1)S(1)} %dynamic-update-slice.1, bf16[768]{0:T(1024)(128)(2,1)S(1)} %dynamic-update-slice), channel_id=1, replica_groups=mesh['section'=2,'dp'=16,'mp'=4] {'dp'}, use_global_device_ids=true, to_apply=%add.1 | all-reduce | flops 1536 | bytes 6144
  49.7 14.8 %all_gather.17 = bf16[1,32,3]{2,0,1:T(2,128)(2,1)S(1)} all-gather(bf16[1,2,3]{2,0,1:T(2,128)(2,1)S(1)} %copy.171), channel_id=1, replica_groups=mesh['section'=2,'dp'=16,'mp'=4] {'dp'}, dimensions={1}, use_global_device_ids=true | all-gather | bytes 204 | tf_op jit(solution)/shard_map/all_gather | solution.py:218
  64.5 97.2 %gather_fusion = s32[16384]{0:T(1024)S(1)} fusion(s32[128]{0:T(128)S(1)} %copy-done.1, s32[16384]{0:T(1024)S(1)} %fusion.293), kind=kCustom, calls=%fused_computation | custom fusion | bytes 196608 | tf_op jit(solution)/shard_map/gather | solution.py:237
  162.5 20.6 %all_gather.18 = bf16[1,768,192]{2,1,0:T(8,128)(2,1)} all-gather(bf16[1,48,192]{2,1,0:T(8,128)(2,1)S(1)} %copy-done.108), channel_id=1, replica_groups=mesh['section'=2,'dp'=16,'mp'=4] {'dp'}, dimensions={1}, use_global_device_ids=true | all-gather | bytes 313344 | tf_op jit(solution)/shard_map/all_gather | solution.py:215
  183.1 18.4 %all_gather.16 = bf16[1,768,3,192]{3,1,2,0:T(8,128)(2,1)S(1)} all-gather(bf16[1,48,3,192]{3,1,2,0:T(8,128)(2,1)} %param.20), channel_id=1, replica_groups=mesh['section'=2,'dp'=16,'mp'=4] {'dp'}, dimensions={1}, use_global_device_ids=true | all-gather | bytes 940032 | tf_op jit(solution)/shard_map/all_gather | solution.py:214
  223.9 48.5 %all-reduce.24.cloned.1.call-done = f32[128,768]{1,0:T(8,128)} async-done(((f32[128,768]{1,0:T(8,128)}), f32[128,768]{1,0:T(8,128)}) %all-reduce.24.cloned.1.call-update) | async-done | bytes 393232 | tf_op jit(solution)/shard_map/psum | solution.py:65
  283.1 17.2 %all_to_all.60 = bf16[2,16,16,768]{3,2,0,1:T(8,128)(2,1)S(1)} all-to-all(bf16[2,16,16,768]{3,2,0,1:T(8,128)(2,1)S(1)} %copy.181), channel_id=1, replica_groups=mesh['section'=2,'dp'=16,'mp'=4] {'dp'}, dimensions={1} | all-to-all | bytes 1572864 | tf_op jit(solution)/shard_map/all_to_all | solution.py:74
  304.4 31.7 %all-reduce.37 = bf16[2,16,16,768]{3,2,0,1:T(8,128)(2,1)} all-reduce(f32[2,16,16,768]{3,2,0,1:T(8,128)} %copy.183), channel_id=1, replica_groups=mesh['section'=2,'dp'=16,'mp'=4] {'mp'}, use_global_device_ids=true, to_apply=%region_9.10 | all-reduce | flops 393216 | bytes 2359296 | tf_op jit(solution)/shard_map/psum | solution.py:88
  396.1 33.7 %all-reduce.26.cloned.1.call-done = f32[128,768]{1,0:T(8,128)} async-done(((f32[128,768]{1,0:T(8,128)}), f32[128,768]{1,0:T(8,128)}) %all-reduce.26.cloned.1.call-update) | async-done | bytes 393232 | tf_op jit(solution)/shard_map/psum | solution.py:65
  440.4 17.2 %all_to_all.61 = bf16[2,16,16,768]{3,2,0,1:T(8,128)(2,1)S(1)} all-to-all(bf16[2,16,16,768]{3,2,0,1:T(8,128)(2,1)S(1)} %copy.191), channel_id=1, replica_groups=mesh['section'=2,'dp'=16,'mp'=4] {'dp'}, dimensions={1} | all-to-all | bytes 1572864 | tf_op jit(solution)/shard_map/all_to_all | solution.py:74
  461.7 31.7 %all-reduce.38 = bf16[2,16,16,768]{3,2,0,1:T(8,128)(2,1)} all-reduce(f32[2,16,16,768]{3,2,0,1:T(8,128)} %copy.193), channel_id=1, replica_groups=mesh['section'=2,'dp'=16,'mp'=4] {'mp'}, use_global_device_ids=true, to_apply=%region_20.21 | all-reduce | flops 393216 | bytes 2359296 | tf_op jit(solution)/shard_map/psum | solution.py:88
  522.2 9.8 collective-permute-done.1
  559.4 18.0 %all-reduce.28.cloned.1.call-done = f32[128,768]{1,0:T(8,128)} async-done(((f32[128,768]{1,0:T(8,128)}), f32[128,768]{1,0:T(8,128)}) %all-reduce.28.cloned.1.call-update) | async-done | bytes 393232 | tf_op jit(solution)/shard_map/psum | solution.py:65
  598.7 7.4 all-to-all-done.4
  616.9 31.2 %all-reduce.39 = bf16[2,16,16,768]{3,2,0,1:T(8,128)(2,1)} all-reduce(f32[2,16,16,768]{3,2,0,1:T(8,128)} %copy.211), channel_id=1, replica_groups=mesh['section'=2,'dp'=16,'mp'=4] {'mp'}, use_global_device_ids=true, to_apply=%region_34.35 | all-reduce | flops 393216 | bytes 2359296 | tf_op jit(solution)/shard_map/psum | solution.py:142
  686.6 40.1 %all-reduce.30.cloned.1.call-done = f32[128,768]{1,0:T(8,128)} async-done(((f32[128,768]{1,0:T(8,128)}), f32[128,768]{1,0:T(8,128)}) %all-reduce.30.cloned.1.call-update) | async-done | bytes 393232 | tf_op jit(solution)/shard_map/psum | solution.py:181
  759.3 12.0 all-to-all-done.8
  777.9 32.6 %all-reduce.40 = bf16[2,16,16,768]{3,2,0,1:T(8,128)(2,1)} all-reduce(f32[2,16,16,768]{3,2,0,1:T(8,128)} %copy.219), channel_id=1, replica_groups=mesh['section'=2,'dp'=16,'mp'=4] {'mp'}, use_global_device_ids=true, to_apply=%region_41.42 | all-reduce | flops 393216 | bytes 2359296 | tf_op jit(solution)/shard_map/psum | solution.py:142
  853.2 38.4 %all-reduce.32.cloned.1.call-done = f32[128,768]{1,0:T(8,128)} async-done(((f32[128,768]{1,0:T(8,128)}), f32[128,768]{1,0:T(8,128)}) %all-reduce.32.cloned.1.call-update) | async-done | bytes 393232 | tf_op jit(solution)/shard_map/psum | solution.py:181
  944.9 58.6 %all-reduce.41 = (bf16[2,16,16,768]{3,2,0,1:T(8,128)(2,1)}, bf16[2,16,16,768]{3,2,0,1:T(8,128)(2,1)}) all-reduce(f32[2,16,16,768]{3,2,0,1:T(8,128)} %copy.203, f32[2,16,16,768]{3,2,0,1:T(8,128)} %copy.227), channel_id=1, replica_groups=mesh['section'=2,'dp'=16,'mp'=4] {'mp'}, use_global_device_ids=true, to_apply=%region_31.32 | all-reduce | flops 786432 | bytes 4718592 | tf_op jit(solution)/shard_map/psum | solution.py:88
  1055.6 29.5 %all-reduce.34.cloned.1.call-done = f32[128,768]{1,0:T(8,128)} async-done(((f32[128,768]{1,0:T(8,128)}), f32[128,768]{1,0:T(8,128)}) %all-reduce.34.cloned.1.call-update) | async-done | bytes 393232 | tf_op jit(solution)/shard_map/psum | solution.py:181
  1107.6 8.2 add_bitcast_fusion
  1116.5 60.7 %all-reduce.7 = (f32[1,768]{1,0:T(1,128)S(1)}, f32[1,32,3]{2,0,1:T(1,128)S(1)}, f32[1,768]{1,0:T(1,128)S(1)}) all-reduce(f32[1,768]{1,0:T(1,128)S(1)} %add.853, f32[1,32,3]{2,0,1:T(1,128)S(1)} %copy.237, f32[1,768]{1,0:T(1,128)S(1)} %add.862), channel_id=2, replica_groups=mesh['section'=2,'dp'=16,'mp'=4] {'dp'}, use_global_device_ids=true, to_apply=%region_57.58.clone | all-reduce | flops 1632 | bytes 13056
  1182.7 15.2 %all-reduce.36.cloned.1.call-done = (f32[1,768,3,192]{3,0,2,1:T(1,128)}, f32[1,768,192]{2,0,1:T(1,128)}) async-done(((f32[1,768,3,192]{3,0,2,1:T(1,128)}, f32[1,768,192]{2,0,1:T(1,128)}), (f32[1,768,3,192]{3,0,2,1:T(1,128)}, f32[1,768,192]{2,0,1:T(1,128)})) %all-reduce.36.cloned.1.call-update) | async-done | bytes 2359312
  (595 shorter events, 461.2 us)
Async XLA Ops:
  7.2 294.8 %copy-start = (bf16[1,2,768,768]{3,2,1,0:T(8,128)(2,1)S(1)}, bf16[1,2,768,768]{3,2,1,0:T(8,128)(2,1)}, u32[]{:S(2)}) copy-start(bf16[1,2,768,768]{3,2,1,0:T(8,128)(2,1)} %param.25) | copy-start | bytes 7077892
  7.2 265.2 %all-reduce.24.cloned.1.call-start = ((), (), s32[]{:S(2)}) async-start(), calls=%async_computation.12 | async-start | bytes 786432 | tf_op jit(solution)/shard_map/psum | solution.py:65
  64.5 97.9 %copy-start.108 = (bf16[1,48,192]{2,1,0:T(8,128)(2,1)S(1)}, bf16[1,48,192]{2,1,0:T(8,128)(2,1)}, u32[]{:S(2)}) copy-start(bf16[1,48,192]{2,1,0:T(8,128)(2,1)} %param.21) | copy-start | bytes 55300
  336.1 19.2 %all-to-all-start.1 = ((bf16[2,16,16,768]{3,2,0,1:T(8,128)(2,1)}), bf16[2,16,16,768]{3,2,0,1:T(8,128)(2,1)}, u32[]{:S(2)}, u32[]{:S(2)}) async-start(bf16[2,16,16,768]{3,2,0,1:T(8,128)(2,1)} %all-reduce.37), calls=%async_computation.1 | async-start | bytes 1572864 | tf_op jit(solution)/shard_map/all_to_all | solution.py:89
  340.5 89.2 %all-reduce.26.cloned.1.call-start = ((), (), s32[]{:S(2)}) async-start(), calls=%async_computation.13 | async-start | bytes 786432 | tf_op jit(solution)/shard_map/psum | solution.py:65
  366.9 11.2 collective-permute-start
  493.3 14.9 %all-to-all-start.3 = ((bf16[2,16,16,768]{3,2,0,1:T(8,128)(2,1)}), bf16[2,16,16,768]{3,2,0,1:T(8,128)(2,1)}, u32[]{:S(2)}, u32[]{:S(2)}) async-start(bf16[2,16,16,768]{3,2,0,1:T(8,128)(2,1)} %all-reduce.38), calls=%async_computation.3 | async-start | bytes 1572864 | tf_op jit(solution)/shard_map/all_to_all | solution.py:89
  497.6 79.8 %all-reduce.28.cloned.1.call-start = ((), (), s32[]{:S(2)}) async-start(), calls=%async_computation.14 | async-start | bytes 786432 | tf_op jit(solution)/shard_map/psum | solution.py:65
  520.3 11.8 collective-permute-start.1
  553.5 35.5 %all-to-all-start.6 = ((bf16[2,16,16,768]{3,2,0,1:T(8,128)(2,1)}), bf16[2,16,16,768]{3,2,0,1:T(8,128)(2,1)}, u32[]{:S(2)}, u32[]{:S(2)}) async-start(bf16[2,16,16,768]{3,2,0,1:T(8,128)(2,1)} %copy.209), calls=%async_computation.6 | async-start | bytes 1572864 | tf_op jit(solution)/shard_map/all_to_all | solution.py:123
  589.0 17.1 %all-to-all-start.4 = ((bf16[2,16,16,768]{3,2,0,1:T(8,128)(2,1)}), bf16[2,16,16,768]{3,2,0,1:T(8,128)(2,1)}, u32[]{:S(2)}, u32[]{:S(2)}) async-start(bf16[2,16,16,768]{3,2,0,1:T(8,128)(2,1)} %copy.201), calls=%async_computation.4 | async-start | bytes 1572864 | tf_op jit(solution)/shard_map/all_to_all | solution.py:74
  648.2 16.1 %all-to-all-start.7 = ((bf16[2,16,16,768]{3,2,0,1:T(8,128)(2,1)}), bf16[2,16,16,768]{3,2,0,1:T(8,128)(2,1)}, u32[]{:S(2)}, u32[]{:S(2)}) async-start(bf16[2,16,16,768]{3,2,0,1:T(8,128)(2,1)} %all-reduce.39), calls=%async_computation.7 | async-start | bytes 1572864 | tf_op jit(solution)/shard_map/all_to_all | solution.py:143
  653.9 72.8 %all-reduce.30.cloned.1.call-start = ((), (), s32[]{:S(2)}) async-start(), calls=%async_computation.15 | async-start | bytes 786432 | tf_op jit(solution)/shard_map/psum | solution.py:181
  730.4 8.3 collective-permute-start.2
  749.8 21.5 %all-to-all-start.8 = ((bf16[2,16,16,768]{3,2,0,1:T(8,128)(2,1)}), bf16[2,16,16,768]{3,2,0,1:T(8,128)(2,1)}, u32[]{:S(2)}, u32[]{:S(2)}) async-start(bf16[2,16,16,768]{3,2,0,1:T(8,128)(2,1)} %copy.217), calls=%async_computation.8 | async-start | bytes 1572864 | tf_op jit(solution)/shard_map/all_to_all | solution.py:123
  810.5 18.9 %all-to-all-start.9 = ((bf16[2,16,16,768]{3,2,0,1:T(8,128)(2,1)}), bf16[2,16,16,768]{3,2,0,1:T(8,128)(2,1)}, u32[]{:S(2)}, u32[]{:S(2)}) async-start(bf16[2,16,16,768]{3,2,0,1:T(8,128)(2,1)} %all-reduce.40), calls=%async_computation.9 | async-start | bytes 1572864 | tf_op jit(solution)/shard_map/all_to_all | solution.py:143
  814.8 76.8 %all-reduce.32.cloned.1.call-start = ((), (), s32[]{:S(2)}) async-start(), calls=%async_computation.16 | async-start | bytes 786432 | tf_op jit(solution)/shard_map/psum | solution.py:181
  894.9 11.2 collective-permute-start.3
  916.4 21.8 %all-to-all-start.10 = ((bf16[2,16,16,768]{3,2,0,1:T(8,128)(2,1)}), bf16[2,16,16,768]{3,2,0,1:T(8,128)(2,1)}, u32[]{:S(2)}, u32[]{:S(2)}) async-start(bf16[2,16,16,768]{3,2,0,1:T(8,128)(2,1)} %copy.225), calls=%async_computation.10 | async-start | bytes 1572864 | tf_op jit(solution)/shard_map/all_to_all | solution.py:123
  1003.4 14.9 %all-to-all-start.11 = ((bf16[2,16,16,768]{3,2,0,1:T(8,128)(2,1)}), bf16[2,16,16,768]{3,2,0,1:T(8,128)(2,1)}, u32[]{:S(2)}, u32[]{:S(2)}) async-start(bf16[2,16,16,768]{3,2,0,1:T(8,128)(2,1)} %get-tuple-element.63), calls=%async_computation.11 | async-start | bytes 1572864 | tf_op jit(solution)/shard_map/all_to_all | solution.py:143
  1018.3 27.3 %all-to-all-start.5 = ((bf16[2,16,16,768]{3,2,0,1:T(8,128)(2,1)}), bf16[2,16,16,768]{3,2,0,1:T(8,128)(2,1)}, u32[]{:S(2)}, u32[]{:S(2)}) async-start(bf16[2,16,16,768]{3,2,0,1:T(8,128)(2,1)} %get-tuple-element.62), calls=%async_computation.5 | async-start | bytes 1572864 | tf_op jit(solution)/shard_map/all_to_all | solution.py:89
  1024.0 61.1 %all-reduce.34.cloned.1.call-start = ((), (), s32[]{:S(2)}) async-start(), calls=%async_computation.17 | async-start | bytes 786432 | tf_op jit(solution)/shard_map/psum | solution.py:181
  1042.3 155.6 %all-reduce.36.cloned.1.call-start = ((), (), s32[]{:S(2)}) async-start(), calls=%async_computation.18 | async-start | bytes 6291456
  1107.6 71.3 %copy-start.64 = (bf16[128,768]{1,0:T(8,128)(2,1)S(1)}, bf16[128,768]{1,0:T(8,128)(2,1)}, u32[]{:S(2)}) copy-start(bf16[128,768]{1,0:T(8,128)(2,1)} %copy-done.63) | copy-start | bytes 589828
  (130 other events, 839.6 us)
Sparse Core Ops, SparseCore 0:
  211.1 61.2 all-reduce.23
  385.4 44.2 all-reduce.25
  537.6 39.6 all-reduce.27
  682.2 44.3 all-reduce.29
  847.9 43.6 all-reduce.31
  1042.4 42.5 all-reduce.33
  1099.5 98.4 all-reduce.35
where the time goes:
time: 1220 us; the launch traced here: 1210 us
  blocking collectives  371 us (30%)
  local copies, waits for them, and re-layouts  272 us (22%)
  waiting for transfers between devices  271 us (22%)
  other arithmetic  129 us (11%)
  matrix products  77.9 us (6%)
  starting transfers between devices  68.6 us (6%)
  between operations  18.3 us (2%)
    psum x3, blocking collectives, forward_layer(): summed = lax.psum(partial_rows, 'mp').astype(jnp.bfloat16)  122 us
    psum x3, waiting for transfers between devices, backward_layer(): normed_grad = lax.psum(normed_part, 'mp')  108 us
    psum x3, waiting for transfers between devices, forward_layer(): middle = hidden + lax.psum(partial_value, 'mp')  100 us
    gather x2, local copies, waits for them, and re-layouts, body(): bucket_grid = buckets[jnp.clip(distance, 0, tokens - 1)]  97.9 us
    unnamed x2, blocking collectives  96.9 us
    psum x2, blocking collectives, backward_layer(): rows_back = lax.psum(rows_part, 'mp').astype(jnp.bfloat16)  63.8 us
    all_to_all x2, blocking collectives, forward_layer(): lax.all_to_all(buffer.reshape(per_device, groups, capacity, width), 'dp',...  34.4 us
    another operation x21, other arithmetic, body(): stacked = jax.tree.map(lambda *items: jnp.stack(items), *keeps)  27.5 us
  transfers between devices with their start and end apart: 21, of which 14 were waited for; matrix products, arithmetic and copies ran while one was open for 16% of the time, Pallas kernels for 0%

commit v1 on v0

v1 whole, which is shorter than its diff:
```python
import functools

import jax
import jax.numpy as jnp
from jax import lax
from jax.experimental import pallas as pl
from jax.experimental.pallas import tpu as pltpu
from jax.sharding import PartitionSpec as P

bf16 = jnp.bfloat16
f32 = jnp.float32
epsilon = 1e-06
negative = -1e30
root = 0.7978845608028654
cubic = 0.044715
TOK = 128
WIDTH = 768
HEADS = 3
DH = 64
SPLIT = 192
PACK = 896
SLOTS = 512
CAP = 16


def dot(a, b):
    return lax.dot_general(a, b, (((1,), (0,)), ((), ())), preferred_element_type=f32)


def dot_nt(a, b):
    return lax.dot_general(a, b, (((1,), (1,)), ((), ())), preferred_element_type=f32)


def dot_tn(a, b):
    return lax.dot_general(a, b, (((0,), (0,)), ((), ())), preferred_element_type=f32)


def iota(shape, dim):
    return lax.broadcasted_iota(jnp.int32, shape, dim)


def norm_scale(values):
    return lax.rsqrt(jnp.mean(values * values, axis=-1, keepdims=True) + epsilon)


def swapped(x):
    return lax.ppermute(x, "section", [(0, 1), (1, 0)])


def sent(x, source):
    return lax.ppermute(x, "section", [(source, 1 - source)])


def call(kernel, outs, any_args=(), scalars=1, scratch=(), args=(), name=None):
    specs = []
    for index in range(len(args)):
        if index < scalars:
            specs.append(pl.BlockSpec(memory_space=pltpu.SMEM))
        elif index in any_args:
            specs.append(pl.BlockSpec(memory_space=pl.ANY))
        else:
            specs.append(pl.BlockSpec(memory_space=pltpu.VMEM))
    return pl.pallas_call(
        kernel,
        out_shape=[jax.ShapeDtypeStruct(shape, dtype) for shape, dtype in outs],
        in_specs=specs,
        out_specs=[pl.BlockSpec(memory_space=pltpu.VMEM) for _ in outs],
        scratch_shapes=list(scratch),
        compiler_params=pltpu.CompilerParams(vmem_limit_bytes=48 * 1024 * 1024),
        name=name,
    )(*args)


def fetch(here, own, other, buffer, sems):
    count = buffer.shape[0]

    @pl.when(here)
    def _():
        for i in range(count):
            pltpu.make_async_copy(own.at[i], buffer.at[i], sems.at[i]).start()

    @pl.when(jnp.logical_not(here))
    def _():
        for i in range(count):
            pltpu.make_async_copy(other.at[i], buffer.at[i], sems.at[i]).start()

    def arrived(i):
        pltpu.make_async_copy(own.at[i], buffer.at[i], sems.at[i]).wait()

    return arrived


def prepare_kernel(ids, own, other, segments, cotangent, pick, gated, mask, sent_grad):
    section = ids[0]
    first = section == 0
    row = jnp.where(first, segments[0:1, :], segments[1:2, :]).astype(f32)
    column = own[:, 0:1]
    causal = iota((TOK, TOK), 0) >= iota((TOK, TOK), 1)
    mask[...] = jnp.where(causal & (column == row), 1.0, 0.0)
    expert = iota((TOK, 32), 1).astype(f32)
    lower = jnp.where(iota((TOK, TOK), 0) > iota((TOK, TOK), 1), 1.0, 0.0).astype(bf16)
    spread = jnp.where(lax.shift_right_logical(iota((32, SLOTS), 1), 4) == iota((32, SLOTS), 0), 1.0, 0.0).astype(bf16)
    slot = iota((TOK, SLOTS), 1)
    slot_expert = lax.shift_right_logical(slot, 4).astype(f32)
    slot_place = (slot & 15).astype(f32)
    for layer in range(2):
        info = jnp.where(section == layer, own[...], other[...])
        r0, r1, g0, g1 = info[:, 1:2], info[:, 2:3], info[:, 3:4], info[:, 4:5]
        named = jnp.where((r0 == expert) | (r1 == expert), 1.0, 0.0).astype(bf16)
        earlier = dot(lower, named)
        here = dot(earlier.astype(bf16), spread) == slot_place
        d0 = here & (r0 == slot_expert)
        d1 = here & (r1 == slot_expert)
        pick[layer] = jnp.where(d0 | d1, 1.0, 0.0).astype(bf16)
        gates = jnp.where(d0, g0, jnp.where(d1, g1, 0.0)).astype(bf16)
        gated[layer] = gates
        if layer == 1:
            grad = jnp.where(first, cotangent[0], cotangent[1])
            sent_grad[...] = dot_tn(gates, grad).astype(bf16)


def gains(chunk):
    rows = chunk.astype(f32).T
    return rows[0:1], rows[1:2]


def attend(count, arrived, weights, normed, onehot, allowed, proj_out, probs_out, context_out):
    total = None
    for part in range(count):
        arrived(part)
        proj = dot(normed, weights[part, :, : 3 * SPLIT]).astype(bf16)
        proj_out[part] = proj
        line = dot_tn(weights[part, :, WIDTH:], onehot).astype(bf16)
        pieces = []
        for head in range(HEADS):
            at = head * DH
            query = proj[:, at : at + DH]
            key = proj[:, SPLIT + at : SPLIT + at + DH]
            value = proj[:, 2 * SPLIT + at : 2 * SPLIT + at + DH]
            chosen = jnp.where(iota((TOK, TOK), 1) == 2 + head, 1.0, 0.0).astype(bf16)
            bias = pltpu.roll(dot(chosen, line), 0, 1, stride=1, stride_axis=0)
            scores = jnp.where(allowed, dot_nt(query, key) * 0.125 + bias, negative)
            peak = jnp.max(scores, axis=-1, keepdims=True)
            expos = jnp.exp(scores - peak)
            probs = (expos / jnp.sum(expos, axis=-1, keepdims=True)).astype(bf16)
            probs_out[part * HEADS + head] = probs
            pieces.append(dot(probs, value).astype(bf16))
        context = jnp.concatenate(pieces, axis=1)
        context_out[part] = context
        padded = jnp.concatenate([jnp.zeros((TOK, DH), bf16), context], axis=1)
        term = dot_nt(padded, weights[part, :, 512:WIDTH])
        total = term if total is None else total + term
    return total


def forward_kernel(layer, ids, *refs):
    if layer == 0:
        inputs, own, other, onehot, mask, pick = refs[:6]
        rest = refs[6:]
    else:
        before, parts, own, other, onehot, mask, pick = refs[:7]
        rest = refs[7:]
        state_out, rest = rest[0], rest[1:]
    sent_out, middle_out, normed_out, proj_out, probs_out, context_out, weights, sems = rest
    section = ids[0]
    arrived = fetch(section == layer, own, other, weights, sems)
    if layer == 0:
        hidden = jnp.where(section == 0, inputs[0], inputs[1]).astype(f32)
    else:
        added = parts[0].astype(f32)
        for i in range(1, 4):
            added = added + parts[i].astype(f32)
        state = (before[...] + added).astype(bf16)
        state_out[...] = state
        hidden = state.astype(f32)
    scaled = hidden * norm_scale(hidden)
    arrived_first = arrived

    arrived_first(0)
    gain_one, gain_two = gains(weights[0, :, WIDTH:])

    def wait(part):
        if part > 0:
            arrived(part)

    normed = (scaled * gain_one).astype(bf16)
    normed_out[...] = normed
    allowed = mask[...] > 0.5
    attn = attend(4, wait, weights, normed, onehot[...], allowed, proj_out, probs_out, context_out)
    middle = hidden + attn
    middle_out[...] = middle
    normed_two = (middle * norm_scale(middle) * gain_two).astype(bf16)
    sent_out[...] = dot_tn(pick[layer], normed_two).astype(bf16)


def gelu_both(x):
    square = x * x
    th = jnp.tanh(root * (x + cubic * x * square))
    half = 0.5 * (1.0 + th)
    value = x * half
    slope = half + 0.5 * x * (1.0 - th * th) * (root * (1.0 + 3.0 * cubic * square))
    return value, slope


def rows_of(ref, expert):
    return ref[:, expert].reshape(256, WIDTH)


def expert_kernel(mode, layer, ids, *refs):
    if mode == "forward":
        received, in_own, in_other, out_own, out_other, y_out, act_out, slope_out = refs[:8]
    elif mode == "both":
        received, arrived_grad, in_own, in_other, out_own, out_other, y_out, buf_out, act_out, pre_out = refs[:10]
    else:
        arrived_grad, slope_in, in_own, in_other, out_own, out_other, buf_out, pre_out = refs[:8]
    w_in, w_out, in_sems, out_sems = refs[-4:]
    here = ids[0] == layer
    in_arrived = fetch(here, in_own, in_other, w_in, in_sems)
    out_arrived = fetch(here, out_own, out_other, w_out, out_sems)
    for e in range(2):
        in_arrived(e)
        if mode != "backward":
            value, slope = gelu_both(dot(rows_of(received, e), w_in[e]))
            act = value.astype(bf16)
            act_out[e] = act
            out_arrived(e)
            y_out[:, e] = dot(act, w_out[e]).astype(bf16).reshape(16, CAP, WIDTH)
            if mode == "forward":
                slope_out[e] = slope.astype(bf16)
        else:
            out_arrived(e)
            slope = slope_in[e].astype(f32)
        if mode != "forward":
            pre = (dot_nt(rows_of(arrived_grad, e), w_out[e]) * slope).astype(bf16)
            pre_out[e] = pre
            buf_out[:, e] = dot_nt(pre, w_in[e]).astype(bf16).reshape(16, CAP, WIDTH)


def combine_kernel(layer, matrix, returned, out):
    out[...] = dot(matrix[layer], returned[...]).astype(bf16)


def state_kernel(before, parts, out):
    added = parts[0].astype(f32)
    for i in range(1, 4):
        added = added + parts[i].astype(f32)
    out[...] = (before[...] + added).astype(bf16)


def backward_kernel(layer, ids, *refs):
    if layer == 1:
        grads, hidden_ref = refs[0], refs[1]
    else:
        grads, hidden_ref = refs[0], refs[1]
    parts, middle_ref, proj_ref, probs_ref, own, other, onehot = refs[2:9]
    rest = refs[9:]
    if layer == 1:
        gated, rest = rest[0], rest[1:]
    grad_out, rest = rest[0], rest[1:]
    if layer == 1:
        sent_out, rest = rest[0], rest[1:]
    attn_out, proj_grad_out, small_out, weights, all_proj, all_scores, sems = rest
    section = ids[0]
    device = ids[1]
    arrived = fetch(section == layer, own, other, weights, sems)
    first = section == 0
    if layer == 1:
        grad = jnp.where(first, grads[0], grads[1]).astype(f32)
        hidden = hidden_ref[...].astype(f32)
    else:
        grad = grads[...].astype(f32)
        hidden = jnp.where(first, hidden_ref[0], hidden_ref[1]).astype(f32)
    middle = middle_ref[...]
    buf = parts[0].astype(f32)
    for i in range(1, 4):
        buf = buf + parts[i].astype(f32)
    scale_two = norm_scale(middle)
    arrived(0)
    gain_one, gain_two = gains(weights[0, :, WIDTH:])
    small_out[...] = jnp.zeros(small_out.shape, f32)
    unit = middle * scale_two
    small_out[1:2, :] = jnp.sum(buf * unit, axis=0, keepdims=True)
    inner = jnp.mean(unit * gain_two * buf, axis=-1, keepdims=True)
    middle_grad = grad + scale_two * (gain_two * buf - unit * inner)
    attn_low = middle_grad.astype(bf16)
    attn_out[...] = attn_low
    normed_grad = None
    for part in range(4):
        if part > 0:
            arrived(part)
        context_grad = dot(attn_low, weights[part, :, 512:WIDTH]).astype(bf16)
        proj = proj_ref[part]
        q_parts, k_parts, v_parts = [], [], []
        for head in range(HEADS):
            at = head * DH
            query = proj[:, at : at + DH]
            key = proj[:, SPLIT + at : SPLIT + at + DH]
            value = proj[:, 2 * SPLIT + at : 2 * SPLIT + at + DH]
            probs = probs_ref[part * HEADS + head]
            back = context_grad[:, DH + at : DH + at + DH]
            wide = probs.astype(f32)
            prob_grad = dot_nt(back, value)
            inner = jnp.sum(wide * prob_grad, axis=-1, keepdims=True)
            score_grad = (wide * (prob_grad - inner)).astype(bf16)
            all_scores[part * HEADS + head] = score_grad
            q_parts.append(dot(score_grad, key) * 0.125)
            k_parts.append(dot_tn(score_grad, query) * 0.125)
            v_parts.append(dot_tn(probs, back))
        proj_grad = jnp.concatenate(q_parts + k_parts + v_parts, axis=1).astype(bf16)
        all_proj[part] = proj_grad
        term = dot_nt(proj_grad, weights[part, :, : 3 * SPLIT])
        normed_grad = term if normed_grad is None else normed_grad + term
    scale_one = norm_scale(hidden)
    unit = hidden * scale_one
    small_out[0:1, :] = jnp.sum(normed_grad * unit, axis=0, keepdims=True)
    inner = jnp.mean(unit * gain_one * normed_grad, axis=-1, keepdims=True)
    low = (middle_grad + scale_one * (gain_one * normed_grad - unit * inner)).astype(bf16)
    grad_out[...] = low
    if layer == 1:
        sent_out[...] = dot_tn(gated[0], low).astype(bf16)
    proj_grad_out[...] = all_proj[device]
    flip = jnp.where(iota((TOK, TOK), 0) + iota((TOK, TOK), 1) == TOK - 1, 1.0, 0.0).astype(bf16)
    for head in range(HEADS):
        flipped = dot(flip, all_scores[device * HEADS + head])
        lined = pltpu.roll(flipped, 1, 1, stride=1, stride_axis=0)
        small_out[2 + head : 3 + head, 0:TOK] = jnp.sum(lined, axis=0, keepdims=True)


def weight_grad_kernel(ids, *refs):
    layers = (refs[0:10], refs[10:20])
    onehot, out = refs[20], refs[21]
    section = ids[0]
    device = ids[1]
    for layer in range(2):

        @pl.when(section == layer)
        def _(layer=layer):
            normed, proj_grad, attn, context, small, normed2, proj_grad2, attn2, context2, small2 = layers[layer]
            out[:, : 3 * SPLIT] = (
                dot_tn(normed[...], proj_grad[...]) + dot_tn(normed2[...], proj_grad2[...])
            ).astype(bf16)
            out[:, 3 * SPLIT : WIDTH] = (
                dot_tn(attn[...], context[device]) + dot_tn(attn2[...], context2[device])
            ).astype(bf16)
            rows = small[...] + small2[...]
            lines = rows[:, 0:TOK].astype(bf16)
            keep = (iota((TOK, 16), 1) >= 2) & (iota((TOK, 16), 1) < 5) & (iota((TOK, 16), 0) == iota((TOK, 16), 1))
            lines = dot(jnp.where(keep, 1.0, 0.0).astype(bf16), lines).astype(bf16)
            table = dot_nt(onehot[...], lines)
            tall = jnp.concatenate([rows, jnp.zeros((TOK - 16, WIDTH), f32)], axis=0).T
            lane = iota((WIDTH, TOK), 1)
            out[:, WIDTH:] = jnp.where(lane < 2, tall, table).astype(bf16)


def sum_kernel(received, out):
    total = received[0].astype(f32)
    for i in range(1, received.shape[0]):
        total = total + received[i].astype(f32)
    out[...] = total


def expert_grad_kernel(ids, *refs):
    layers = (refs[0:8], refs[8:16])
    in_out, out_out = refs[16], refs[17]
    buffers = refs[18:26]
    sems = refs[26]
    expert = pl.program_id(0)
    section = ids[0]

    @pl.when(expert == 0)
    def _():
        for layer in range(2):

            @pl.when(section == layer)
            def _(layer=layer):
                for i in range(8):
                    pltpu.make_async_copy(layers[layer][i], buffers[i], sems.at[i]).start()

        for i in range(8):
            pltpu.make_async_copy(layers[0][i], buffers[i], sems.at[i]).wait()

    received, act, pre, arrived, received2, act2, pre2, arrived2 = buffers
    rows = received[:, expert].reshape(256, WIDTH)
    rows2 = received2[:, expert].reshape(256, WIDTH)
    in_out[0] = dot_tn(rows, pre[expert]) + dot_tn(rows2, pre2[expert])
    grads = arrived[:, expert].reshape(256, WIDTH)
    grads2 = arrived2[:, expert].reshape(256, WIDTH)
    out_out[0] = dot_tn(act[expert], grads) + dot_tn(act2[expert], grads2)


def exchanged(x):
    return lax.all_to_all(x.reshape(16, -1, x.shape[-1]), "dp", 0, 0, tiled=True)


def gathered_mp(x):
    return lax.all_gather(x, "mp", axis=0)


def body(
    inputs, cotangent, segments, buckets, routes, gates, attn_gain, qkv_weight, out_weight, rel_bias, ffn_gain, w_in, w_out
):
    section = lax.axis_index("section")
    ids = jnp.stack([section, lax.axis_index("mp")]).astype(jnp.int32)
    pack = jnp.concatenate(
        [
            qkv_weight.reshape(48, 3 * SPLIT),
            out_weight.reshape(48, SPLIT),
            attn_gain.reshape(48, 1),
            ffn_gain.reshape(48, 1),
            jnp.pad(rel_bias[0], ((0, 46), (0, 0))),
            jnp.zeros((48, PACK - WIDTH - 5), bf16),
        ],
        axis=1,
    )
    w_own = lax.all_gather(pack, ("mp", "dp"), axis=0).reshape(4, WIDTH, PACK)
    w_other = swapped(w_own)
    in_own, out_own = w_in[0], w_out[0]
    in_other, out_other = swapped(in_own), swapped(out_own)
    info = jnp.concatenate(
        [segments.astype(f32)[:, :, None], routes[0].astype(f32), gates[0], jnp.zeros((2, TOK, 3), f32)], axis=2
    )
    info_own = lax.dynamic_index_in_dim(info, section, 0, False)
    info_other = swapped(lax.dynamic_index_in_dim(info, 1 - section, 0, False))
    reverse = jnp.concatenate([buckets[0:1], buckets[1:][::-1]])
    place = jnp.arange(WIDTH, dtype=jnp.int32)
    number = jnp.where(place % 48 < 2, 2 * (place // 48) + place % 48, -1)
    onehot = (number[:, None] == reverse[None, :]).astype(bf16)

    pick, gated, mask, grad_sent = call(
        prepare_kernel,
        [((2, TOK, SLOTS), bf16), ((2, TOK, SLOTS), bf16), ((TOK, TOK), f32), ((SLOTS, WIDTH), bf16)],
        args=(ids, info_own, info_other, segments, cotangent),
        name="prepare",
    )
    blocks = (16, 2, CAP, WIDTH)
    arrived_one = exchanged(grad_sent).reshape(blocks)

    kept_shapes = [
        ((SLOTS, WIDTH), bf16),
        ((TOK, WIDTH), f32),
        ((TOK, WIDTH), bf16),
        ((4, TOK, 3 * SPLIT), bf16),
        ((12, TOK, TOK), bf16),
        ((4, TOK, SPLIT), bf16),
    ]
    weight_scratch = [pltpu.VMEM((4, WIDTH, PACK), bf16)]
    sems4 = [pltpu.SemaphoreType.DMA((4,))]
    sent_zero, middle_zero, normed_zero, proj_zero, probs_zero, context_zero = call(
        functools.partial(forward_kernel, 0),
        kept_shapes,
        any_args=(2, 3),
        scratch=weight_scratch + sems4,
        args=(ids, inputs, w_own, w_other, onehot, mask, pick),
        name="attention_zero",
    )
    received_zero = exchanged(sent_zero).reshape(blocks)
    expert_scratch = [
        pltpu.VMEM((2, WIDTH, WIDTH), bf16),
        pltpu.VMEM((2, WIDTH, WIDTH), bf16),
        pltpu.SemaphoreType.DMA((2,)),
        pltpu.SemaphoreType.DMA((2,)),
    ]
    hidden_shape = ((2, 256, WIDTH), bf16)
    y_zero, act_zero, slope_zero = call(
        functools.partial(expert_kernel, "forward", 0),
        [(blocks, bf16), hidden_shape, hidden_shape],
        any_args=(2, 3, 4, 5),
        scratch=expert_scratch,
        args=(ids, received_zero, in_own, in_other, out_own, out_other),
        name="experts_zero",
    )
    token_shape = ((TOK, WIDTH), bf16)

    def combined(layer, matrix, rows, name):
        back = exchanged(rows).reshape(SLOTS, WIDTH)
        part = call(
            functools.partial(combine_kernel, layer), [token_shape], scalars=0, args=(matrix, back), name=name
        )[0]
        return gathered_mp(part)

    parts_zero = combined(0, gated, y_zero, "combine_zero")
    state_zero, sent_one, middle_one, normed_one, proj_one, probs_one, context_one = call(
        functools.partial(forward_kernel, 1),
        [token_shape] + kept_shapes,
        any_args=(3, 4),
        scratch=weight_scratch + sems4,
        args=(ids, middle_zero, parts_zero, w_own, w_other, onehot, mask, pick),
        name="attention_one",
    )
    received_one = exchanged(sent_one).reshape(blocks)
    y_one, buf_one, act_one, pre_one = call(
        functools.partial(expert_kernel, "both", 1),
        [(blocks, bf16), (blocks, bf16), hidden_shape, hidden_shape],
        any_args=(3, 4, 5, 6),
        scratch=expert_scratch,
        args=(ids, received_one, arrived_one, in_own, in_other, out_own, out_other),
        name="experts_one",
    )
    buf_parts_one = combined(1, pick, buf_one, "combine_back_one")
    y_parts_one = combined(1, gated, y_one, "combine_one")
    state_one = call(
        state_kernel, [token_shape], scalars=0, args=(middle_one, y_parts_one), name="state_one"
    )[0]
    grad_scratch = weight_scratch + [pltpu.VMEM((4, TOK, 3 * SPLIT), bf16), pltpu.VMEM((12, TOK, TOK), bf16)] + sems4
    grad_shapes = [token_shape, ((TOK, 3 * SPLIT), bf16), ((16, WIDTH), f32)]
    grad_one, grad_sent_zero, attn_grad_one, proj_grad_one, small_one = call(
        functools.partial(backward_kernel, 1),
        [token_shape, ((SLOTS, WIDTH), bf16)] + grad_shapes,
        any_args=(7, 8),
        scratch=grad_scratch,
        args=(
            ids, cotangent, state_zero, buf_parts_one, middle_one, proj_one, probs_one, w_own, w_other, onehot, gated
        ),
        name="attention_back_one",
    )
    arrived_zero = exchanged(grad_sent_zero).reshape(blocks)
    buf_zero, pre_zero = call(
        functools.partial(expert_kernel, "backward", 0),
        [(blocks, bf16), hidden_shape],
        any_args=(3, 4, 5, 6),
        scratch=expert_scratch,
        args=(ids, arrived_zero, slope_zero, in_own, in_other, out_own, out_other),
        name="experts_back_zero",
    )
    buf_parts_zero = combined(0, pick, buf_zero, "combine_back_zero")
    grad_zero, attn_grad_zero, proj_grad_zero, small_zero = call(
        functools.partial(backward_kernel, 0),
        [token_shape] + grad_shapes,
        any_args=(7, 8),
        scratch=grad_scratch,
        args=(ids, grad_one, inputs, buf_parts_zero, middle_zero, proj_zero, probs_zero, w_own, w_other, onehot),
        name="attention_back_zero",
    )

    def with_peer(arrays, source):
        return tuple(arrays) + tuple(sent(x, source) for x in arrays)

    experts_zero = with_peer((received_zero, act_zero, pre_zero, arrived_zero), 1)
    experts_one = with_peer((received_one, act_one, pre_one, arrived_one), 0)
    in_grad, out_grad = pl.pallas_call(
        expert_grad_kernel,
        out_shape=[jax.ShapeDtypeStruct((2, WIDTH, WIDTH), f32)] * 2,
        grid=(2,),
        in_specs=[pl.BlockSpec(memory_space=pltpu.SMEM)] + [pl.BlockSpec(memory_space=pl.ANY)] * 16,
        out_specs=[pl.BlockSpec((1, WIDTH, WIDTH), lambda e: (e, 0, 0))] * 2,
        scratch_shapes=[
            pltpu.VMEM(shape, bf16) for _ in range(2) for shape in (blocks, (2, 256, WIDTH), (2, 256, WIDTH), blocks)
        ]
        + [pltpu.SemaphoreType.DMA((8,))],
        compiler_params=pltpu.CompilerParams(vmem_limit_bytes=48 * 1024 * 1024),
        name="expert_grads",
    )(ids, *experts_zero, *experts_one)

    layer_zero = with_peer((normed_zero, proj_grad_zero, attn_grad_zero, context_zero, small_zero), 1)
    layer_one = with_peer((normed_one, proj_grad_one, attn_grad_one, context_one, small_one), 0)
    packed = call(
        weight_grad_kernel,
        [((WIDTH, PACK), bf16)],
        args=(ids, *layer_zero, *layer_one, onehot),
        name="attention_grads",
    )[0]
    shares = exchanged(packed.reshape(16, 48, PACK))
    total = call(sum_kernel, [((48, PACK), f32)], scalars=0, args=(shares,), name="sum_grads")[0]

    def outputs(zero, one):
        mine = jnp.where(section == 0, zero, one)
        peer = swapped(jnp.where(section == 0, one, zero))
        return jnp.where(section == 0, jnp.stack([mine, peer]), jnp.stack([peer, mine]))[None]

    states = outputs(state_zero, state_one)
    input_grads = outputs(grad_zero, grad_one)
    return (
        states,
        input_grads,
        total[:, WIDTH].reshape(1, 48),
        total[:, : 3 * SPLIT].reshape(1, 48, 3, SPLIT),
        total[:, 3 * SPLIT : WIDTH].reshape(1, 48, SPLIT),
        total[0:2, WIDTH + 2 : WIDTH + 5].reshape(1, 2, 3),
        total[:, WIDTH + 1].reshape(1, 48),
        in_grad[None],
        out_grad[None],
    )


def solution(mesh):
    return jax.shard_map(
        body,
        mesh=mesh,
        in_specs=(
            P(None, "dp", None),
            P(None, "dp", None),
            P(None, "dp"),
            P(),
            P("section", None, "dp", None),
            P("section", None, "dp", None),
            P("section", "dp"),
            P("section", "dp", None, "mp"),
            P("section", "dp", "mp"),
            P("section", "dp", "mp"),
            P("section", "dp"),
            P("section", "dp", None, "mp"),
            P("section", "dp", "mp", None),
        ),
        out_specs=(
            P("section", None, "dp", None),
            P("section", None, "dp", None),
            P("section", "dp"),
            P("section", "dp", None, "mp"),
            P("section", "dp", "mp"),
            P("section", "dp", "mp"),
            P("section", "dp"),
            P("section", "dp", None, "mp"),
            P("section", "dp", "mp", None),
        ),
        check_vma=False,
    )
```

time: 1220 us -> 408 us (0.33)
  blocking collectives: 371 us -> 107 us
  local copies, waits for them, and re-layouts: 272 us -> 35.3 us
  waiting for transfers between devices: 271 us -> 89.9 us
  other arithmetic: 129 us -> 5.76 us
  matrix products: 77.9 us -> 0 us
  Pallas kernels: 0 us -> 71.4 us
  starting transfers between devices: 68.6 us -> 81.6 us
    psum x6 -> x0, waiting for transfers between devices: 208 us -> none  [the longest x3 108 us: backward_layer(): normed_grad = lax.psum(normed_part, 'mp')]
    psum x5 -> x0, blocking collectives: 186 us -> none  [the longest x3 122 us: forward_layer(): summed = lax.psum(partial_rows, 'mp').astype(jnp.bfloat16)]
    gather x8 -> x0, local copies, waits for them, and re-layouts: 117 us -> none  [the longest x2 97.9 us: body(): bucket_grid = buckets[jnp.clip(distance, 0, tokens - 1)]]
    unnamed x2 -> x0, blocking collectives: 96.9 us -> none
    all_gather x0 -> x1, waiting for transfers between devices: none -> 73.1 us  [body(): w_own = lax.all_gather(pack, ('mp', 'dp'), axis=0).reshape(4, WIDTH, PACK)]
    dot_general x55 -> x0, matrix products: 73 us -> none  [the longest x3 17.9 us: backward_layer(): jnp.einsum('erf,erd->efd', active_low, arrived, preferred_element_type=jn...]
    pallas_call x0 -> x16, Pallas kernels: none -> 71.4 us  [the longest x15 63.3 us: call(): pl.pallas_call(kernel, out_shape=[jax.ShapeDtypeStruct(shape, dtype) for...]
    ppermute x4 -> x24, starting transfers between devices: 13 us -> 54.3 us  [the longest x18 50.7 us: sent(): return lax.ppermute(x, 'section', [(source, 1 - source)])]
  transfers between devices with their start and end apart: 21 -> 30, of which waited for: 14 -> 3; matrix products, arithmetic and copies ran while one was open for 16% -> 2% of each run, Pallas kernels for 0% -> 11%
where the time goes in v1:
time: 408 us; the launch traced here: 406 us
  blocking collectives  107 us (26%)
  waiting for transfers between devices  89.9 us (22%)
  starting transfers between devices  81.6 us (20%)
  Pallas kernels  71.4 us (18%)
  local copies, waits for them, and re-layouts  35.3 us (9%)
  between operations  14.9 us (4%)
  other arithmetic  5.76 us (1%)
    all_gather x1, waiting for transfers between devices, body(): w_own = lax.all_gather(pack, ('mp', 'dp'), axis=0).reshape(4, WIDTH, PACK)  73.1 us
    pallas_call x15, Pallas kernels, call(): pl.pallas_call(kernel, out_shape=[jax.ShapeDtypeStruct(shape, dtype) for...  63.3 us
    all_to_all x4, blocking collectives, exchanged(): lax.all_to_all(x.reshape(16, -1, x.shape[-1]), 'dp', 0, 0, tiled=True)  60 us
    ppermute x18, starting transfers between devices, sent(): return lax.ppermute(x, 'section', [(source, 1 - source)])  50.7 us
    all_gather x4, blocking collectives, gathered_mp(): return lax.all_gather(x, 'mp', axis=0)  47.3 us
    unnamed x132, local copies, waits for them, and re-layouts  28.2 us
    all_to_all x5, starting transfers between devices, exchanged(): lax.all_to_all(x.reshape(16, -1, x.shape[-1]), 'dp', 0, 0, tiled=True)  27.3 us
    all_to_all x5, waiting for transfers between devices, exchanged(): lax.all_to_all(x.reshape(16, -1, x.shape[-1]), 'dp', 0, 0, tiled=True)  12.7 us
  transfers between devices with their start and end apart: 30, of which 3 were waited for; matrix products, arithmetic and copies ran while one was open for 2% of the time, Pallas kernels for 11%

profile of v1, /device:TPU:1, one launch (start us, length us, event | category | flops | bytes accessed | tf_op | source)
XLA Modules:
  0.0 406.2 jit_solution(17007007087577946566)
XLA Ops:
  12.0 73.1 %all-gather.7.cloned.1.call-done = bf16[3072,896]{1,0:T(8,128)(2,1)} async-done(((bf16[48,896]{1,0:T(8,128)(2,1)}), bf16[3072,896]{1,0:T(8,128)(2,1)}) %all-gather.7.cloned.1.call-update) | async-done | bytes 5505040 | tf_op jit(solution)/shard_map/all_gather | solution.py:415
  101.7 10.1 %attention_zero.1 = (bf16[512,768]{1,0:T(8,128)(2,1)S(1)}, f32[128,768]{1,0:T(8,128)S(1)}, bf16[128,768]{1,0:T(8,128)(2,1)S(1)}, bf16[4,128,576]{2,1,0:T(8,128)(...) custom-call(s32[2]{0:T(128)S(1)} %pad_add_fusion.ids, bf16[2,128,768]{2,1,0:T(8,128)(2,1)S(1)} %copy-done.11, ...), custom_call_target="tpu_custom_call" | custom-call | tf_op jit(solution)/shard_map/attention_zero/pallas_call | solution.py:63
  116.4 5.0 %all-to-all-start = ((bf16[16,32,768]{2,1,0:T(8,128)(2,1)}), bf16[16,32,768]{2,1,0:T(8,128)(2,1)S(1)}, u32[]{:S(2)}, u32[]{:S(2)}) async-start(bf16[16,32,768]{2,1,0:T(8,128)(2,1)} %bitcast.77), calls=%async_computation | async-start | bytes 1572864 | tf_op jit(solution)/shard_map/all_to_all | solution.py:392
  121.5 12.7 %all-to-all-done = bf16[16,32,768]{2,1,0:T(8,128)(2,1)S(1)} async-done(((bf16[16,32,768]{2,1,0:T(8,128)(2,1)}), bf16[16,32,768]{2,1,0:T(8,128)(2,1)S(1)}, u32[]{:S(2)}, u32[]{:S(2)}) %all-to-all-start) | async-done | bytes 786464 | tf_op jit(solution)/shard_map/all_to_all | solution.py:392
  134.2 4.6 %experts_zero.1 = (bf16[16,2,16,768]{3,2,1,0:T(8,128)(2,1)S(1)}, bf16[2,256,768]{2,1,0:T(8,128)(2,1)S(1)}, bf16[2,256,768]{2,1,0:T(8,128)(2,1)S(1)}) custom-call(s32[2]{0:T(128)S(1)} %pad_add_fusion.ids, bf16[16,2,16,768]{3,2,1,0:T(8,128)(2,1)S(1)} %bitcast.55, bf16[2,768,768]{2,1,0:T(8,128)(2,1)S(1)} %bitcast.53, ...), custom_call_target="tpu_custom_call" | custom-call | tf_op jit(solution)/shard_map/experts_zero/pallas_call | solution.py:63
  139.7 15.9 %all_to_all.45 = bf16[16,32,768]{2,1,0:T(8,128)(2,1)S(1)} all-to-all(bf16[16,32,768]{2,1,0:T(8,128)(2,1)S(1)} %bitcast.81), channel_id=1, replica_groups=mesh['section'=2,'dp'=16,'mp'=4] {'dp'}, dimensions={0} | all-to-all | bytes 1572864 | tf_op jit(solution)/shard_map/all_to_all | solution.py:392
  160.1 12.0 %all-gather.1 = bf16[512,768]{1,0:T(8,128)(2,1)S(1)} all-gather(bf16[128,768]{1,0:T(8,128)(2,1)S(1)} %combine_zero.1), channel_id=3, replica_groups=mesh['section'=2,'dp'=16,'mp'=4] {'mp'}, dimensions={0}, use_global_device_ids=true | all-gather | bytes 983040 | tf_op jit(solution)/shard_map/all_gather | solution.py:396
  172.1 10.0 %attention_one.1 = (bf16[128,768]{1,0:T(8,128)(2,1)S(1)}, bf16[512,768]{1,0:T(8,128)(2,1)S(1)}, f32[128,768]{1,0:T(8,128)S(1)}, bf16[128,768]{1,0:T(8,128)(2,1)S...) custom-call(s32[2]{0:T(128)S(1)} %pad_add_fusion.ids, ...), custom_call_target="tpu_custom_call" | custom-call | tf_op jit(solution)/shard_map/attention_one/pallas_call | solution.py:63
  187.5 16.9 %all_to_all.46 = bf16[16,32,768]{2,1,0:T(8,128)(2,1)S(1)} all-to-all(bf16[16,32,768]{2,1,0:T(8,128)(2,1)} %bitcast.78), channel_id=1, replica_groups=mesh['section'=2,'dp'=16,'mp'=4] {'dp'}, dimensions={0} | all-to-all | bytes 1572864 | tf_op jit(solution)/shard_map/all_to_all | solution.py:392
  204.4 5.8 %experts_one.1 = (bf16[16,2,16,768]{3,2,1,0:T(8,128)(2,1)S(1)}, bf16[16,2,16,768]{3,2,1,0:T(8,128)(2,1)S(1)}, bf16[2,256,768]{2,1,0:T(8,128)(2,1)S(1)}, bf16[2,256,768]{2,1,0:T(8,128)(2,1)S(1)}) custom-call(s32[2]{0:T(128)S(1)} %pad_add_fusion.ids, bf16[16,2,16,768]{3,2,1,0:T(8,128)(2,1)S(1)} %bitcast.61, bf16[16,2,16,768]{3,2,1,0:T(8,128)(2,1)S(1)} %bitcast.58, ...), custom_call_target="tpu_custom_call" | custom-call | tf_op jit(solution)/shard_map/experts_one/pallas_call | solution.py:63
  211.1 13.9 %all_to_all.47 = bf16[16,32,768]{2,1,0:T(8,128)(2,1)S(1)} all-to-all(bf16[16,32,768]{2,1,0:T(8,128)(2,1)S(1)} %bitcast.80), channel_id=1, replica_groups=mesh['section'=2,'dp'=16,'mp'=4] {'dp'}, dimensions={0} | all-to-all | bytes 1572864 | tf_op jit(solution)/shard_map/all_to_all | solution.py:392
  225.3 10.9 %all-gather.3 = bf16[512,768]{1,0:T(8,128)(2,1)S(1)} all-gather(bf16[128,768]{1,0:T(8,128)(2,1)S(1)} %combine_back_one.1), channel_id=5, replica_groups=mesh['section'=2,'dp'=16,'mp'=4] {'mp'}, dimensions={0}, use_global_device_ids=true | all-gather | bytes 983040 | tf_op jit(solution)/shard_map/all_gather | solution.py:396
  236.3 10.1 %attention_back_one.1 = (bf16[128,768]{1,0:T(8,128)(2,1)S(1)}, bf16[512,768]{1,0:T(8,128)(2,1)S(1)}, bf16[128,768]{1,0:T(8,128)(2,1)S(1)}, bf16[128,576]{1,0:T(8,128)(2,1)S(1)}, f32[16,768]{1,0:T(8,128)S(1)}) custom-call(s32[2]{0:T(128)S(1)} %pad_add_fusion.ids, bf16[2,128,768]{2,1,0:T(8,128)(2,1)S(1)} %copy-done.17, bf16[128,768]{1,0:T(8,128)(2,1)S(1)} %copy-done.22, ...), custom_call_target="tpu_custom_call" | custom-call | tf_op jit(solution)/shard_map/attention_back_one/pallas_call | solution.py:63
  248.4 13.3 %all_to_all.48 = bf16[16,32,768]{2,1,0:T(8,128)(2,1)S(1)} all-to-all(bf16[16,32,768]{2,1,0:T(8,128)(2,1)S(1)} %bitcast.79), channel_id=1, replica_groups=mesh['section'=2,'dp'=16,'mp'=4] {'dp'}, dimensions={0} | all-to-all | bytes 1572864 | tf_op jit(solution)/shard_map/all_to_all | solution.py:392
  271.9 13.8 %collective-permute-start.6 = (bf16[128,768]{1,0:T(8,128)(2,1)}, bf16[128,768]{1,0:T(8,128)(2,1)}, u32[]{:S(2)}, u32[]{:S(2)}) collective-permute-start(bf16[128,768]{1,0:T(8,128)(2,1)} %copy-done.51), channel_id=1, source_target_pairs={{64,0},{65,1},{66,2},{67,3},{68,4},{69,5},{70,6},{71,7},{72,8},{73... | collective-permute-start | bytes 589832 | tf_op jit(solution)/shard_map/ppermute | solution.py:51
  290.4 6.9 %all-to-all-start.4 = ((bf16[16,32,768]{2,1,0:T(8,128)(2,1)}), bf16[16,32,768]{2,1,0:T(8,128)(2,1)}, u32[]{:S(2)}, u32[]{:S(2)}) async-start(bf16[16,32,768]{2,1,0:T(8,128)(2,1)} %bitcast.74), calls=%async_computation.4 | async-start | bytes 1572864 | tf_op jit(solution)/shard_map/all_to_all | solution.py:392
  299.9 6.4 %collective-permute-start.16 = (bf16[16,2,16,768]{3,2,1,0:T(8,128)(2,1)S(1)}, bf16[16,2,16,768]{3,2,1,0:T(8,128)(2,1)}, u32[]{:S(2)}, u32[]{:S(2)}) collective-permute-start(bf16[16,2,16,768]{3,2,1,0:T(8,128)(2,1)S(1)} %bitcast.56), channel_id=1, source_target_pairs={{64,0},{65,1},{66,2},{67,3},{68,4},{69,5},{70,6},{71,7},{72,8},{73... | collective-permute-start | bytes 2359304 | tf_op jit(solution)/shard_map/ppermute | solution.py:51
  313.6 11.4 %all-gather.4 = bf16[512,768]{1,0:T(8,128)(2,1)S(1)} all-gather(bf16[128,768]{1,0:T(8,128)(2,1)S(1)} %combine_back_zero.1), channel_id=6, replica_groups=mesh['section'=2,'dp'=16,'mp'=4] {'mp'}, dimensions={0}, use_global_device_ids=true | all-gather | bytes 983040 | tf_op jit(solution)/shard_map/all_gather | solution.py:396
  325.2 9.2 %attention_back_zero.1 = (bf16[128,768]{1,0:T(8,128)(2,1)S(1)}, bf16[128,768]{1,0:T(8,128)(2,1)S(1)}, bf16[128,576]{1,0:T(8,128)(2,1)S(1)}, f32[16,768]{1,0:T(8,128)S(1)}) custom-call(s32[2]{0:T(128)S(1)} %pad_add_fusion.ids, bf16[128,768]{1,0:T(8,128)(2,1)S(1)} %copy-done.35, bf16[2,128,768]{2,1,0:T(8,128)(2,1)S(1)} %copy-done.12, ...), custom_call_target="tpu_custom_call" | custom-call | tf_op jit(solution)/shard_map/attention_back_zero/pallas_call | solution.py:63
  335.1 5.7 %collective-permute-start.10 = (f32[16,768]{1,0:T(8,128)S(1)}, f32[16,768]{1,0:T(8,128)S(1)}, u32[]{:S(2)}, u32[]{:S(2)}) collective-permute-start(f32[16,768]{1,0:T(8,128)S(1)} %get-tuple-element.71.refs_4_), channel_id=1, source_target_pairs={{64,0},{65,1},{66,2},{67,3},{68,4},{69,5},{70,6},{71,7},{72,8},{73... | collective-permute-start | bytes 147464 | tf_op jit(solution)/shard_map/ppermute | solution.py:51
  349.0 6.9 %all-to-all-start.8 = ((bf16[16,48,896]{2,1,0:T(8,128)(2,1)}), bf16[16,48,896]{2,1,0:T(8,128)(2,1)}, u32[]{:S(2)}, u32[]{:S(2)}) async-start(bf16[16,48,896]{2,1,0:T(8,128)(2,1)} %bitcast.67), calls=%async_computation.8 | async-start | bytes 2752512 | tf_op jit(solution)/shard_map/all_to_all | solution.py:392
  360.9 4.3 %collective-permute-start.19 = (bf16[16,2,16,768]{3,2,1,0:T(8,128)(2,1)S(1)}, bf16[16,2,16,768]{3,2,1,0:T(8,128)(2,1)S(1)}, u32[]{:S(2)}, u32[]{:S(2)}) collective-permute-start(bf16[16,2,16,768]{3,2,1,0:T(8,128)(2,1)S(1)} %bitcast.65), channel_id=1, source_target_pairs={{64,0},{65,1},{66,2},{67,3},{68,4},{69,5},{70,6},{71,7},{72,8},{73... | collective-permute-start | bytes 2359304 | tf_op jit(solution)/shard_map/ppermute | solution.py:51
  366.8 12.9 %all-gather.2 = bf16[512,768]{1,0:T(8,128)(2,1)S(1)} all-gather(bf16[128,768]{1,0:T(8,128)(2,1)S(1)} %combine_one.1), channel_id=4, replica_groups=mesh['section'=2,'dp'=16,'mp'=4] {'mp'}, dimensions={0}, use_global_device_ids=true | all-gather | bytes 983040 | tf_op jit(solution)/shard_map/all_gather | solution.py:396
  386.0 8.1 %expert_grads.1 = (f32[2,768,768]{2,1,0:T(8,128)}, f32[2,768,768]{2,1,0:T(8,128)}) custom-call(s32[2]{0:T(128)S(1)} %pad_add_fusion.ids, bf16[16,2,16,768]{3,2,1,0:T(8,128)(2,1)S(1)} %bitcast.57, bf16[2,256,768]{2,1,0:T(8,128)(2,1)S(1)} %copy-done.24, bf16[2,256,768]{2,1,0:T(8,128)(2,1)S(1)} %copy-done.28, bf16[16,2,16,768]{3,2,1,0:T(8,128)(2,1)S(1)} %bitcast.66, ...), custom_call_target="tpu_custom_call" | custom-call | tf_op jit(solution)/shard_map/expert_grads/pallas_call | solution.py:540
  (222 shorter events, 91.0 us)
Async XLA Ops:
  7.2 77.8 %all-gather.7.cloned.1.call-start = ((), (), s32[]{:S(2)}) async-start(), calls=%async_computation.9 | async-start | bytes 5591040 | tf_op jit(solution)/shard_map/all_gather | solution.py:415
  85.0 15.6 %collective-permute-start = (bf16[4,768,896]{2,1,0:T(8,128)(2,1)}, bf16[4,768,896]{2,1,0:T(8,128)(2,1)}, u32[]{:S(2)}, u32[]{:S(2)}) collective-permute-start(bf16[4,768,896]{2,1,0:T(8,128)(2,1)} %bitcast.83), channel_id=1, source_target_pairs={{0,64},{64,0},{1,65},{65,1},{2,66},{66,2},{3,67},{67,3},{4,68},{68... | collective-permute-start | bytes 16515080 | tf_op jit(solution)/shard_map/ppermute | solution.py:47
  86.9 34.5 %collective-permute-start.2 = (bf16[2,768,768]{2,1,0:T(8,128)(2,1)}, bf16[2,768,768]{2,1,0:T(8,128)(2,1)}, u32[]{:S(2)}, u32[]{:S(2)}) collective-permute-start(bf16[2,768,768]{2,1,0:T(8,128)(2,1)} %bitcast.51), channel_id=1, source_target_pairs={{0,64},{64,0},{1,65},{65,1},{2,66},{66,2},{3,67},{67,3},{4,68},{68... | collective-permute-start | bytes 7077896 | tf_op jit(solution)/shard_map/ppermute | solution.py:47
  86.9 34.5 %collective-permute-start.3 = (bf16[2,768,768]{2,1,0:T(8,128)(2,1)}, bf16[2,768,768]{2,1,0:T(8,128)(2,1)}, u32[]{:S(2)}, u32[]{:S(2)}) collective-permute-start(bf16[2,768,768]{2,1,0:T(8,128)(2,1)} %bitcast.88), channel_id=1, source_target_pairs={{0,64},{64,0},{1,65},{65,1},{2,66},{66,2},{3,67},{67,3},{4,68},{68... | collective-permute-start | bytes 7077896 | tf_op jit(solution)/shard_map/ppermute | solution.py:47
  116.4 17.8 %all-to-all-start = ((bf16[16,32,768]{2,1,0:T(8,128)(2,1)}), bf16[16,32,768]{2,1,0:T(8,128)(2,1)S(1)}, u32[]{:S(2)}, u32[]{:S(2)}) async-start(bf16[16,32,768]{2,1,0:T(8,128)(2,1)} %bitcast.77), calls=%async_computation | async-start | bytes 1572864 | tf_op jit(solution)/shard_map/all_to_all | solution.py:392
  155.7 31.8 %all-to-all-start.3 = ((bf16[16,32,768]{2,1,0:T(8,128)(2,1)}), bf16[16,32,768]{2,1,0:T(8,128)(2,1)S(1)}, u32[]{:S(2)}, u32[]{:S(2)}) async-start(bf16[16,32,768]{2,1,0:T(8,128)(2,1)} %bitcast.75), calls=%async_computation.3 | async-start | bytes 1572864 | tf_op jit(solution)/shard_map/all_to_all | solution.py:392
  267.6 22.7 %all-to-all-start.7 = ((bf16[16,32,768]{2,1,0:T(8,128)(2,1)}), bf16[16,32,768]{2,1,0:T(8,128)(2,1)}, u32[]{:S(2)}, u32[]{:S(2)}) async-start(bf16[16,32,768]{2,1,0:T(8,128)(2,1)} %bitcast.76), calls=%async_computation.7 | async-start | bytes 1572864 | tf_op jit(solution)/shard_map/all_to_all | solution.py:392
  271.9 26.6 %collective-permute-start.6 = (bf16[128,768]{1,0:T(8,128)(2,1)}, bf16[128,768]{1,0:T(8,128)(2,1)}, u32[]{:S(2)}, u32[]{:S(2)}) collective-permute-start(bf16[128,768]{1,0:T(8,128)(2,1)} %copy-done.51), channel_id=1, source_target_pairs={{64,0},{65,1},{66,2},{67,3},{68,4},{69,5},{70,6},{71,7},{72,8},{73... | collective-permute-start | bytes 589832 | tf_op jit(solution)/shard_map/ppermute | solution.py:51
  285.8 14.1 %collective-permute-start.9 = (bf16[4,128,192]{2,1,0:T(8,128)(2,1)}, bf16[4,128,192]{2,1,0:T(8,128)(2,1)}, u32[]{:S(2)}, u32[]{:S(2)}) collective-permute-start(bf16[4,128,192]{2,1,0:T(8,128)(2,1)} %copy-done.46), channel_id=1, source_target_pairs={{64,0},{65,1},{66,2},{67,3},{68,4},{69,5},{70,6},{71,7},{72,8},{73... | collective-permute-start | bytes 589832 | tf_op jit(solution)/shard_map/ppermute | solution.py:51
  287.8 18.5 %collective-permute-start.11 = (bf16[128,768]{1,0:T(8,128)(2,1)}, bf16[128,768]{1,0:T(8,128)(2,1)}, u32[]{:S(2)}, u32[]{:S(2)}) collective-permute-start(bf16[128,768]{1,0:T(8,128)(2,1)} %copy-done.53), channel_id=1, source_target_pairs={{0,64},{1,65},{2,66},{3,67},{4,68},{5,69},{6,70},{7,71},{8,72},{9,... | collective-permute-start | bytes 589832 | tf_op jit(solution)/shard_map/ppermute | solution.py:51
  289.1 22.0 %collective-permute-start.14 = (bf16[4,128,192]{2,1,0:T(8,128)(2,1)}, bf16[4,128,192]{2,1,0:T(8,128)(2,1)}, u32[]{:S(2)}, u32[]{:S(2)}) collective-permute-start(bf16[4,128,192]{2,1,0:T(8,128)(2,1)} %copy-done.48), channel_id=1, source_target_pairs={{0,64},{1,65},{2,66},{3,67},{4,68},{5,69},{6,70},{7,71},{8,72},{9,... | collective-permute-start | bytes 589832 | tf_op jit(solution)/shard_map/ppermute | solution.py:51
  290.4 58.6 %all-to-all-start.4 = ((bf16[16,32,768]{2,1,0:T(8,128)(2,1)}), bf16[16,32,768]{2,1,0:T(8,128)(2,1)}, u32[]{:S(2)}, u32[]{:S(2)}) async-start(bf16[16,32,768]{2,1,0:T(8,128)(2,1)} %bitcast.74), calls=%async_computation.4 | async-start | bytes 1572864 | tf_op jit(solution)/shard_map/all_to_all | solution.py:392
  297.2 15.1 %collective-permute-start.15 = (f32[16,768]{1,0:T(8,128)}, f32[16,768]{1,0:T(8,128)S(1)}, u32[]{:S(2)}, u32[]{:S(2)}) collective-permute-start(f32[16,768]{1,0:T(8,128)} %copy-done.59), channel_id=1, source_target_pairs={{0,64},{1,65},{2,66},{3,67},{4,68},{5,69},{6,70},{7,71},{8,72},{9,... | collective-permute-start | bytes 147464 | tf_op jit(solution)/shard_map/ppermute | solution.py:51
  298.6 61.1 %collective-permute-start.23 = (bf16[16,2,16,768]{3,2,1,0:T(8,128)(2,1)S(1)}, bf16[16,2,16,768]{3,2,1,0:T(8,128)(2,1)}, u32[]{:S(2)}, u32[]{:S(2)}) collective-permute-start(bf16[16,2,16,768]{3,2,1,0:T(8,128)(2,1)S(1)} %bitcast.59), channel_id=1, source_target_pairs={{0,64},{1,65},{2,66},{3,67},{4,68},{5,69},{6,70},{7,71},{8,72},{9,... | collective-permute-start | bytes 2359304 | tf_op jit(solution)/shard_map/ppermute | solution.py:51
  299.9 61.1 %collective-permute-start.16 = (bf16[16,2,16,768]{3,2,1,0:T(8,128)(2,1)S(1)}, bf16[16,2,16,768]{3,2,1,0:T(8,128)(2,1)}, u32[]{:S(2)}, u32[]{:S(2)}) collective-permute-start(bf16[16,2,16,768]{3,2,1,0:T(8,128)(2,1)S(1)} %bitcast.56), channel_id=1, source_target_pairs={{64,0},{65,1},{66,2},{67,3},{68,4},{69,5},{70,6},{71,7},{72,8},{73... | collective-permute-start | bytes 2359304 | tf_op jit(solution)/shard_map/ppermute | solution.py:51
  306.3 59.0 %collective-permute-start.17 = (bf16[2,256,768]{2,1,0:T(8,128)(2,1)}, bf16[2,256,768]{2,1,0:T(8,128)(2,1)}, u32[]{:S(2)}, u32[]{:S(2)}) collective-permute-start(bf16[2,256,768]{2,1,0:T(8,128)(2,1)} %copy-done.23), channel_id=1, source_target_pairs={{64,0},{65,1},{66,2},{67,3},{68,4},{69,5},{70,6},{71,7},{72,8},{73... | collective-permute-start | bytes 2359304 | tf_op jit(solution)/shard_map/ppermute | solution.py:51
  311.0 24.1 %collective-permute-start.12 = (bf16[128,576]{1,0:T(8,128)(2,1)}, bf16[128,576]{1,0:T(8,128)(2,1)S(1)}, u32[]{:S(2)}, u32[]{:S(2)}) collective-permute-start(bf16[128,576]{1,0:T(8,128)(2,1)} %copy-done.57), channel_id=1, source_target_pairs={{0,64},{1,65},{2,66},{3,67},{4,68},{5,69},{6,70},{7,71},{8,72},{9,... | collective-permute-start | bytes 442376 | tf_op jit(solution)/shard_map/ppermute | solution.py:51
  312.3 28.5 %collective-permute-start.13 = (bf16[128,768]{1,0:T(8,128)(2,1)}, bf16[128,768]{1,0:T(8,128)(2,1)S(1)}, u32[]{:S(2)}, u32[]{:S(2)}) collective-permute-start(bf16[128,768]{1,0:T(8,128)(2,1)} %copy-done.55), channel_id=1, source_target_pairs={{0,64},{1,65},{2,66},{3,67},{4,68},{5,69},{6,70},{7,71},{8,72},{9,... | collective-permute-start | bytes 589832 | tf_op jit(solution)/shard_map/ppermute | solution.py:51
  343.9 36.9 %collective-permute-start.20 = (bf16[16,2,16,768]{3,2,1,0:T(8,128)(2,1)S(1)}, bf16[16,2,16,768]{3,2,1,0:T(8,128)(2,1)}, u32[]{:S(2)}, u32[]{:S(2)}) collective-permute-start(bf16[16,2,16,768]{3,2,1,0:T(8,128)(2,1)S(1)} %bitcast.62), channel_id=1, source_target_pairs={{0,64},{1,65},{2,66},{3,67},{4,68},{5,69},{6,70},{7,71},{8,72},{9,... | collective-permute-start | bytes 2359304 | tf_op jit(solution)/shard_map/ppermute | solution.py:51
  349.0 46.0 %all-to-all-start.8 = ((bf16[16,48,896]{2,1,0:T(8,128)(2,1)}), bf16[16,48,896]{2,1,0:T(8,128)(2,1)}, u32[]{:S(2)}, u32[]{:S(2)}) async-start(bf16[16,48,896]{2,1,0:T(8,128)(2,1)} %bitcast.67), calls=%async_computation.8 | async-start | bytes 2752512 | tf_op jit(solution)/shard_map/all_to_all | solution.py:392
  355.9 28.0 %collective-permute-start.21 = (bf16[2,256,768]{2,1,0:T(8,128)(2,1)}, bf16[2,256,768]{2,1,0:T(8,128)(2,1)S(1)}, u32[]{:S(2)}, u32[]{:S(2)}) collective-permute-start(bf16[2,256,768]{2,1,0:T(8,128)(2,1)} %copy-done.25), channel_id=1, source_target_pairs={{0,64},{1,65},{2,66},{3,67},{4,68},{5,69},{6,70},{7,71},{8,72},{9,... | collective-permute-start | bytes 2359304 | tf_op jit(solution)/shard_map/ppermute | solution.py:51
  359.6 24.3 %collective-permute-start.22 = (bf16[2,256,768]{2,1,0:T(8,128)(2,1)}, bf16[2,256,768]{2,1,0:T(8,128)(2,1)S(1)}, u32[]{:S(2)}, u32[]{:S(2)}) collective-permute-start(bf16[2,256,768]{2,1,0:T(8,128)(2,1)} %copy-done.26), channel_id=1, source_target_pairs={{0,64},{1,65},{2,66},{3,67},{4,68},{5,69},{6,70},{7,71},{8,72},{9,... | collective-permute-start | bytes 2359304 | tf_op jit(solution)/shard_map/ppermute | solution.py:51
  360.9 23.0 %collective-permute-start.19 = (bf16[16,2,16,768]{3,2,1,0:T(8,128)(2,1)S(1)}, bf16[16,2,16,768]{3,2,1,0:T(8,128)(2,1)S(1)}, u32[]{:S(2)}, u32[]{:S(2)}) collective-permute-start(bf16[16,2,16,768]{3,2,1,0:T(8,128)(2,1)S(1)} %bitcast.65), channel_id=1, source_target_pairs={{64,0},{65,1},{66,2},{67,3},{68,4},{69,5},{70,6},{71,7},{72,8},{73... | collective-permute-start | bytes 2359304 | tf_op jit(solution)/shard_map/ppermute | solution.py:51
  365.3 18.7 %collective-permute-start.18 = (bf16[2,256,768]{2,1,0:T(8,128)(2,1)}, bf16[2,256,768]{2,1,0:T(8,128)(2,1)S(1)}, u32[]{:S(2)}, u32[]{:S(2)}) collective-permute-start(bf16[2,256,768]{2,1,0:T(8,128)(2,1)} %copy-done.27), channel_id=1, source_target_pairs={{64,0},{65,1},{66,2},{67,3},{68,4},{69,5},{70,6},{71,7},{72,8},{73... | collective-permute-start | bytes 2359304 | tf_op jit(solution)/shard_map/ppermute | solution.py:51
  (71 other events, 935.2 us)
Sparse Core Ops, SparseCore 0:
  12.1 72.8 all-gather.6

commit v2 on v1

v2 whole, which is shorter than its diff:
```python
import functools

import jax
import jax.numpy as jnp
from jax import lax
from jax.experimental import pallas as pl
from jax.experimental.pallas import tpu as pltpu
from jax.sharding import PartitionSpec as P

bf16 = jnp.bfloat16
f32 = jnp.float32
epsilon = 1e-06
negative = -1e30
root = 0.7978845608028654
cubic = 0.044715
TOK = 128
WIDTH = 768
HEADS = 3
DH = 64
SPLIT = 192
PACK = 896
SLOTS = 512
CAP = 16


def dot(a, b):
    return lax.dot_general(a, b, (((1,), (0,)), ((), ())), preferred_element_type=f32)


def dot_nt(a, b):
    return lax.dot_general(a, b, (((1,), (1,)), ((), ())), preferred_element_type=f32)


def dot_tn(a, b):
    return lax.dot_general(a, b, (((0,), (0,)), ((), ())), preferred_element_type=f32)


def iota(shape, dim):
    return lax.broadcasted_iota(jnp.int32, shape, dim)


def norm_scale(values):
    return lax.rsqrt(jnp.mean(values * values, axis=-1, keepdims=True) + epsilon)


def swapped(x):
    return lax.ppermute(x, "section", [(0, 1), (1, 0)])


def sent(x, source):
    return lax.ppermute(x, "section", [(source, 1 - source)])


class Loaded:
    def __init__(self, source, buffer, sem):
        self.copy = pltpu.make_async_copy(source, buffer, sem)
        self.buffer, self.waiting = buffer, True
        self.copy.start()

    def ready(self):
        if self.waiting:
            self.copy.wait()
            self.waiting = False

    def __getitem__(self, index):
        self.ready()
        return self.buffer[index]


class Stored:
    def __init__(self, target, buffer, sems):
        self.target, self.buffer, self.sems, self.copies = target, buffer, sems, []
        self.dtype = target.dtype

    def __setitem__(self, index, value):
        self.buffer[index] = value

    def start(self, *index):
        source = self.buffer.at[index] if index else self.buffer
        target = self.target.at[index] if index else self.target
        copy = pltpu.make_async_copy(source, target, self.sems.at[len(self.copies)])
        copy.start()
        self.copies.append(copy)

    def finish(self):
        for copy in self.copies:
            copy.wait()


def far(x):
    return pltpu.with_memory_space_constraint(x, pltpu.HBM)


def call(kernel, outs, raw=(), load=(), store=(), scalars=1, scratch=(), args=(), name=None, limit=16):
    specs = []
    for index in range(len(args)):
        if index < scalars:
            specs.append(pl.BlockSpec(memory_space=pltpu.SMEM))
        elif index in raw or index in load:
            specs.append(pl.BlockSpec(memory_space=pltpu.HBM))
        else:
            specs.append(pl.BlockSpec(memory_space=pltpu.VMEM))
    extra = [pltpu.VMEM(args[i].shape, args[i].dtype) for i in load]
    extra += [pltpu.VMEM(*outs[i]) for i in store]
    if load:
        extra.append(pltpu.SemaphoreType.DMA((len(load),)))
    if store:
        extra.append(pltpu.SemaphoreType.DMA((len(store), 8)))

    def wrapped(*refs):
        refs = list(refs)
        count = len(args) + len(outs)
        own = refs[count : len(refs) - len(extra)]
        more = refs[len(refs) - len(extra) :]
        load_sems = more[len(load) + len(store)] if load else None
        store_sems = more[-1] if store else None
        for n, i in enumerate(load):
            refs[i] = Loaded(refs[i], more[n], load_sems.at[n])
        stored = []
        for n, i in enumerate(store):
            refs[len(args) + i] = Stored(refs[len(args) + i], more[len(load) + n], store_sems.at[n])
            stored.append(refs[len(args) + i])
        kernel(*refs[:count], *own)
        for item in refs[:count]:
            if isinstance(item, Loaded):
                item.ready()
        for item in stored:
            if not item.copies:
                item.start()
        for item in stored:
            item.finish()

    args = [far(x) if i in raw or i in load else x for i, x in enumerate(args)]
    return pl.pallas_call(
        wrapped,
        out_shape=[
            pltpu.HBM(shape, dtype) if i in store else jax.ShapeDtypeStruct(shape, dtype)
            for i, (shape, dtype) in enumerate(outs)
        ],
        in_specs=specs,
        out_specs=[
            pl.BlockSpec(memory_space=pltpu.HBM if i in store else pltpu.VMEM) for i in range(len(outs))
        ],
        scratch_shapes=list(scratch) + extra,
        compiler_params=pltpu.CompilerParams(vmem_limit_bytes=limit * 1024 * 1024),
        name=name,
    )(*args)


def fetch(here, own, other, buffer, sems):
    count = buffer.shape[0]

    @pl.when(here)
    def _():
        for i in range(count):
            pltpu.make_async_copy(own.at[i], buffer.at[i], sems.at[i]).start()

    @pl.when(jnp.logical_not(here))
    def _():
        for i in range(count):
            pltpu.make_async_copy(other.at[i], buffer.at[i], sems.at[i]).start()

    def arrived():
        for i in range(count):
            pltpu.make_async_copy(own.at[i], buffer.at[i], sems.at[i]).wait()

    return arrived


def pack_kernel(qkv, out_part, gain_one, gain_two, table, whole, halves):
    eye = iota((48, 48), 0) == iota((48, 48), 1)
    one = jnp.sum(jnp.where(eye, gain_one[...].astype(f32), 0.0), axis=1, keepdims=True)
    two = jnp.sum(jnp.where(eye, gain_two[...].astype(f32), 0.0), axis=1, keepdims=True)
    row, lane = iota((48, TOK), 0), iota((48, TOK), 1)
    extra = jnp.where(lane == 0, one, jnp.where(lane == 1, two, 0.0))
    values = table[...].astype(f32)
    for r in range(2):
        for h in range(HEADS):
            extra = extra + jnp.where((row == r) & (lane == 2 + h), values[r : r + 1, h : h + 1], 0.0)
    parts = [qkv[0], qkv[1], qkv[2], out_part[...]]
    line = jnp.concatenate(parts + [extra.astype(bf16), jnp.zeros((48, TOK), bf16)], axis=1)
    whole[...] = line[:, :PACK]
    halves[0] = line[:, :512]
    halves[1] = line[:, 512:]


def spread_kernel(ids, halves, received, out):
    chosen = jnp.where(ids[0] == 0, halves[0], received[...])
    for i in range(16):
        out[i] = chosen


def first_kernel(ids, inputs, own, other, onehot, mask, part_out, gains_out):
    first = ids[0] == 0
    hidden = jnp.where(first, inputs[0], inputs[1]).astype(f32)
    scaled = hidden * norm_scale(hidden)
    low = jnp.where(first, own[...], other[...])
    high = jnp.where(first, other[...], own[...])
    weight = jnp.concatenate([low, high], axis=1)
    rows = weight[:, WIDTH:PACK].astype(f32).T
    gains_out[...] = rows[0:8]
    normed = (scaled * rows[0:1]).astype(bf16)
    proj = dot(normed, weight[:, : 3 * SPLIT]).astype(bf16)
    line = dot_tn(weight[:, WIDTH:PACK], onehot[...]).astype(bf16)
    allowed = mask[...] > 0.5
    pieces = [jnp.zeros((TOK, DH), bf16)]
    for head in range(HEADS):
        probs, value = head_probs(proj, head_bias(line, allowed, head), head)
        pieces.append(dot(probs, value).astype(bf16))
    part_out[...] = dot_nt(jnp.concatenate(pieces, axis=1), weight[:, 512:WIDTH]).astype(bf16)


def dispatch_kernel(ids, inputs, parts, gain_rows, pick, middle_out, sent_out):
    hidden = jnp.where(ids[0] == 0, inputs[0], inputs[1]).astype(f32)
    for i in range(4):
        hidden = hidden + parts[i].astype(f32)
    middle_out[...] = hidden
    normed = (hidden * norm_scale(hidden) * gain_rows[1:2, :]).astype(bf16)
    sent_out[...] = dot_tn(pick[...], normed).astype(bf16)


def prepare_kernel(ids, own, other, segments, cotangent, pick_zero, pick_one, gated_zero, gated_one, mask, sent_grad):
    section = ids[0]
    first = section == 0
    row = jnp.where(first, segments[0:1, :], segments[1:2, :]).astype(f32)
    column = own[:, 0:1]
    causal = iota((TOK, TOK), 0) >= iota((TOK, TOK), 1)
    mask[...] = jnp.where(causal & (column == row), 1.0, 0.0)
    expert = iota((TOK, 32), 1).astype(f32)
    lower = jnp.where(iota((TOK, TOK), 0) > iota((TOK, TOK), 1), 1.0, 0.0).astype(bf16)
    spread = jnp.where(lax.shift_right_logical(iota((32, SLOTS), 1), 4) == iota((32, SLOTS), 0), 1.0, 0.0).astype(bf16)
    slot = iota((TOK, SLOTS), 1)
    slot_expert = lax.shift_right_logical(slot, 4).astype(f32)
    slot_place = (slot & 15).astype(f32)
    for layer in range(2):
        info = jnp.where(section == layer, own[...], other[...])
        r0, r1, g0, g1 = info[:, 1:2], info[:, 2:3], info[:, 3:4], info[:, 4:5]
        named = jnp.where((r0 == expert) | (r1 == expert), 1.0, 0.0).astype(bf16)
        earlier = dot(lower, named)
        here = dot(earlier.astype(bf16), spread) == slot_place
        d0 = here & (r0 == slot_expert)
        d1 = here & (r1 == slot_expert)
        (pick_zero, pick_one)[layer][...] = jnp.where(d0 | d1, 1.0, 0.0).astype(bf16)
        gates = jnp.where(d0, g0, jnp.where(d1, g1, 0.0)).astype(bf16)
        (gated_zero, gated_one)[layer][...] = gates
        if layer == 1:
            grad = jnp.where(first, cotangent[0], cotangent[1])
            sent_grad[...] = dot_tn(gates, grad).astype(bf16)


def head_bias(line, allowed, head):
    chosen = jnp.where(iota((TOK, TOK), 1) == 2 + head, 1.0, 0.0).astype(bf16)
    bias = pltpu.roll(dot(chosen, line), 0, 1, stride=1, stride_axis=0)
    return jnp.where(allowed, bias, negative)


def head_probs(proj, bias, head):
    at = head * DH
    query = proj[:, at : at + DH]
    key = proj[:, SPLIT + at : SPLIT + at + DH]
    value = proj[:, 2 * SPLIT + at : 2 * SPLIT + at + DH]
    scores = dot_nt(query * jnp.asarray(0.125, bf16), key) + bias
    peak = jnp.max(scores, axis=-1, keepdims=True)
    expos = jnp.exp(scores - peak)
    return (expos / jnp.sum(expos, axis=-1, keepdims=True)).astype(bf16), value


def bias_kernel(layer, ids, own, other, onehot, mask, bias_out, gains_out, extra, sem):
    lanes = pl.ds(WIDTH, TOK)

    @pl.when(ids[0] == layer)
    def _():
        pltpu.make_async_copy(own.at[:, :, lanes], extra, sem).start()

    @pl.when(ids[0] != layer)
    def _():
        pltpu.make_async_copy(other.at[:, :, lanes], extra, sem).start()

    pltpu.make_async_copy(own.at[:, :, lanes], extra, sem).wait()
    gains_out[...] = extra[0].astype(f32).T[0:8]
    allowed = mask[...] > 0.5
    for part in range(4):
        line = dot_tn(extra[part], onehot[...]).astype(bf16)
        for head in range(HEADS):
            bias_out[part * HEADS + head] = head_bias(line, allowed, head).astype(bf16)


def forward_kernel(layer, ids, *refs):
    if layer == 0:
        inputs, own, other, gain_rows, bias = refs[:5]
        rest = refs[5:]
    else:
        before, parts, own, other, gain_rows, bias, pick, state_out, sent_out, middle_out = refs[:10]
        rest = refs[10:]
    normed_out, proj_out, probs_out, context_out, contexts, weights, sems = rest
    section = ids[0]
    arrived = fetch(section == layer, own, other, weights, sems)
    if layer == 0:
        hidden = jnp.where(section == 0, inputs[0], inputs[1]).astype(f32)
    else:
        added = parts[0].astype(f32)
        for i in range(1, 4):
            added = added + parts[i].astype(f32)
        state = (before[...] + added).astype(bf16)
        state_out[...] = state
        state_out.start()
        hidden = state.astype(f32)
    normed = (hidden * norm_scale(hidden) * gain_rows[0:1, :]).astype(bf16)
    normed_out[...] = normed
    normed_out.start()
    attn = None
    arrived()
    for part in range(4):
        proj = dot(normed, weights[part, :, : 3 * SPLIT]).astype(bf16)
        proj_out[part] = proj
        proj_out.start(part)
        pieces = []
        for head in range(HEADS):
            probs, value = head_probs(proj, bias[part * HEADS + head].astype(f32), head)
            probs_out[part * HEADS + head] = probs
            pieces.append(dot(probs, value).astype(bf16))
        probs_out.start(pl.ds(part * HEADS, HEADS))
        contexts[part] = jnp.concatenate(pieces, axis=1)
        if layer == 1:
            padded = jnp.concatenate([jnp.zeros((TOK, DH), bf16)] + pieces, axis=1)
            term = dot_nt(padded, weights[part, :, 512:WIDTH])
            attn = term if attn is None else attn + term
    context_out[...] = contexts[ids[1]]
    context_out.start()
    if layer == 1:
        middle = hidden + attn
        middle_out[...] = middle
        middle_out.start()
        normed_two = (middle * norm_scale(middle) * gain_rows[1:2, :]).astype(bf16)
        sent_out[...] = dot_tn(pick[...], normed_two).astype(bf16)


def gelu_both(x):
    square = x * x
    th = jnp.tanh(root * (x + cubic * x * square))
    half = 0.5 * (1.0 + th)
    value = x * half
    slope = half + 0.5 * x * (1.0 - th * th) * (root * (1.0 + 3.0 * cubic * square))
    return value, slope


def rows_of(ref, expert):
    return ref[:, expert].reshape(256, WIDTH)


def expert_kernel(mode, layer, ids, *refs):
    if mode == "forward":
        received, in_own, in_other, out_own, out_other, y_out, ahead, slope_out = refs[:8]
    elif mode == "both":
        received, arrived_grad, in_own, in_other, out_own, out_other, y_out, buf_out, ahead, behind = refs[:10]
    else:
        slope_in, arrived_grad, in_own, in_other, out_own, out_other, buf_out, behind = refs[:8]
    w_in, w_out, in_sems, out_sems = refs[-4:]
    in_arrived = fetch(ids[0] == layer, in_own, in_other, w_in, in_sems)
    out_arrived = fetch(ids[0] == layer, out_own, out_other, w_out, out_sems)
    in_arrived()
    out_arrived()
    for e in range(2):
        if mode != "backward":
            rows = rows_of(received, e)
            value, slope = gelu_both(dot(rows, w_in[e]))
            act = value.astype(bf16)
            ahead[0, e] = rows
            ahead[1, e] = act
            ahead.start(slice(None), e)
            y_out[:, e] = dot(act, w_out[e]).astype(bf16).reshape(16, CAP, WIDTH)
            if mode == "forward":
                slope_out[e] = slope.astype(bf16)
                slope_out.start(e)
        else:
            slope = slope_in[e].astype(f32)
        if mode != "forward":
            back = rows_of(arrived_grad, e)
            pre = (dot_nt(back, w_out[e]) * slope).astype(bf16)
            behind[0, e] = pre
            behind[1, e] = back
            behind.start(slice(None), e)
            buf_out[:, e] = dot_nt(pre, w_in[e]).astype(bf16).reshape(16, CAP, WIDTH)


def combine_kernel(matrix, returned, out):
    out[...] = dot(matrix[...], returned[...]).astype(out.dtype)


def state_kernel(ids, before, *refs):
    parts, out, ordered = refs[:4], refs[4], refs[5]
    for by in range(4):
        ordered[(ids[1] + 4 - by) & 3] = parts[by][...]
    total = before[...]
    for i in range(4):
        total = total + ordered[i].astype(f32)
    out[...] = total.astype(bf16)


def backward_kernel(layer, ids, *refs):
    if layer == 1:
        grads, hidden_ref = refs[0], refs[1]
    else:
        grads, hidden_ref = refs[0], refs[1]
    parts, middle_ref, proj_ref, probs_ref, own, other, gain_rows, normed_ref, context_ref = refs[2:11]
    rest = refs[11:]
    if layer == 1:
        gated, rest = rest[0], rest[1:]
    if layer == 1:
        sent_out, rest = rest[0], rest[1:]
    bundle, all_proj, all_scores, small_out, weights, sems = rest
    arrived = fetch(ids[0] == layer, own, other, weights, sems)
    section = ids[0]
    device = ids[1]
    first = section == 0
    if layer == 1:
        grad = jnp.where(first, grads[0], grads[1]).astype(f32)
        hidden = hidden_ref[...].astype(f32)
    else:
        grad = grads[3 * TOK : 4 * TOK].astype(f32)
        hidden = jnp.where(first, hidden_ref[0], hidden_ref[1]).astype(f32)
    middle = middle_ref[...]
    buf = parts[0].astype(f32)
    for i in range(1, 4):
        buf = buf + parts[i].astype(f32)
    scale_two = norm_scale(middle)
    gain_one, gain_two = gain_rows[0:1, :], gain_rows[1:2, :]
    small_out[...] = jnp.zeros(small_out.shape, f32)
    unit = middle * scale_two
    small_out[1:2, :] = jnp.sum(buf * unit, axis=0, keepdims=True)
    inner = jnp.mean(unit * gain_two * buf, axis=-1, keepdims=True)
    middle_grad = grad + scale_two * (gain_two * buf - unit * inner)
    attn_low = middle_grad.astype(bf16)
    bundle[0:TOK] = normed_ref[...]
    bundle[TOK : 2 * TOK] = attn_low
    normed_grad = None
    arrived()
    for part in range(4):
        context_grad = dot(attn_low, weights[part, :, 512:WIDTH]).astype(bf16)
        proj = proj_ref[part]
        q_parts, k_parts, v_parts = [], [], []
        for head in range(HEADS):
            at = head * DH
            query = proj[:, at : at + DH]
            key = proj[:, SPLIT + at : SPLIT + at + DH]
            value = proj[:, 2 * SPLIT + at : 2 * SPLIT + at + DH]
            probs = probs_ref[part * HEADS + head]
            back = context_grad[:, DH + at : DH + at + DH]
            wide = probs.astype(f32)
            prob_grad = dot_nt(back, value)
            inner = jnp.sum(wide * prob_grad, axis=-1, keepdims=True)
            score_grad = (wide * (prob_grad - inner)).astype(bf16)
            all_scores[part * HEADS + head] = score_grad
            q_parts.append(dot(score_grad, key) * 0.125)
            k_parts.append(dot_tn(score_grad, query) * 0.125)
            v_parts.append(dot_tn(probs, back))
        proj_grad = jnp.concatenate(q_parts + k_parts + v_parts, axis=1).astype(bf16)
        all_proj[part] = proj_grad
        term = dot_nt(proj_grad, weights[part, :, : 3 * SPLIT])
        normed_grad = term if normed_grad is None else normed_grad + term
    scale_one = norm_scale(hidden)
    unit = hidden * scale_one
    small_out[0:1, :] = jnp.sum(normed_grad * unit, axis=0, keepdims=True)
    inner = jnp.mean(unit * gain_one * normed_grad, axis=-1, keepdims=True)
    low = (middle_grad + scale_one * (gain_one * normed_grad - unit * inner)).astype(bf16)
    bundle[3 * TOK : 4 * TOK] = low
    if layer == 1:
        sent_out[...] = dot_tn(gated[...], low).astype(bf16)
    bundle[2 * TOK : 3 * TOK] = jnp.concatenate([all_proj[device], context_ref[...]], axis=1)
    flip = jnp.where(iota((TOK, TOK), 0) + iota((TOK, TOK), 1) == TOK - 1, 1.0, 0.0).astype(bf16)
    for head in range(HEADS):
        flipped = dot(flip, all_scores[device * HEADS + head])
        lined = pltpu.roll(flipped, 1, 1, stride=1, stride_axis=0)
        small_out[2 + head : 3 + head, 0:TOK] = jnp.sum(lined, axis=0, keepdims=True)
    bundle[4 * TOK :] = small_out[...].astype(bf16)


def weight_grad_kernel(ids, zero, zero_peer, one, one_peer, onehot, out):
    one.ready()
    one_peer.ready()
    for layer, (mine, peer) in enumerate(((zero, zero_peer), (one, one_peer))):

        @pl.when(ids[0] == layer)
        def _(mine=mine, peer=peer):
            both = [jnp.concatenate([mine[i * TOK : i * TOK + TOK], peer[i * TOK : i * TOK + TOK]], axis=0) for i in range(3)]
            normed, attn, third = both
            left = dot_tn(normed, third[:, : 3 * SPLIT])
            right = dot_tn(attn, third[:, 3 * SPLIT :])
            rows = mine[4 * TOK :].astype(f32) + peer[4 * TOK :].astype(f32)
            lines = rows[:, 0:TOK].astype(bf16)
            keep = (iota((TOK, 16), 1) >= 2) & (iota((TOK, 16), 1) < 5) & (iota((TOK, 16), 0) == iota((TOK, 16), 1))
            lines = dot(jnp.where(keep, 1.0, 0.0).astype(bf16), lines).astype(bf16)
            table = dot_nt(onehot[...], lines)
            tall = jnp.concatenate([rows, jnp.zeros((TOK - 16, WIDTH), f32)], axis=0).T
            lane = iota((WIDTH, TOK), 1)
            extra = jnp.where(lane < 2, tall, table)
            out[...] = jnp.concatenate([left, right, extra], axis=1).astype(bf16).reshape(16, 48, PACK)


def sum_kernel(received, qkv, out_part, extra):
    total = received[0].astype(f32)
    for i in range(1, 16):
        total = total + received[i].astype(f32)
    for c in range(3):
        qkv[c] = total[:, c * SPLIT : (c + 1) * SPLIT]
    out_part[...] = total[:, 3 * SPLIT : WIDTH]
    extra[...] = total[:, WIDTH:].T[0:8, :]


def assemble_kernel(ids, state_zero, state_one, state_zero_peer, state_one_peer, zero, one, zero_peer, one_peer, states, grads):
    rows = slice(3 * TOK, 4 * TOK)
    for item in (state_zero, state_zero_peer, state_one_peer, zero, one, zero_peer, one_peer):
        item.ready()

    @pl.when(ids[0] == 0)
    def _():
        states[0] = state_zero[...]
        states[1] = state_zero_peer[...]
        grads[0] = zero[rows]
        grads[1] = zero_peer[rows]

    @pl.when(ids[0] == 1)
    def _():
        states[0] = state_one_peer[...]
        states[1] = state_one[...]
        grads[0] = one_peer[rows]
        grads[1] = one[rows]


def expert_grad_kernel(ids, *refs):
    layers = (refs[0:4], refs[4:8])
    in_out, out_out, buffer, sems = refs[8:]
    expert = pl.program_id(0)

    @pl.when(expert == 0)
    def _():
        for layer, sources in enumerate(layers):

            @pl.when(ids[0] == layer)
            def _(sources=sources):
                for e in range(2):
                    for i, source in enumerate(sources):
                        pltpu.make_async_copy(source.at[:, e], buffer.at[i, :, e], sems.at[e, i]).start()

    for e in range(2):

        @pl.when(expert == e)
        def _(e=e):
            for i, source in enumerate(layers[0]):
                pltpu.make_async_copy(source.at[:, e], buffer.at[i, :, e], sems.at[e, i]).wait()

    rows, act = [jnp.concatenate([buffer[0, i, expert], buffer[2, i, expert]], axis=0) for i in range(2)]
    pre, back = [jnp.concatenate([buffer[1, i, expert], buffer[3, i, expert]], axis=0) for i in range(2)]
    in_out[0] = dot_tn(rows, pre)
    out_out[0] = dot_tn(act, back)


def after(x, *earlier):
    return lax.optimization_barrier((x, *earlier))[0]


def exchanged(x):
    return lax.all_to_all(x.reshape(16, -1, x.shape[-1]), "dp", 0, 0, tiled=True)


def gathered_mp(x):
    return lax.all_gather(x, "mp", axis=0)


def body(
    inputs, cotangent, segments, buckets, routes, gates, attn_gain, qkv_weight, out_weight, rel_bias, ffn_gain, w_in, w_out
):
    section = lax.axis_index("section")
    ids = jnp.stack([section, lax.axis_index("mp")]).astype(jnp.int32)
    pack, halves = call(
        pack_kernel,
        [((48, PACK), bf16), ((2, 48, 512), bf16)],
        scalars=0,
        load=(0, 1, 2, 3, 4),
        args=(qkv_weight[0].transpose(1, 0, 2), out_weight[0], attn_gain, ffn_gain, rel_bias[0]),
        name="pack",
    )
    spread = call(
        spread_kernel, [((16, 48, 512), bf16)], args=(ids, halves, sent(halves[1], 0)), name="spread"
    )[0]
    w_own = lax.all_gather(pack, ("mp", "dp"), axis=0).reshape(4, WIDTH, PACK)
    in_own, out_own = w_in[0], w_out[0]
    in_other, out_other = swapped(after(in_own, spread)), swapped(after(out_own, spread))
    info = jnp.concatenate(
        [segments.astype(f32)[:, :, None], routes[0].astype(f32), gates[0], jnp.zeros((2, TOK, 3), f32)], axis=2
    )
    info_own = lax.dynamic_index_in_dim(info, section, 0, False)
    info_other = swapped(lax.dynamic_index_in_dim(info, 1 - section, 0, False))
    reverse = jnp.concatenate([buckets[0:1], buckets[1:][::-1]])
    place = jnp.arange(WIDTH, dtype=jnp.int32)
    number = jnp.where(place % 48 < 2, 2 * (place // 48) + place % 48, -1)
    onehot = (number[:, None] == reverse[None, :]).astype(bf16)

    choice = ((TOK, SLOTS), bf16)
    token_shape = ((TOK, WIDTH), bf16)
    sent_shape = ((SLOTS, WIDTH), bf16)
    middle_shape = ((TOK, WIDTH), f32)
    gain_shape = ((8, WIDTH), f32)
    pick_zero, pick_one, gated_zero, gated_one, mask, grad_sent = call(
        prepare_kernel,
        [choice, choice, choice, choice, ((TOK, TOK), f32), sent_shape],
        load=(4,),
        args=(ids, info_own, info_other, segments, cotangent),
        name="prepare",
    )
    half_own = after(exchanged(spread).reshape(WIDTH, 512), mask)
    half_other = swapped(half_own)
    blocks = (16, 2, CAP, WIDTH)
    arrived_one = exchanged(grad_sent).reshape(blocks)
    part_zero, gains_zero = call(
        first_kernel,
        [token_shape, gain_shape],
        load=(1,),
        args=(ids, inputs, half_own, half_other, onehot, mask),
        name="first",
    )
    middle_zero, sent_zero = call(
        dispatch_kernel,
        [middle_shape, sent_shape],
        load=(1,),
        store=(0,),
        args=(ids, inputs, after(gathered_mp(part_zero), arrived_one), gains_zero, pick_zero),
        name="dispatch_zero",
    )
    pair_shape = ((2, 2, 256, WIDTH), bf16)
    received_zero = exchanged(sent_zero).reshape(blocks)
    weights = (in_own, in_other, out_own, out_other)
    expert_scratch = [
        pltpu.VMEM((2, WIDTH, WIDTH), bf16),
        pltpu.VMEM((2, WIDTH, WIDTH), bf16),
        pltpu.SemaphoreType.DMA((2,)),
        pltpu.SemaphoreType.DMA((2,)),
    ]
    y_zero, ahead_zero, slope_zero = call(
        functools.partial(expert_kernel, "forward", 0),
        [(blocks, bf16), pair_shape, ((2, 256, WIDTH), bf16)],
        raw=(2, 3, 4, 5),
        store=(1, 2),
        scratch=expert_scratch,
        args=(ids, received_zero, *weights),
        name="experts_zero",
        limit=20,
    )
    w_own = after(w_own, y_zero)
    w_other = swapped(w_own)

    def combined(matrix, back, name):
        return call(
            combine_kernel, [token_shape], scalars=0, args=(matrix, back.reshape(SLOTS, WIDTH)), name=name
        )[0]

    bias_shape = ((12, TOK, TOK), bf16)
    bias_scratch = [pltpu.VMEM((4, WIDTH, TOK), bf16), pltpu.SemaphoreType.DMA]

    def biased(layer, name):
        return call(
            functools.partial(bias_kernel, layer),
            [bias_shape, gain_shape],
            raw=(1, 2),
            store=(0,),
            scratch=bias_scratch,
            args=(ids, w_own, w_other, onehot, mask),
            name=name,
        )

    bias_one, gains_one = biased(1, "bias_one")
    y_back_zero = after(exchanged(y_zero), gains_one)
    parts_zero = gathered_mp(combined(gated_zero, y_back_zero, "combine_zero"))
    kept_shapes = [token_shape, ((4, TOK, 3 * SPLIT), bf16), bias_shape, ((TOK, SPLIT), bf16)]
    weight_scratch = [pltpu.VMEM((4, WIDTH, PACK), bf16), pltpu.SemaphoreType.DMA((4,))]
    forward_scratch = [pltpu.VMEM((4, TOK, SPLIT), bf16)] + weight_scratch
    state_zero, sent_one, middle_one, normed_one, proj_one, probs_one, context_one = call(
        functools.partial(forward_kernel, 1),
        [token_shape, sent_shape, middle_shape] + kept_shapes,
        raw=(3, 4),
        load=(1, 6),
        store=(0, 2, 3, 4, 5, 6),
        scratch=forward_scratch,
        args=(ids, middle_zero, parts_zero, w_own, w_other, gains_one, bias_one, pick_one),
        name="attention_one",
        limit=20,
    )
    bias_zero = biased(0, "bias_zero")[0]
    normed_zero, proj_zero, probs_zero, context_zero = call(
        functools.partial(forward_kernel, 0),
        kept_shapes,
        raw=(2, 3),
        load=(1, 5),
        store=(0, 1, 2, 3),
        scratch=forward_scratch,
        args=(ids, inputs, w_own, after(w_other, sent_one), gains_zero, bias_zero),
        name="attention_zero",
        limit=20,
    )
    received_one = after(exchanged(sent_one).reshape(blocks), normed_zero)
    y_one, buf_one, ahead_one, behind_one = call(
        functools.partial(expert_kernel, "both", 1),
        [(blocks, bf16), (blocks, bf16), pair_shape, pair_shape],
        raw=(3, 4, 5, 6),
        store=(2, 3),
        scratch=expert_scratch,
        args=(ids, received_one, arrived_one, *weights),
        name="experts_one",
        limit=24,
    )
    ahead_zero_peer = sent(ahead_zero, 1)
    ahead_one_peer = sent(ahead_one, 0)
    behind_one_peer = sent(behind_one, 0)
    buf_back_one = exchanged(buf_one)
    y_back_one = exchanged(after(y_one, buf_back_one))
    buf_parts_one = after(gathered_mp(combined(pick_one, buf_back_one, "combine_back_one")), y_back_one)
    y_part_one = combined(gated_one, y_back_one, "combine_one")
    y_parts_one = [y_part_one] + [
        lax.ppermute(y_part_one, "mp", [(i, (i + by) % 4) for i in range(4)]) for by in range(1, 4)
    ]
    grad_scratch = [
        pltpu.VMEM((4, TOK, 3 * SPLIT), bf16),
        pltpu.VMEM((12, TOK, TOK), bf16),
        pltpu.VMEM((16, WIDTH), f32),
    ] + weight_scratch
    back_shape = ((4 * TOK + 16, WIDTH), bf16)
    grad_sent_zero, back_one = call(
        functools.partial(backward_kernel, 1),
        [sent_shape, back_shape],
        raw=(7, 8),
        load=(1, 2, 4, 5, 6, 10, 11),
        store=(1,),
        scratch=grad_scratch,
        args=(
            ids, cotangent, state_zero, buf_parts_one, middle_one, proj_one, probs_one, w_own, w_other, gains_one,
            normed_one, context_one, gated_zero
        ),
        name="attention_back_one",
        limit=24,
    )
    back_one_peer = sent(back_one, 0)
    arrived_zero = exchanged(after(grad_sent_zero, y_part_one)).reshape(blocks)
    state_one = call(
        state_kernel,
        [token_shape],
        load=(1,),
        scratch=[pltpu.VMEM((4, TOK, WIDTH), bf16)],
        args=(ids, middle_one, *y_parts_one),
        name="state_one",
    )[0]
    arrived_zero = after(arrived_zero, ahead_zero_peer, ahead_one_peer, *y_parts_one)
    buf_zero, behind_zero = call(
        functools.partial(expert_kernel, "backward", 0),
        [(blocks, bf16), pair_shape],
        raw=(3, 4, 5, 6),
        load=(1,),
        store=(1,),
        scratch=expert_scratch,
        args=(ids, slope_zero, arrived_zero, *weights),
        name="experts_back_zero",
        limit=20,
    )
    behind_zero_peer = sent(behind_zero, 1)
    buf_back_zero = after(exchanged(buf_zero), back_one_peer, behind_one_peer)
    buf_parts_zero = gathered_mp(combined(pick_zero, buf_back_zero, "combine_back_zero"))
    back_zero = call(
        functools.partial(backward_kernel, 0),
        [back_shape],
        raw=(7, 8),
        load=(1, 2, 4, 5, 6, 10, 11),
        scratch=grad_scratch,
        args=(
            ids, back_one, inputs, buf_parts_zero, middle_zero, proj_zero, probs_zero, w_own, w_other, gains_zero,
            normed_zero, context_zero
        ),
        name="attention_back_zero",
        limit=24,
    )[0]
    back_zero_peer = sent(back_zero, 1)
    packed = call(
        weight_grad_kernel,
        [((16, 48, PACK), bf16)],
        load=(3, 4),
        args=(ids, back_zero, back_zero_peer, back_one, back_one_peer, onehot),
        name="attention_grads",
    )[0]
    shares = exchanged(packed)
    in_grad, out_grad = pl.pallas_call(
        expert_grad_kernel,
        out_shape=[jax.ShapeDtypeStruct((2, WIDTH, WIDTH), f32)] * 2,
        grid=(2,),
        in_specs=[pl.BlockSpec(memory_space=pltpu.SMEM)] + [pl.BlockSpec(memory_space=pltpu.HBM)] * 8,
        out_specs=[pl.BlockSpec((1, WIDTH, WIDTH), lambda e: (e, 0, 0))] * 2,
        scratch_shapes=[pltpu.VMEM((4, 2, 2, 256, WIDTH), bf16), pltpu.SemaphoreType.DMA((2, 4))],
        compiler_params=pltpu.CompilerParams(vmem_limit_bytes=24 * 1024 * 1024),
        name="expert_grads",
    )(
        ids,
        *map(far, (
        ahead_zero, behind_zero, ahead_zero_peer, behind_zero_peer, ahead_one, behind_one, ahead_one_peer,
        behind_one_peer
        ))
    )
    states, input_grads = call(
        assemble_kernel,
        [((2, TOK, WIDTH), bf16)] * 2,
        load=(1, 3, 4, 5, 6, 7, 8),
        args=(
            ids, state_zero, state_one, sent(state_zero, 1), sent(state_one, 0), back_zero, back_one, back_zero_peer,
            back_one_peer
        ),
        name="assemble",
    )
    qkv_grad, out_grad_part, extra = call(
        sum_kernel,
        [((3, 48, SPLIT), f32), ((48, SPLIT), f32), ((8, 48), f32)],
        scalars=0,
        args=(after(shares, in_grad, input_grads),),
        name="sum_grads",
    )
    return (
        states[None],
        input_grads[None],
        extra[0:1],
        qkv_grad.transpose(1, 0, 2)[None],
        out_grad_part[None],
        extra[2:5, 0:2].T[None],
        extra[1:2],
        in_grad[None],
        out_grad[None],
    )


def solution(mesh):
    return jax.shard_map(
        body,
        mesh=mesh,
        in_specs=(
            P(None, "dp", None),
            P(None, "dp", None),
            P(None, "dp"),
            P(),
            P("section", None, "dp", None),
            P("section", None, "dp", None),
            P("section", "dp"),
            P("section", "dp", None, "mp"),
            P("section", "dp", "mp"),
            P("section", "dp", "mp"),
            P("section", "dp"),
            P("section", "dp", None, "mp"),
            P("section", "dp", "mp", None),
        ),
        out_specs=(
            P("section", None, "dp", None),
            P("section", None, "dp", None),
            P("section", "dp"),
            P("section", "dp", None, "mp"),
            P("section", "dp", "mp"),
            P("section", "dp", "mp"),
            P("section", "dp"),
            P("section", "dp", None, "mp"),
            P("section", "dp", "mp", None),
        ),
        check_vma=False,
    )
```

time: 408 us -> 330 us (0.81)
  waiting for transfers between devices: 89.9 us -> 44.8 us
  blocking collectives: 107 us -> 73.9 us
  local copies, waits for them, and re-layouts: 35.3 us -> 2.35 us
  Pallas kernels: 71.4 us -> 100 us
  starting transfers between devices: 81.6 us -> 92.4 us
  other arithmetic: 5.76 us -> 0.44 us
    all_gather x1, waiting for transfers between devices: 73.1 us -> 2.49 us  [body(): w_own = lax.all_gather(pack, ('mp', 'dp'), axis=0).reshape(4, WIDTH, PACK)]
    all_to_all x4 -> x1, blocking collectives: 60 us -> 25.4 us  [exchanged(): lax.all_to_all(x.reshape(16, -1, x.shape[-1]), 'dp', 0, 0, tiled=True)]
    pallas_call x15 -> x22, Pallas kernels: 63.3 us -> 92.9 us  [call(): pl.pallas_call(wrapped, out_shape=[pltpu.HBM(shape, dtype) if i in store...]
    unnamed x132 -> x20, local copies, waits for them, and re-layouts: 28.2 us -> 0.72 us
    all_to_all x5 -> x9, starting transfers between devices: 27.3 us -> 48.5 us  [exchanged(): lax.all_to_all(x.reshape(16, -1, x.shape[-1]), 'dp', 0, 0, tiled=True)]
    ppermute x18 -> x9, starting transfers between devices: 50.7 us -> 34.1 us  [sent(): return lax.ppermute(x, 'section', [(source, 1 - source)])]
    all_to_all x5 -> x9, waiting for transfers between devices: 12.7 us -> 26.1 us  [exchanged(): lax.all_to_all(x.reshape(16, -1, x.shape[-1]), 'dp', 0, 0, tiled=True)]
    ppermute x6 -> x5, waiting for transfers between devices: 4.06 us -> 8.19 us  [swapped(): return lax.ppermute(x, 'section', [(0, 1), (1, 0)])]
  transfers between devices with their start and end apart: 30 -> 27, of which waited for: 3 -> 13; matrix products, arithmetic and copies ran while one was open for 2% -> 0% of each run, Pallas kernels for 11% -> 21%
where the time goes in v2:
time: 330 us; the launch traced here: 328 us
  Pallas kernels  100 us (30%)
  starting transfers between devices  92.4 us (28%)
  blocking collectives  73.9 us (22%)
  waiting for transfers between devices  44.8 us (14%)
  between operations  14.5 us (4%)
    pallas_call x22, Pallas kernels, call(): pl.pallas_call(wrapped, out_shape=[pltpu.HBM(shape, dtype) if i in store...  92.9 us
    all_to_all x9, starting transfers between devices, exchanged(): lax.all_to_all(x.reshape(16, -1, x.shape[-1]), 'dp', 0, 0, tiled=True)  48.5 us
    all_gather x4, blocking collectives, gathered_mp(): return lax.all_gather(x, 'mp', axis=0)  48.5 us
    ppermute x9, starting transfers between devices, sent(): return lax.ppermute(x, 'section', [(source, 1 - source)])  34.1 us
    all_to_all x9, waiting for transfers between devices, exchanged(): lax.all_to_all(x.reshape(16, -1, x.shape[-1]), 'dp', 0, 0, tiled=True)  26.1 us
    all_to_all x1, blocking collectives, exchanged(): lax.all_to_all(x.reshape(16, -1, x.shape[-1]), 'dp', 0, 0, tiled=True)  25.4 us
    ppermute x5, waiting for transfers between devices, swapped(): return lax.ppermute(x, 'section', [(0, 1), (1, 0)])  8.19 us
    pallas_call x1, Pallas kernels, body(): pl.pallas_call(expert_grad_kernel, out_shape=[jax.ShapeDtypeStruct((2, WI...  7.19 us
  transfers between devices with their start and end apart: 27, of which 13 were waited for; matrix products, arithmetic and copies ran while one was open for 0% of the time, Pallas kernels for 21%

profile of v2, /device:TPU:1, one launch (start us, length us, event | category | flops | bytes accessed | tf_op | source)
XLA Modules:
  0.0 328.5 jit_solution(1058040523540553577)
XLA Ops:
  14.0 8.3 %all-to-all-start = ((bf16[16,48,512]{2,1,0:T(8,128)(2,1)}), bf16[16,48,512]{2,1,0:T(8,128)(2,1)S(1)}, u32[]{:S(2)}, u32[]{:S(2)}) async-start(bf16[16,48,512]{2,1,0:T(8,128)(2,1)} %spread.1), calls=%async_computation | async-start | bytes 1572864 | tf_op jit(solution)/shard_map/all_to_all | solution.py:563
  30.0 5.2 %all-to-all-done = bf16[16,48,512]{2,1,0:T(8,128)(2,1)S(1)} async-done(((bf16[16,48,512]{2,1,0:T(8,128)(2,1)}), bf16[16,48,512]{2,1,0:T(8,128)(2,1)S(1)}, u32[]{:S(2)}, u32[]{:S(2)}) %all-to-all-start) | async-done | bytes 786464 | tf_op jit(solution)/shard_map/all_to_all | solution.py:563
  46.0 14.6 %all-gather = bf16[512,768]{1,0:T(8,128)(2,1)S(1)} all-gather(bf16[128,768]{1,0:T(8,128)(2,1)S(1)} %get-tuple-element.70), channel_id=2, replica_groups=mesh['section'=2,'dp'=16,'mp'=4] {'mp'}, dimensions={0}, use_global_device_ids=true | all-gather | bytes 983040 | tf_op jit(solution)/shard_map/all_gather | solution.py:567
  63.0 25.4 %all_to_all.50 = bf16[16,32,768]{2,1,0:T(8,128)(2,1)S(1)} all-to-all(bf16[16,32,768]{2,1,0:T(8,128)(2,1)S(1)} %bitcast.65), channel_id=1, replica_groups=mesh['section'=2,'dp'=16,'mp'=4] {'dp'}, dimensions={0} | all-to-all | bytes 1572864 | tf_op jit(solution)/shard_map/all_to_all | solution.py:563
  88.5 6.7 %experts_zero.1 = (bf16[16,2,16,768]{3,2,1,0:T(8,128)(2,1)}, bf16[2,2,256,768]{3,2,1,0:T(8,128)(2,1)}, bf16[2,256,768]{2,1,0:T(8,128)(2,1)}) custom-call(s32[2]{0:T(128)S(1)} %pad_add_fusion.refs_0_.ids, bf16[16,2,16,768]{3,2,1,0:T(8,128)(2,1)S(1)} %bitcast.54, bf16[2,768,768]{2,1,0:T(8,128)(2,1)} %bitcast.75, ...), custom_call_target="tpu_custom_call" | custom-call | tf_op jit(solution)/shard_map/experts_zero/pallas_call | solution.py:134
  104.4 4.7 %collective-permute-done.5.refs_2_.refs_4_.refs_3_.refs_8_ = bf16[4,768,896]{2,1,0:T(8,128)(2,1)} collective-permute-done((bf16[4,768,896]{2,1,0:T(8,128)(2,1)}, bf16[4,768,896]{2,1,0:T(8,128)(2,1)}, u32[]{:S(2)}, u32[]{:S(2)}) %collective-permute-start.5) | collective-permute-done | bytes 5505056 | tf_op jit(solution)/shard_map/ppermute | solution.py:47
  112.9 5.0 %all-to-all-done.3 = bf16[16,32,768]{2,1,0:T(8,128)(2,1)S(1)} async-done(((bf16[16,32,768]{2,1,0:T(8,128)(2,1)}), bf16[16,32,768]{2,1,0:T(8,128)(2,1)S(1)}, u32[]{:S(2)}, u32[]{:S(2)}) %all-to-all-start.3) | async-done | bytes 786464 | tf_op jit(solution)/shard_map/all_to_all | solution.py:563
  118.1 10.9 %all-gather.2 = bf16[512,768]{1,0:T(8,128)(2,1)S(1)} all-gather(bf16[128,768]{1,0:T(8,128)(2,1)S(1)} %combine_zero.1), channel_id=4, replica_groups=mesh['section'=2,'dp'=16,'mp'=4] {'mp'}, dimensions={0}, use_global_device_ids=true | all-gather | bytes 983040 | tf_op jit(solution)/shard_map/all_gather | solution.py:567
  129.1 9.7 %attention_one.1 = (bf16[128,768]{1,0:T(8,128)(2,1)}, bf16[512,768]{1,0:T(8,128)(2,1)}, f32[128,768]{1,0:T(8,128)}, bf16[128,768]{1,0:T(8,128)(2,1)}, bf16[4,128...) custom-call(s32[2]{0:T(128)S(1)} %pad_add_fusion.refs_0_.ids, ...), custom_call_target="tpu_custom_call" | custom-call | tf_op jit(solution)/shard_map/attention_one/pallas_call | solution.py:134
  146.9 7.5 %attention_zero.1 = (bf16[128,768]{1,0:T(8,128)(2,1)}, bf16[4,128,576]{2,1,0:T(8,128)(2,1)}, bf16[12,128,128]{2,1,0:T(8,128)(2,1)}, bf16[128,192]{1,0:T(8,128)(2,1)}) custom-call(s32[2]{0:T(128)S(1)} %pad_add_fusion.refs_0_.ids, bf16[2,128,768]{2,1,0:T(8,128)(2,1)} %refs_2_.3, bf16[4,768,896]{2,1,0:T(8,128)(2,1)} %bitcast.71, ...), custom_call_target="tpu_custom_call" | custom-call | tf_op jit(solution)/shard_map/attention_zero/pallas_call | solution.py:134
  154.4 7.9 %experts_one.1 = (bf16[16,2,16,768]{3,2,1,0:T(8,128)(2,1)}, bf16[16,2,16,768]{3,2,1,0:T(8,128)(2,1)}, bf16[2,2,256,768]{3,2,1,0:T(8,128)(2,1)}, bf16[2,2,256,768]{3,2,1,0:T(8,128)(2,1)}) custom-call(s32[2]{0:T(128)S(1)} %pad_add_fusion.refs_0_.ids, bf16[16,2,16,768]{3,2,1,0:T(8,128)(2,1)S(1)} %bitcast.64, bf16[16,2,16,768]{3,2,1,0:T(8,128)(2,1)S(1)} %bitcast.62, ...), custom_call_target="tpu_custom_call" | custom-call | tf_op jit(solution)/shard_map/experts_one/pallas_call | solution.py:134
  162.3 6.6 %all-to-all-start.5 = ((bf16[16,32,768]{2,1,0:T(8,128)(2,1)}), bf16[16,32,768]{2,1,0:T(8,128)(2,1)S(1)}, u32[]{:S(2)}, u32[]{:S(2)}) async-start(bf16[16,32,768]{2,1,0:T(8,128)(2,1)} %bitcast.26), calls=%async_computation.5 | async-start | bytes 1572864 | tf_op jit(solution)/shard_map/all_to_all | solution.py:563
  168.9 8.5 %collective-permute-start.11 = (bf16[2,2,256,768]{3,2,1,0:T(8,128)(2,1)}, bf16[2,2,256,768]{3,2,1,0:T(8,128)(2,1)}, u32[]{:S(2)}, u32[]{:S(2)}) collective-permute-start(bf16[2,2,256,768]{3,2,1,0:T(8,128)(2,1)} %get-tuple-element.107.refs_0_), channel_id=1, source_target_pairs={{64,0},{65,1},{66,2},{67,3},{68,4},{69,5},{70,6},{71,7},{72,8},{73... | collective-permute-start | bytes 4718600 | tf_op jit(solution)/shard_map/ppermute | solution.py:51
  179.3 6.4 %all-to-all-start.6 = ((bf16[16,32,768]{2,1,0:T(8,128)(2,1)}), bf16[16,32,768]{2,1,0:T(8,128)(2,1)S(1)}, u32[]{:S(2)}, u32[]{:S(2)}) async-start(bf16[16,32,768]{2,1,0:T(8,128)(2,1)} %bitcast.27), calls=%async_computation.6 | async-start | bytes 1572864 | tf_op jit(solution)/shard_map/all_to_all | solution.py:563
  187.2 12.0 %all-gather.3 = bf16[512,768]{1,0:T(8,128)(2,1)S(1)} all-gather(bf16[128,768]{1,0:T(8,128)(2,1)S(1)} %combine_back_one.1), channel_id=5, replica_groups=mesh['section'=2,'dp'=16,'mp'=4] {'mp'}, dimensions={0}, use_global_device_ids=true | all-gather | bytes 983040 | tf_op jit(solution)/shard_map/all_gather | solution.py:567
  199.5 12.7 %attention_back_one.1 = (bf16[512,768]{1,0:T(8,128)(2,1)}, bf16[528,768]{1,0:T(8,128)(2,1)}) custom-call(s32[2]{0:T(128)S(1)} %pad_add_fusion.refs_0_.ids, bf16[2,128,768]{2,1,0:T(8,128)(2,1)} %refs_1_.7, bf16[128,768]{1,0:T(8,128)(2,1)} %get-tuple-element.87.refs_2_.refs_1_, bf16[4,128,768]{2,1,0:T(8,128)(2,1)S(1)} %bitcast.57, ...), custom_call_target="tpu_custom_call" | custom-call | tf_op jit(solution)/shard_map/attention_back_one/pallas_call | solution.py:134
  212.2 6.9 %all-to-all-start.7 = ((bf16[16,32,768]{2,1,0:T(8,128)(2,1)}), bf16[16,32,768]{2,1,0:T(8,128)(2,1)S(1)}, u32[]{:S(2)}, u32[]{:S(2)}) async-start(bf16[16,32,768]{2,1,0:T(8,128)(2,1)} %bitcast.31), calls=%async_computation.7 | async-start | bytes 1572864 | tf_op jit(solution)/shard_map/all_to_all | solution.py:563
  229.5 6.3 %experts_back_zero.1 = (bf16[16,2,16,768]{3,2,1,0:T(8,128)(2,1)}, bf16[2,2,256,768]{3,2,1,0:T(8,128)(2,1)}) custom-call(s32[2]{0:T(128)S(1)} %pad_add_fusion.refs_0_.ids, bf16[2,256,768]{2,1,0:T(8,128)(2,1)} %get-tuple-element.104.refs_1_, bf16[16,2,16,768]{3,2,1,0:T(8,128)(2,1)S(1)} %bitcast.63, bf16[2,768,768]{2,1,0:T(8,128)(2,1)} %bitcast.77, ...), custom_call_target="tpu_custom_call" | custom-call | tf_op jit(solution)/shard_map/experts_back_zero/pallas_call | solution.py:134
  235.8 4.8 %all-to-all-start.8 = ((bf16[16,32,768]{2,1,0:T(8,128)(2,1)}), bf16[16,32,768]{2,1,0:T(8,128)(2,1)S(1)}, u32[]{:S(2)}, u32[]{:S(2)}) async-start(bf16[16,32,768]{2,1,0:T(8,128)(2,1)} %bitcast.33), calls=%async_computation.8 | async-start | bytes 1572864 | tf_op jit(solution)/shard_map/all_to_all | solution.py:563
  240.6 10.3 %all-to-all-done.8 = bf16[16,32,768]{2,1,0:T(8,128)(2,1)S(1)} async-done(((bf16[16,32,768]{2,1,0:T(8,128)(2,1)}), bf16[16,32,768]{2,1,0:T(8,128)(2,1)S(1)}, u32[]{:S(2)}, u32[]{:S(2)}) %all-to-all-start.8) | async-done | bytes 786464 | tf_op jit(solution)/shard_map/all_to_all | solution.py:563
  251.2 11.0 %all-gather.4 = bf16[512,768]{1,0:T(8,128)(2,1)S(1)} all-gather(bf16[128,768]{1,0:T(8,128)(2,1)S(1)} %combine_back_zero.1), channel_id=6, replica_groups=mesh['section'=2,'dp'=16,'mp'=4] {'mp'}, dimensions={0}, use_global_device_ids=true | all-gather | bytes 983040 | tf_op jit(solution)/shard_map/all_gather | solution.py:567
  262.2 10.7 %attention_back_zero.1.refs_5_.refs_1_ = bf16[528,768]{1,0:T(8,128)(2,1)S(1)} custom-call(s32[2]{0:T(128)S(1)} %pad_add_fusion.refs_0_.ids, bf16[528,768]{1,0:T(8,128)(2,1)} %get-tuple-element.103.refs_1_.refs_6_.refs_3_, bf16[2,128,768]{2,1,0:T(8,128)(2,1)} %refs_2_.3, bf16[4,128,768]{2,1,0:T(8,128)(2,1)S(1)} %bitcast.51, ...), custom_call_target="tpu_custom_call" | custom-call | tf_op jit(solution)/shard_map/attention_back_zero/pallas_call | solution.py:134
  272.9 14.9 %collective-permute-start.15 = (bf16[528,768]{1,0:T(8,128)(2,1)S(1)}, bf16[528,768]{1,0:T(8,128)(2,1)S(1)}, u32[]{:S(2)}, u32[]{:S(2)}) collective-permute-start(bf16[528,768]{1,0:T(8,128)(2,1)S(1)} %attention_back_zero.1.refs_5_.refs_1_), channel_id=1, source_target_pairs={{64,0},{65,1},{66,2},{67,3},{68,4},{69,5},{70,6},{71,7},{72,8},{73... | collective-permute-start | bytes 2433032 | tf_op jit(solution)/shard_map/ppermute | solution.py:51
  309.2 7.2 %expert_grads.1 = (f32[2,768,768]{2,1,0:T(8,128)}, f32[2,768,768]{2,1,0:T(8,128)}) custom-call(s32[2]{0:T(128)S(1)} %pad_add_fusion.refs_0_.ids, bf16[2,2,256,768]{3,2,1,0:T(8,128)(2,1)} %get-tuple-element.107.refs_0_, bf16[2,2,256,768]{3,2,1,0:T(8,128)(2,1)} %get-tuple-element.118.refs_1_, bf16[2,2,256,768]{3,2,1,0:T(8,128)(2,1)} %collective-permute-done.11.refs_2_, ...), custom_call_target="tpu_custom_call" | custom-call | tf_op jit(solution)/shard_map/expert_grads/pallas_call | solution.py:788
  (97 shorter events, 89.8 us)
Async XLA Ops:
  7.2 90.5 %all-gather.7.cloned.1.call-start = ((), (), s32[]{:S(2)}) async-start(), calls=%async_computation.10 | async-start | bytes 5591040 | tf_op jit(solution)/shard_map/all_gather | solution.py:586
  14.0 21.3 %all-to-all-start = ((bf16[16,48,512]{2,1,0:T(8,128)(2,1)}), bf16[16,48,512]{2,1,0:T(8,128)(2,1)S(1)}, u32[]{:S(2)}, u32[]{:S(2)}) async-start(bf16[16,48,512]{2,1,0:T(8,128)(2,1)} %spread.1), calls=%async_computation | async-start | bytes 1572864 | tf_op jit(solution)/shard_map/all_to_all | solution.py:563
  22.4 66.1 %collective-permute-start.3 = (bf16[2,768,768]{2,1,0:T(8,128)(2,1)}, bf16[2,768,768]{2,1,0:T(8,128)(2,1)}, u32[]{:S(2)}, u32[]{:S(2)}) collective-permute-start(bf16[2,768,768]{2,1,0:T(8,128)(2,1)} %bitcast.74), channel_id=1, source_target_pairs={{0,64},{64,0},{1,65},{65,1},{2,66},{66,2},{3,67},{67,3},{4,68},{68... | collective-permute-start | bytes 7077896 | tf_op jit(solution)/shard_map/ppermute | solution.py:47
  22.9 65.6 %collective-permute-start.4 = (bf16[2,768,768]{2,1,0:T(8,128)(2,1)}, bf16[2,768,768]{2,1,0:T(8,128)(2,1)}, u32[]{:S(2)}, u32[]{:S(2)}) collective-permute-start(bf16[2,768,768]{2,1,0:T(8,128)(2,1)} %bitcast.78), channel_id=1, source_target_pairs={{0,64},{64,0},{1,65},{65,1},{2,66},{66,2},{3,67},{67,3},{4,68},{68... | collective-permute-start | bytes 7077896 | tf_op jit(solution)/shard_map/ppermute | solution.py:47
  35.2 7.1 %collective-permute-start.2 = (bf16[768,512]{1,0:T(8,128)(2,1)S(1)}, bf16[768,512]{1,0:T(8,128)(2,1)S(1)}, u32[]{:S(2)}, u32[]{:S(2)}) collective-permute-start(bf16[768,512]{1,0:T(8,128)(2,1)S(1)} %bitcast.52), channel_id=1, source_target_pairs={{0,64},{64,0},{1,65},{65,1},{2,66},{66,2},{3,67},{67,3},{4,68},{68... | collective-permute-start | bytes 2359304 | tf_op jit(solution)/shard_map/ppermute | solution.py:47
  38.4 22.1 %all-to-all-start.1 = ((bf16[16,32,768]{2,1,0:T(8,128)(2,1)}), bf16[16,32,768]{2,1,0:T(8,128)(2,1)S(1)}, u32[]{:S(2)}, u32[]{:S(2)}) async-start(bf16[16,32,768]{2,1,0:T(8,128)(2,1)} %bitcast.14), calls=%async_computation.1 | async-start | bytes 1572864 | tf_op jit(solution)/shard_map/all_to_all | solution.py:563
  97.7 11.4 %collective-permute-start.5 = (bf16[4,768,896]{2,1,0:T(8,128)(2,1)}, bf16[4,768,896]{2,1,0:T(8,128)(2,1)}, u32[]{:S(2)}, u32[]{:S(2)}) collective-permute-start(bf16[4,768,896]{2,1,0:T(8,128)(2,1)} %bitcast.67), channel_id=1, source_target_pairs={{0,64},{64,0},{1,65},{65,1},{2,66},{66,2},{3,67},{67,3},{4,68},{68... | collective-permute-start | bytes 16515080 | tf_op jit(solution)/shard_map/ppermute | solution.py:47
  100.1 17.7 %all-to-all-start.3 = ((bf16[16,32,768]{2,1,0:T(8,128)(2,1)}), bf16[16,32,768]{2,1,0:T(8,128)(2,1)S(1)}, u32[]{:S(2)}, u32[]{:S(2)}) async-start(bf16[16,32,768]{2,1,0:T(8,128)(2,1)} %bitcast.20), calls=%async_computation.3 | async-start | bytes 1572864 | tf_op jit(solution)/shard_map/all_to_all | solution.py:563
  138.8 15.6 %all-to-all-start.4 = ((bf16[16,32,768]{2,1,0:T(8,128)(2,1)}), bf16[16,32,768]{2,1,0:T(8,128)(2,1)S(1)}, u32[]{:S(2)}, u32[]{:S(2)}) async-start(bf16[16,32,768]{2,1,0:T(8,128)(2,1)} %bitcast.24), calls=%async_computation.4 | async-start | bytes 1572864 | tf_op jit(solution)/shard_map/all_to_all | solution.py:563
  162.3 17.0 %all-to-all-start.5 = ((bf16[16,32,768]{2,1,0:T(8,128)(2,1)}), bf16[16,32,768]{2,1,0:T(8,128)(2,1)S(1)}, u32[]{:S(2)}, u32[]{:S(2)}) async-start(bf16[16,32,768]{2,1,0:T(8,128)(2,1)} %bitcast.26), calls=%async_computation.5 | async-start | bytes 1572864 | tf_op jit(solution)/shard_map/all_to_all | solution.py:563
  168.9 51.8 %collective-permute-start.11 = (bf16[2,2,256,768]{3,2,1,0:T(8,128)(2,1)}, bf16[2,2,256,768]{3,2,1,0:T(8,128)(2,1)}, u32[]{:S(2)}, u32[]{:S(2)}) collective-permute-start(bf16[2,2,256,768]{3,2,1,0:T(8,128)(2,1)} %get-tuple-element.107.refs_0_), channel_id=1, source_target_pairs={{64,0},{65,1},{66,2},{67,3},{68,4},{69,5},{70,6},{71,7},{72,8},{73... | collective-permute-start | bytes 4718600 | tf_op jit(solution)/shard_map/ppermute | solution.py:51
  177.4 45.0 %collective-permute-start.12 = (bf16[2,2,256,768]{3,2,1,0:T(8,128)(2,1)}, bf16[2,2,256,768]{3,2,1,0:T(8,128)(2,1)}, u32[]{:S(2)}, u32[]{:S(2)}) collective-permute-start(bf16[2,2,256,768]{3,2,1,0:T(8,128)(2,1)} %get-tuple-element.108.refs_4_), channel_id=1, source_target_pairs={{0,64},{1,65},{2,66},{3,67},{4,68},{5,69},{6,70},{7,71},{8,72},{9,... | collective-permute-start | bytes 4718600 | tf_op jit(solution)/shard_map/ppermute | solution.py:51
  179.3 19.9 %all-to-all-start.6 = ((bf16[16,32,768]{2,1,0:T(8,128)(2,1)}), bf16[16,32,768]{2,1,0:T(8,128)(2,1)S(1)}, u32[]{:S(2)}, u32[]{:S(2)}) async-start(bf16[16,32,768]{2,1,0:T(8,128)(2,1)} %bitcast.27), calls=%async_computation.6 | async-start | bytes 1572864 | tf_op jit(solution)/shard_map/all_to_all | solution.py:563
  185.7 54.9 %collective-permute-start.14 = (bf16[2,2,256,768]{3,2,1,0:T(8,128)(2,1)}, bf16[2,2,256,768]{3,2,1,0:T(8,128)(2,1)}, u32[]{:S(2)}, u32[]{:S(2)}) collective-permute-start(bf16[2,2,256,768]{3,2,1,0:T(8,128)(2,1)} %get-tuple-element.111.refs_5_), channel_id=1, source_target_pairs={{0,64},{1,65},{2,66},{3,67},{4,68},{5,69},{6,70},{7,71},{8,72},{9,... | collective-permute-start | bytes 4718600 | tf_op jit(solution)/shard_map/ppermute | solution.py:51
  212.2 17.2 %all-to-all-start.7 = ((bf16[16,32,768]{2,1,0:T(8,128)(2,1)}), bf16[16,32,768]{2,1,0:T(8,128)(2,1)S(1)}, u32[]{:S(2)}, u32[]{:S(2)}) async-start(bf16[16,32,768]{2,1,0:T(8,128)(2,1)} %bitcast.31), calls=%async_computation.7 | async-start | bytes 1572864 | tf_op jit(solution)/shard_map/all_to_all | solution.py:563
  219.1 7.9 %collective-permute-start.6 = (bf16[128,768]{1,0:T(8,128)(2,1)S(1)}, bf16[128,768]{1,0:T(8,128)(2,1)S(1)}, u32[]{:S(2)}, u32[]{:S(2)}) collective-permute-start(bf16[128,768]{1,0:T(8,128)(2,1)S(1)} %combine_one.1.refs_2_), channel_id=1, source_target_pairs={{0,1},{1,2},{2,3},{3,0},{4,5},{5,6},{6,7},{7,4},{8,9},{9,10},{10,1... | collective-permute-start | bytes 589832 | tf_op jit(solution)/shard_map/ppermute | solution.py:719
  219.2 7.8 %collective-permute-start.7 = (bf16[128,768]{1,0:T(8,128)(2,1)S(1)}, bf16[128,768]{1,0:T(8,128)(2,1)S(1)}, u32[]{:S(2)}, u32[]{:S(2)}) collective-permute-start(bf16[128,768]{1,0:T(8,128)(2,1)S(1)} %combine_one.1.refs_2_), channel_id=1, source_target_pairs={{0,2},{1,3},{2,0},{3,1},{4,6},{5,7},{6,4},{7,5},{8,10},{9,11},{10,... | collective-permute-start | bytes 589832 | tf_op jit(solution)/shard_map/ppermute | solution.py:719
  220.7 7.0 %collective-permute-start.8 = (bf16[128,768]{1,0:T(8,128)(2,1)S(1)}, bf16[128,768]{1,0:T(8,128)(2,1)S(1)}, u32[]{:S(2)}, u32[]{:S(2)}) collective-permute-start(bf16[128,768]{1,0:T(8,128)(2,1)S(1)} %combine_one.1.refs_2_), channel_id=1, source_target_pairs={{0,3},{1,0},{2,1},{3,2},{4,7},{5,4},{6,5},{7,6},{8,11},{9,8},{10,9... | collective-permute-start | bytes 589832 | tf_op jit(solution)/shard_map/ppermute | solution.py:719
  222.4 18.1 %collective-permute-start.13 = (bf16[528,768]{1,0:T(8,128)(2,1)S(1)}, bf16[528,768]{1,0:T(8,128)(2,1)}, u32[]{:S(2)}, u32[]{:S(2)}) collective-permute-start(bf16[528,768]{1,0:T(8,128)(2,1)S(1)} %copy-done.3), channel_id=1, source_target_pairs={{0,64},{1,65},{2,66},{3,67},{4,68},{5,69},{6,70},{7,71},{8,72},{9,... | collective-permute-start | bytes 2433032 | tf_op jit(solution)/shard_map/ppermute | solution.py:51
  235.8 15.1 %all-to-all-start.8 = ((bf16[16,32,768]{2,1,0:T(8,128)(2,1)}), bf16[16,32,768]{2,1,0:T(8,128)(2,1)S(1)}, u32[]{:S(2)}, u32[]{:S(2)}) async-start(bf16[16,32,768]{2,1,0:T(8,128)(2,1)} %bitcast.33), calls=%async_computation.8 | async-start | bytes 1572864 | tf_op jit(solution)/shard_map/all_to_all | solution.py:563
  272.9 17.4 %collective-permute-start.15 = (bf16[528,768]{1,0:T(8,128)(2,1)S(1)}, bf16[528,768]{1,0:T(8,128)(2,1)S(1)}, u32[]{:S(2)}, u32[]{:S(2)}) collective-permute-start(bf16[528,768]{1,0:T(8,128)(2,1)S(1)} %attention_back_zero.1.refs_5_.refs_1_), channel_id=1, source_target_pairs={{64,0},{65,1},{66,2},{67,3},{68,4},{69,5},{70,6},{71,7},{72,8},{73... | collective-permute-start | bytes 2433032 | tf_op jit(solution)/shard_map/ppermute | solution.py:51
  287.8 21.4 %collective-permute-start.16 = (bf16[2,2,256,768]{3,2,1,0:T(8,128)(2,1)}, bf16[2,2,256,768]{3,2,1,0:T(8,128)(2,1)}, u32[]{:S(2)}, u32[]{:S(2)}) collective-permute-start(bf16[2,2,256,768]{3,2,1,0:T(8,128)(2,1)} %get-tuple-element.118.refs_1_), channel_id=1, source_target_pairs={{64,0},{65,1},{66,2},{67,3},{68,4},{69,5},{70,6},{71,7},{72,8},{73... | collective-permute-start | bytes 4718600 | tf_op jit(solution)/shard_map/ppermute | solution.py:51
  294.3 25.3 %all-to-all-start.9 = ((bf16[16,48,896]{2,1,0:T(8,128)(2,1)}), bf16[16,48,896]{2,1,0:T(8,128)(2,1)S(1)}, u32[]{:S(2)}, u32[]{:S(2)}) async-start(bf16[16,48,896]{2,1,0:T(8,128)(2,1)} %attention_grads.1), calls=%async_computation.9 | async-start | bytes 2752512 | tf_op jit(solution)/shard_map/all_to_all | solution.py:563
  298.1 4.7 %collective-permute-start.9 = (bf16[128,768]{1,0:T(8,128)(2,1)S(1)}, bf16[128,768]{1,0:T(8,128)(2,1)S(1)}, u32[]{:S(2)}, u32[]{:S(2)}) collective-permute-start(bf16[128,768]{1,0:T(8,128)(2,1)S(1)} %copy-done.4), channel_id=1, source_target_pairs={{64,0},{65,1},{66,2},{67,3},{68,4},{69,5},{70,6},{71,7},{72,8},{73... | collective-permute-start | bytes 589832 | tf_op jit(solution)/shard_map/ppermute | solution.py:51
  (13 other events, 127.3 us)
Sparse Core Ops, SparseCore 0:
  11.5 86.2 all-gather.6

commit v3 on v2

--- a/solution.py
+++ b/solution.py
@@ -149,20 +149,21 @@
 
 def fetch(here, own, other, buffer, sems):
     count = buffer.shape[0]
+    lanes = pl.ds(0, WIDTH)
 
     @pl.when(here)
     def _():
         for i in range(count):
-            pltpu.make_async_copy(own.at[i], buffer.at[i], sems.at[i]).start()
+            pltpu.make_async_copy(own.at[i, :, lanes], buffer.at[i], sems.at[i]).start()
 
     @pl.when(jnp.logical_not(here))
     def _():
         for i in range(count):
-            pltpu.make_async_copy(other.at[i], buffer.at[i], sems.at[i]).start()
+            pltpu.make_async_copy(other.at[i, :, lanes], buffer.at[i], sems.at[i]).start()
 
     def arrived():
         for i in range(count):
-            pltpu.make_async_copy(own.at[i], buffer.at[i], sems.at[i]).wait()
+            pltpu.make_async_copy(own.at[i, :, lanes], buffer.at[i], sems.at[i]).wait()
 
     return arrived
 
@@ -356,31 +357,44 @@
     else:
         slope_in, arrived_grad, in_own, in_other, out_own, out_other, buf_out, behind = refs[:8]
     w_in, w_out, in_sems, out_sems = refs[-4:]
-    in_arrived = fetch(ids[0] == layer, in_own, in_other, w_in, in_sems)
-    out_arrived = fetch(ids[0] == layer, out_own, out_other, w_out, out_sems)
-    in_arrived()
-    out_arrived()
-    for e in range(2):
-        if mode != "backward":
+    here = ids[0] == layer
+    if mode == "backward":
+        out_arrived = fetch(here, out_own, out_other, w_out, out_sems)
+        in_arrived = fetch(here, in_own, in_other, w_in, in_sems)
+        slopes = [slope_in[e].astype(f32) for e in range(2)]
+        out_arrived()
+    else:
+        in_arrived = fetch(here, in_own, in_other, w_in, in_sems)
+        out_arrived = fetch(here, out_own, out_other, w_out, out_sems)
+        in_arrived()
+        acts, slopes = [], []
+        for e in range(2):
             rows = rows_of(received, e)
             value, slope = gelu_both(dot(rows, w_in[e]))
-            act = value.astype(bf16)
+            acts.append(value.astype(bf16))
+            slopes.append(slope)
             ahead[0, e] = rows
-            ahead[1, e] = act
-            ahead.start(slice(None), e)
-            y_out[:, e] = dot(act, w_out[e]).astype(bf16).reshape(16, CAP, WIDTH)
+            ahead[1, e] = acts[e]
             if mode == "forward":
                 slope_out[e] = slope.astype(bf16)
-                slope_out.start(e)
-        else:
-            slope = slope_in[e].astype(f32)
-        if mode != "forward":
+        ahead.start()
+        if mode == "forward":
+            slope_out.start()
+        out_arrived()
+        for e in range(2):
+            y_out[:, e] = dot(acts[e], w_out[e]).astype(bf16).reshape(16, CAP, WIDTH)
+    if mode != "forward":
+        pres = []
+        for e in range(2):
             back = rows_of(arrived_grad, e)
-            pre = (dot_nt(back, w_out[e]) * slope).astype(bf16)
-            behind[0, e] = pre
+            pres.append((dot_nt(back, w_out[e]) * slopes[e]).astype(bf16))
+            behind[0, e] = pres[e]
             behind[1, e] = back
-            behind.start(slice(None), e)
-            buf_out[:, e] = dot_nt(pre, w_in[e]).astype(bf16).reshape(16, CAP, WIDTH)
+        behind.start()
+        if mode == "backward":
+            in_arrived()
+        for e in range(2):
+            buf_out[:, e] = dot_nt(pres[e], w_in[e]).astype(bf16).reshape(16, CAP, WIDTH)
 
 
 def combine_kernel(matrix, returned, out):
@@ -475,13 +489,19 @@
     bundle[4 * TOK :] = small_out[...].astype(bf16)
 
 
-def weight_grad_kernel(ids, zero, zero_peer, one, one_peer, onehot, out):
-    one.ready()
-    one_peer.ready()
-    for layer, (mine, peer) in enumerate(((zero, zero_peer), (one, one_peer))):
+def weight_grad_kernel(ids, zero, zero_peer, one, one_peer, onehot, out, buffer, sems):
+    for layer in range(2):
 
         @pl.when(ids[0] == layer)
-        def _(mine=mine, peer=peer):
+        def _(layer=layer):
+            mine, peer = zero, zero_peer
+            if layer == 1:
+                copies = [pltpu.make_async_copy(x, buffer.at[i], sems.at[i]) for i, x in enumerate((one, one_peer))]
+                for copy in copies:
+                    copy.start()
+                for copy in copies:
+                    copy.wait()
+                mine, peer = buffer.at[0], buffer.at[1]
             both = [jnp.concatenate([mine[i * TOK : i * TOK + TOK], peer[i * TOK : i * TOK + TOK]], axis=0) for i in range(3)]
             normed, attn, third = both
             left = dot_tn(normed, third[:, : 3 * SPLIT])
@@ -497,14 +517,17 @@
             out[...] = jnp.concatenate([left, right, extra], axis=1).astype(bf16).reshape(16, 48, PACK)
 
 
-def sum_kernel(received, qkv, out_part, extra):
+def sum_kernel(received, qkv, out_part, gain_one, gain_two, table):
     total = received[0].astype(f32)
     for i in range(1, 16):
         total = total + received[i].astype(f32)
     for c in range(3):
         qkv[c] = total[:, c * SPLIT : (c + 1) * SPLIT]
     out_part[...] = total[:, 3 * SPLIT : WIDTH]
-    extra[...] = total[:, WIDTH:].T[0:8, :]
+    rows = total[:, WIDTH:].T
+    gain_one[...] = rows[0:1, :]
+    gain_two[...] = rows[1:2, :]
+    table[...] = total[0:2, WIDTH + 2 : WIDTH + 5]
 
 
 def assemble_kernel(ids, state_zero, state_one, state_zero_peer, state_one_peer, zero, one, zero_peer, one_peer, states, grads):
@@ -672,7 +695,7 @@
     y_back_zero = after(exchanged(y_zero), gains_one)
     parts_zero = gathered_mp(combined(gated_zero, y_back_zero, "combine_zero"))
     kept_shapes = [token_shape, ((4, TOK, 3 * SPLIT), bf16), bias_shape, ((TOK, SPLIT), bf16)]
-    weight_scratch = [pltpu.VMEM((4, WIDTH, PACK), bf16), pltpu.SemaphoreType.DMA((4,))]
+    weight_scratch = [pltpu.VMEM((4, WIDTH, WIDTH), bf16), pltpu.SemaphoreType.DMA((4,))]
     forward_scratch = [pltpu.VMEM((4, TOK, SPLIT), bf16)] + weight_scratch
     state_zero, sent_one, middle_one, normed_one, proj_one, probs_one, context_one = call(
         functools.partial(forward_kernel, 1),
@@ -748,7 +771,7 @@
         args=(ids, middle_one, *y_parts_one),
         name="state_one",
     )[0]
-    arrived_zero = after(arrived_zero, ahead_zero_peer, ahead_one_peer, *y_parts_one)
+    arrived_zero = after(arrived_zero, ahead_zero_peer, ahead_one_peer, behind_one_peer, *y_parts_one)
     buf_zero, behind_zero = call(
         functools.partial(expert_kernel, "backward", 0),
         [(blocks, bf16), pair_shape],
@@ -760,8 +783,7 @@
         name="experts_back_zero",
         limit=20,
     )
-    behind_zero_peer = sent(behind_zero, 1)
-    buf_back_zero = after(exchanged(buf_zero), back_one_peer, behind_one_peer)
+    buf_back_zero = after(exchanged(buf_zero), back_one_peer)
     buf_parts_zero = gathered_mp(combined(pick_zero, buf_back_zero, "combine_back_zero"))
     back_zero = call(
         functools.partial(backward_kernel, 0),
@@ -780,11 +802,13 @@
     packed = call(
         weight_grad_kernel,
         [((16, 48, PACK), bf16)],
-        load=(3, 4),
+        raw=(3, 4),
+        scratch=[pltpu.VMEM((2,) + back_shape[0], bf16), pltpu.SemaphoreType.DMA((2,))],
         args=(ids, back_zero, back_zero_peer, back_one, back_one_peer, onehot),
         name="attention_grads",
     )[0]
     shares = exchanged(packed)
+    behind_zero_peer = sent(after(behind_zero, packed), 1)
     in_grad, out_grad = pl.pallas_call(
         expert_grad_kernel,
         out_shape=[jax.ShapeDtypeStruct((2, WIDTH, WIDTH), f32)] * 2,
@@ -811,9 +835,9 @@
         ),
         name="assemble",
     )
-    qkv_grad, out_grad_part, extra = call(
+    qkv_grad, out_grad_part, gain_one_grad, gain_two_grad, table_grad = call(
         sum_kernel,
-        [((3, 48, SPLIT), f32), ((48, SPLIT), f32), ((8, 48), f32)],
+        [((3, 48, SPLIT), f32), ((48, SPLIT), f32), ((1, 48), f32), ((1, 48), f32), ((2, 3), f32)],
         scalars=0,
         args=(after(shares, in_grad, input_grads),),
         name="sum_grads",
@@ -821,11 +845,11 @@
     return (
         states[None],
         input_grads[None],
-        extra[0:1],
+        gain_one_grad,
         qkv_grad.transpose(1, 0, 2)[None],
         out_grad_part[None],
-        extra[2:5, 0:2].T[None],
-        extra[1:2],
+        table_grad[None],
+        gain_two_grad,
         in_grad[None],
         out_grad[None],
     )

time: 330 us -> 326 us (0.988)
  transfers between devices with their start and end apart: 27 -> 27, of which waited for: 13 -> 13; matrix products, arithmetic and copies ran while one was open for 0% -> 0% of each run, Pallas kernels for 21% -> 20%
where the time goes in v3:
time: 326 us; the launch traced here: 325 us
  Pallas kernels  98.4 us (30%)
  starting transfers between devices  91.7 us (28%)
  blocking collectives  73.7 us (23%)
  waiting for transfers between devices  45 us (14%)
  between operations  14.5 us (4%)
    pallas_call x22, Pallas kernels, call(): pl.pallas_call(wrapped, out_shape=[pltpu.HBM(shape, dtype) if i in store...  91.2 us
    all_to_all x9, starting transfers between devices, exchanged(): lax.all_to_all(x.reshape(16, -1, x.shape[-1]), 'dp', 0, 0, tiled=True)  49 us
    all_gather x4, blocking collectives, gathered_mp(): return lax.all_gather(x, 'mp', axis=0)  48.3 us
    ppermute x9, starting transfers between devices, sent(): return lax.ppermute(x, 'section', [(source, 1 - source)])  32.8 us
    all_to_all x1, blocking collectives, exchanged(): lax.all_to_all(x.reshape(16, -1, x.shape[-1]), 'dp', 0, 0, tiled=True)  25.4 us
    all_to_all x9, waiting for transfers between devices, exchanged(): lax.all_to_all(x.reshape(16, -1, x.shape[-1]), 'dp', 0, 0, tiled=True)  24.3 us
    ppermute x5, waiting for transfers between devices, swapped(): return lax.ppermute(x, 'section', [(0, 1), (1, 0)])  8.19 us
    pallas_call x1, Pallas kernels, body(): pl.pallas_call(expert_grad_kernel, out_shape=[jax.ShapeDtypeStruct((2, WI...  7.19 us
  transfers between devices with their start and end apart: 27, of which 13 were waited for; matrix products, arithmetic and copies ran while one was open for 0% of the time, Pallas kernels for 20%

profile of v3, /device:TPU:1, one launch (start us, length us, event | category | flops | bytes accessed | tf_op | source)
XLA Modules:
  0.0 324.9 jit_solution(6328829157308026583)
XLA Ops:
  14.0 8.3 %all-to-all-start = ((bf16[16,48,512]{2,1,0:T(8,128)(2,1)}), bf16[16,48,512]{2,1,0:T(8,128)(2,1)S(1)}, u32[]{:S(2)}, u32[]{:S(2)}) async-start(bf16[16,48,512]{2,1,0:T(8,128)(2,1)} %spread.1), calls=%async_computation | async-start | bytes 1572864 | tf_op jit(solution)/shard_map/all_to_all | solution.py:586
  30.0 5.2 %all-to-all-done = bf16[16,48,512]{2,1,0:T(8,128)(2,1)S(1)} async-done(((bf16[16,48,512]{2,1,0:T(8,128)(2,1)}), bf16[16,48,512]{2,1,0:T(8,128)(2,1)S(1)}, u32[]{:S(2)}, u32[]{:S(2)}) %all-to-all-start) | async-done | bytes 786464 | tf_op jit(solution)/shard_map/all_to_all | solution.py:586
  46.0 14.5 %all-gather = bf16[512,768]{1,0:T(8,128)(2,1)S(1)} all-gather(bf16[128,768]{1,0:T(8,128)(2,1)S(1)} %get-tuple-element.73), channel_id=2, replica_groups=mesh['section'=2,'dp'=16,'mp'=4] {'mp'}, dimensions={0}, use_global_device_ids=true | all-gather | bytes 983040 | tf_op jit(solution)/shard_map/all_gather | solution.py:590
  63.0 25.4 %all_to_all.50 = bf16[16,32,768]{2,1,0:T(8,128)(2,1)S(1)} all-to-all(bf16[16,32,768]{2,1,0:T(8,128)(2,1)S(1)} %bitcast.63), channel_id=1, replica_groups=mesh['section'=2,'dp'=16,'mp'=4] {'dp'}, dimensions={0} | all-to-all | bytes 1572864 | tf_op jit(solution)/shard_map/all_to_all | solution.py:586
  88.5 6.6 %experts_zero.1 = (bf16[16,2,16,768]{3,2,1,0:T(8,128)(2,1)}, bf16[2,2,256,768]{3,2,1,0:T(8,128)(2,1)}, bf16[2,256,768]{2,1,0:T(8,128)(2,1)}) custom-call(s32[2]{0:T(128)S(1)} %pad_add_fusion.refs_0_.ids, bf16[16,2,16,768]{3,2,1,0:T(8,128)(2,1)S(1)} %bitcast.52, bf16[2,768,768]{2,1,0:T(8,128)(2,1)} %bitcast.73, ...), custom_call_target="tpu_custom_call" | custom-call | tf_op jit(solution)/shard_map/experts_zero/pallas_call | solution.py:134
  104.3 4.7 %collective-permute-done.5.refs_2_.refs_4_.refs_3_.refs_8_ = bf16[4,768,896]{2,1,0:T(8,128)(2,1)} collective-permute-done((bf16[4,768,896]{2,1,0:T(8,128)(2,1)}, bf16[4,768,896]{2,1,0:T(8,128)(2,1)}, u32[]{:S(2)}, u32[]{:S(2)}) %collective-permute-start.5) | collective-permute-done | bytes 5505056 | tf_op jit(solution)/shard_map/ppermute | solution.py:47
  112.7 5.0 %all-to-all-done.3 = bf16[16,32,768]{2,1,0:T(8,128)(2,1)S(1)} async-done(((bf16[16,32,768]{2,1,0:T(8,128)(2,1)}), bf16[16,32,768]{2,1,0:T(8,128)(2,1)S(1)}, u32[]{:S(2)}, u32[]{:S(2)}) %all-to-all-start.3) | async-done | bytes 786464 | tf_op jit(solution)/shard_map/all_to_all | solution.py:586
  118.0 10.9 %all-gather.2 = bf16[512,768]{1,0:T(8,128)(2,1)S(1)} all-gather(bf16[128,768]{1,0:T(8,128)(2,1)S(1)} %combine_zero.1), channel_id=4, replica_groups=mesh['section'=2,'dp'=16,'mp'=4] {'mp'}, dimensions={0}, use_global_device_ids=true | all-gather | bytes 983040 | tf_op jit(solution)/shard_map/all_gather | solution.py:590
  128.9 9.5 %attention_one.1 = (bf16[128,768]{1,0:T(8,128)(2,1)}, bf16[512,768]{1,0:T(8,128)(2,1)}, f32[128,768]{1,0:T(8,128)}, bf16[128,768]{1,0:T(8,128)(2,1)}, bf16[4,128...) custom-call(s32[2]{0:T(128)S(1)} %pad_add_fusion.refs_0_.ids, ...), custom_call_target="tpu_custom_call" | custom-call | tf_op jit(solution)/shard_map/attention_one/pallas_call | solution.py:134
  146.5 7.2 %attention_zero.1 = (bf16[128,768]{1,0:T(8,128)(2,1)}, bf16[4,128,576]{2,1,0:T(8,128)(2,1)}, bf16[12,128,128]{2,1,0:T(8,128)(2,1)}, bf16[128,192]{1,0:T(8,128)(2,1)}) custom-call(s32[2]{0:T(128)S(1)} %pad_add_fusion.refs_0_.ids, bf16[2,128,768]{2,1,0:T(8,128)(2,1)} %refs_2_.3, bf16[4,768,896]{2,1,0:T(8,128)(2,1)} %bitcast.69, ...), custom_call_target="tpu_custom_call" | custom-call | tf_op jit(solution)/shard_map/attention_zero/pallas_call | solution.py:134
  153.7 7.9 %experts_one.1 = (bf16[16,2,16,768]{3,2,1,0:T(8,128)(2,1)}, bf16[16,2,16,768]{3,2,1,0:T(8,128)(2,1)}, bf16[2,2,256,768]{3,2,1,0:T(8,128)(2,1)}, bf16[2,2,256,768]{3,2,1,0:T(8,128)(2,1)}) custom-call(s32[2]{0:T(128)S(1)} %pad_add_fusion.refs_0_.ids, bf16[16,2,16,768]{3,2,1,0:T(8,128)(2,1)S(1)} %bitcast.62, bf16[16,2,16,768]{3,2,1,0:T(8,128)(2,1)S(1)} %bitcast.60, ...), custom_call_target="tpu_custom_call" | custom-call | tf_op jit(solution)/shard_map/experts_one/pallas_call | solution.py:134
  161.6 6.6 %all-to-all-start.5 = ((bf16[16,32,768]{2,1,0:T(8,128)(2,1)}), bf16[16,32,768]{2,1,0:T(8,128)(2,1)S(1)}, u32[]{:S(2)}, u32[]{:S(2)}) async-start(bf16[16,32,768]{2,1,0:T(8,128)(2,1)} %bitcast.26), calls=%async_computation.5 | async-start | bytes 1572864 | tf_op jit(solution)/shard_map/all_to_all | solution.py:586
  168.2 8.5 %collective-permute-start.11 = (bf16[2,2,256,768]{3,2,1,0:T(8,128)(2,1)}, bf16[2,2,256,768]{3,2,1,0:T(8,128)(2,1)}, u32[]{:S(2)}, u32[]{:S(2)}) collective-permute-start(bf16[2,2,256,768]{3,2,1,0:T(8,128)(2,1)} %get-tuple-element.110.refs_0_), channel_id=1, source_target_pairs={{64,0},{65,1},{66,2},{67,3},{68,4},{69,5},{70,6},{71,7},{72,8},{73... | collective-permute-start | bytes 4718600 | tf_op jit(solution)/shard_map/ppermute | solution.py:51
  179.3 6.9 %all-to-all-start.6 = ((bf16[16,32,768]{2,1,0:T(8,128)(2,1)}), bf16[16,32,768]{2,1,0:T(8,128)(2,1)S(1)}, u32[]{:S(2)}, u32[]{:S(2)}) async-start(bf16[16,32,768]{2,1,0:T(8,128)(2,1)} %bitcast.27), calls=%async_computation.6 | async-start | bytes 1572864 | tf_op jit(solution)/shard_map/all_to_all | solution.py:586
  186.5 11.8 %all-gather.3 = bf16[512,768]{1,0:T(8,128)(2,1)S(1)} all-gather(bf16[128,768]{1,0:T(8,128)(2,1)S(1)} %combine_back_one.1), channel_id=5, replica_groups=mesh['section'=2,'dp'=16,'mp'=4] {'mp'}, dimensions={0}, use_global_device_ids=true | all-gather | bytes 983040 | tf_op jit(solution)/shard_map/all_gather | solution.py:590
  198.6 12.5 %attention_back_one.1 = (bf16[512,768]{1,0:T(8,128)(2,1)}, bf16[528,768]{1,0:T(8,128)(2,1)}) custom-call(s32[2]{0:T(128)S(1)} %pad_add_fusion.refs_0_.ids, bf16[2,128,768]{2,1,0:T(8,128)(2,1)} %refs_1_.7, bf16[128,768]{1,0:T(8,128)(2,1)} %get-tuple-element.90.refs_2_.refs_1_, bf16[4,128,768]{2,1,0:T(8,128)(2,1)S(1)} %bitcast.54, ...), custom_call_target="tpu_custom_call" | custom-call | tf_op jit(solution)/shard_map/attention_back_one/pallas_call | solution.py:134
  211.1 6.7 %all-to-all-start.7 = ((bf16[16,32,768]{2,1,0:T(8,128)(2,1)}), bf16[16,32,768]{2,1,0:T(8,128)(2,1)S(1)}, u32[]{:S(2)}, u32[]{:S(2)}) async-start(bf16[16,32,768]{2,1,0:T(8,128)(2,1)} %bitcast.31), calls=%async_computation.7 | async-start | bytes 1572864 | tf_op jit(solution)/shard_map/all_to_all | solution.py:586
  228.1 5.8 %experts_back_zero.1 = (bf16[16,2,16,768]{3,2,1,0:T(8,128)(2,1)}, bf16[2,2,256,768]{3,2,1,0:T(8,128)(2,1)}) custom-call(s32[2]{0:T(128)S(1)} %pad_add_fusion.refs_0_.ids, bf16[2,256,768]{2,1,0:T(8,128)(2,1)} %get-tuple-element.107.refs_1_, bf16[16,2,16,768]{3,2,1,0:T(8,128)(2,1)S(1)} %bitcast.61, bf16[2,768,768]{2,1,0:T(8,128)(2,1)} %bitcast.75, ...), custom_call_target="tpu_custom_call" | custom-call | tf_op jit(solution)/shard_map/experts_back_zero/pallas_call | solution.py:134
  233.9 5.1 %all-to-all-start.8 = ((bf16[16,32,768]{2,1,0:T(8,128)(2,1)}), bf16[16,32,768]{2,1,0:T(8,128)(2,1)S(1)}, u32[]{:S(2)}, u32[]{:S(2)}) async-start(bf16[16,32,768]{2,1,0:T(8,128)(2,1)} %bitcast.33), calls=%async_computation.8 | async-start | bytes 1572864 | tf_op jit(solution)/shard_map/all_to_all | solution.py:586
  239.0 10.3 %all-to-all-done.8 = bf16[16,32,768]{2,1,0:T(8,128)(2,1)S(1)} async-done(((bf16[16,32,768]{2,1,0:T(8,128)(2,1)}), bf16[16,32,768]{2,1,0:T(8,128)(2,1)S(1)}, u32[]{:S(2)}, u32[]{:S(2)}) %all-to-all-start.8) | async-done | bytes 786464 | tf_op jit(solution)/shard_map/all_to_all | solution.py:586
  249.6 11.0 %all-gather.4 = bf16[512,768]{1,0:T(8,128)(2,1)S(1)} all-gather(bf16[128,768]{1,0:T(8,128)(2,1)S(1)} %combine_back_zero.1), channel_id=6, replica_groups=mesh['section'=2,'dp'=16,'mp'=4] {'mp'}, dimensions={0}, use_global_device_ids=true | all-gather | bytes 983040 | tf_op jit(solution)/shard_map/all_gather | solution.py:590
  260.6 10.4 %attention_back_zero.1.refs_5_.refs_1_ = bf16[528,768]{1,0:T(8,128)(2,1)S(1)} custom-call(s32[2]{0:T(128)S(1)} %pad_add_fusion.refs_0_.ids, bf16[528,768]{1,0:T(8,128)(2,1)} %get-tuple-element.106.refs_1_.refs_6_.refs_3_, bf16[2,128,768]{2,1,0:T(8,128)(2,1)} %refs_2_.3, bf16[4,128,768]{2,1,0:T(8,128)(2,1)S(1)} %bitcast.49, ...), custom_call_target="tpu_custom_call" | custom-call | tf_op jit(solution)/shard_map/attention_back_zero/pallas_call | solution.py:134
  271.1 13.9 %collective-permute-start.15 = (bf16[528,768]{1,0:T(8,128)(2,1)S(1)}, bf16[528,768]{1,0:T(8,128)(2,1)S(1)}, u32[]{:S(2)}, u32[]{:S(2)}) collective-permute-start(bf16[528,768]{1,0:T(8,128)(2,1)S(1)} %attention_back_zero.1.refs_5_.refs_1_), channel_id=1, source_target_pairs={{64,0},{65,1},{66,2},{67,3},{68,4},{69,5},{70,6},{71,7},{72,8},{73... | collective-permute-start | bytes 2433032 | tf_op jit(solution)/shard_map/ppermute | solution.py:51
  307.9 7.2 %expert_grads.1 = (f32[2,768,768]{2,1,0:T(8,128)}, f32[2,768,768]{2,1,0:T(8,128)}) custom-call(s32[2]{0:T(128)S(1)} %pad_add_fusion.refs_0_.ids, bf16[2,2,256,768]{3,2,1,0:T(8,128)(2,1)} %get-tuple-element.110.refs_0_, bf16[2,2,256,768]{3,2,1,0:T(8,128)(2,1)} %get-tuple-element.122.refs_1_, bf16[2,2,256,768]{3,2,1,0:T(8,128)(2,1)} %collective-permute-done.11.refs_2_, ...), custom_call_target="tpu_custom_call" | custom-call | tf_op jit(solution)/shard_map/expert_grads/pallas_call | solution.py:812
  (94 shorter events, 88.5 us)
Async XLA Ops:
  7.2 90.5 %all-gather.7.cloned.1.call-start = ((), (), s32[]{:S(2)}) async-start(), calls=%async_computation.10 | async-start | bytes 5591040 | tf_op jit(solution)/shard_map/all_gather | solution.py:609
  14.0 21.3 %all-to-all-start = ((bf16[16,48,512]{2,1,0:T(8,128)(2,1)}), bf16[16,48,512]{2,1,0:T(8,128)(2,1)S(1)}, u32[]{:S(2)}, u32[]{:S(2)}) async-start(bf16[16,48,512]{2,1,0:T(8,128)(2,1)} %spread.1), calls=%async_computation | async-start | bytes 1572864 | tf_op jit(solution)/shard_map/all_to_all | solution.py:586
  22.4 66.1 %collective-permute-start.3 = (bf16[2,768,768]{2,1,0:T(8,128)(2,1)}, bf16[2,768,768]{2,1,0:T(8,128)(2,1)}, u32[]{:S(2)}, u32[]{:S(2)}) collective-permute-start(bf16[2,768,768]{2,1,0:T(8,128)(2,1)} %bitcast.72), channel_id=1, source_target_pairs={{0,64},{64,0},{1,65},{65,1},{2,66},{66,2},{3,67},{67,3},{4,68},{68... | collective-permute-start | bytes 7077896 | tf_op jit(solution)/shard_map/ppermute | solution.py:47
  22.9 65.6 %collective-permute-start.4 = (bf16[2,768,768]{2,1,0:T(8,128)(2,1)}, bf16[2,768,768]{2,1,0:T(8,128)(2,1)}, u32[]{:S(2)}, u32[]{:S(2)}) collective-permute-start(bf16[2,768,768]{2,1,0:T(8,128)(2,1)} %bitcast.76), channel_id=1, source_target_pairs={{0,64},{64,0},{1,65},{65,1},{2,66},{66,2},{3,67},{67,3},{4,68},{68... | collective-permute-start | bytes 7077896 | tf_op jit(solution)/shard_map/ppermute | solution.py:47
  35.2 7.1 %collective-permute-start.2 = (bf16[768,512]{1,0:T(8,128)(2,1)S(1)}, bf16[768,512]{1,0:T(8,128)(2,1)S(1)}, u32[]{:S(2)}, u32[]{:S(2)}) collective-permute-start(bf16[768,512]{1,0:T(8,128)(2,1)S(1)} %bitcast.50), channel_id=1, source_target_pairs={{0,64},{64,0},{1,65},{65,1},{2,66},{66,2},{3,67},{67,3},{4,68},{68... | collective-permute-start | bytes 2359304 | tf_op jit(solution)/shard_map/ppermute | solution.py:47
  38.4 22.1 %all-to-all-start.1 = ((bf16[16,32,768]{2,1,0:T(8,128)(2,1)}), bf16[16,32,768]{2,1,0:T(8,128)(2,1)S(1)}, u32[]{:S(2)}, u32[]{:S(2)}) async-start(bf16[16,32,768]{2,1,0:T(8,128)(2,1)} %bitcast.14), calls=%async_computation.1 | async-start | bytes 1572864 | tf_op jit(solution)/shard_map/all_to_all | solution.py:586
  97.7 11.3 %collective-permute-start.5 = (bf16[4,768,896]{2,1,0:T(8,128)(2,1)}, bf16[4,768,896]{2,1,0:T(8,128)(2,1)}, u32[]{:S(2)}, u32[]{:S(2)}) collective-permute-start(bf16[4,768,896]{2,1,0:T(8,128)(2,1)} %bitcast.65), channel_id=1, source_target_pairs={{0,64},{64,0},{1,65},{65,1},{2,66},{66,2},{3,67},{67,3},{4,68},{68... | collective-permute-start | bytes 16515080 | tf_op jit(solution)/shard_map/ppermute | solution.py:47
  100.0 17.7 %all-to-all-start.3 = ((bf16[16,32,768]{2,1,0:T(8,128)(2,1)}), bf16[16,32,768]{2,1,0:T(8,128)(2,1)S(1)}, u32[]{:S(2)}, u32[]{:S(2)}) async-start(bf16[16,32,768]{2,1,0:T(8,128)(2,1)} %bitcast.20), calls=%async_computation.3 | async-start | bytes 1572864 | tf_op jit(solution)/shard_map/all_to_all | solution.py:586
  138.3 15.3 %all-to-all-start.4 = ((bf16[16,32,768]{2,1,0:T(8,128)(2,1)}), bf16[16,32,768]{2,1,0:T(8,128)(2,1)S(1)}, u32[]{:S(2)}, u32[]{:S(2)}) async-start(bf16[16,32,768]{2,1,0:T(8,128)(2,1)} %bitcast.24), calls=%async_computation.4 | async-start | bytes 1572864 | tf_op jit(solution)/shard_map/all_to_all | solution.py:586
  161.6 17.8 %all-to-all-start.5 = ((bf16[16,32,768]{2,1,0:T(8,128)(2,1)}), bf16[16,32,768]{2,1,0:T(8,128)(2,1)S(1)}, u32[]{:S(2)}, u32[]{:S(2)}) async-start(bf16[16,32,768]{2,1,0:T(8,128)(2,1)} %bitcast.26), calls=%async_computation.5 | async-start | bytes 1572864 | tf_op jit(solution)/shard_map/all_to_all | solution.py:586
  168.2 51.1 %collective-permute-start.11 = (bf16[2,2,256,768]{3,2,1,0:T(8,128)(2,1)}, bf16[2,2,256,768]{3,2,1,0:T(8,128)(2,1)}, u32[]{:S(2)}, u32[]{:S(2)}) collective-permute-start(bf16[2,2,256,768]{3,2,1,0:T(8,128)(2,1)} %get-tuple-element.110.refs_0_), channel_id=1, source_target_pairs={{64,0},{65,1},{66,2},{67,3},{68,4},{69,5},{70,6},{71,7},{72,8},{73... | collective-permute-start | bytes 4718600 | tf_op jit(solution)/shard_map/ppermute | solution.py:51
  176.7 44.6 %collective-permute-start.12 = (bf16[2,2,256,768]{3,2,1,0:T(8,128)(2,1)}, bf16[2,2,256,768]{3,2,1,0:T(8,128)(2,1)}, u32[]{:S(2)}, u32[]{:S(2)}) collective-permute-start(bf16[2,2,256,768]{3,2,1,0:T(8,128)(2,1)} %get-tuple-element.111.refs_4_), channel_id=1, source_target_pairs={{0,64},{1,65},{2,66},{3,67},{4,68},{5,69},{6,70},{7,71},{8,72},{9,... | collective-permute-start | bytes 4718600 | tf_op jit(solution)/shard_map/ppermute | solution.py:51
  178.0 44.6 %collective-permute-start.13 = (bf16[2,2,256,768]{3,2,1,0:T(8,128)(2,1)}, bf16[2,2,256,768]{3,2,1,0:T(8,128)(2,1)}, u32[]{:S(2)}, u32[]{:S(2)}) collective-permute-start(bf16[2,2,256,768]{3,2,1,0:T(8,128)(2,1)} %get-tuple-element.112.refs_5_), channel_id=1, source_target_pairs={{0,64},{1,65},{2,66},{3,67},{4,68},{5,69},{6,70},{7,71},{8,72},{9,... | collective-permute-start | bytes 4718600 | tf_op jit(solution)/shard_map/ppermute | solution.py:51
  179.3 19.0 %all-to-all-start.6 = ((bf16[16,32,768]{2,1,0:T(8,128)(2,1)}), bf16[16,32,768]{2,1,0:T(8,128)(2,1)S(1)}, u32[]{:S(2)}, u32[]{:S(2)}) async-start(bf16[16,32,768]{2,1,0:T(8,128)(2,1)} %bitcast.27), calls=%async_computation.6 | async-start | bytes 1572864 | tf_op jit(solution)/shard_map/all_to_all | solution.py:586
  211.1 17.0 %all-to-all-start.7 = ((bf16[16,32,768]{2,1,0:T(8,128)(2,1)}), bf16[16,32,768]{2,1,0:T(8,128)(2,1)S(1)}, u32[]{:S(2)}, u32[]{:S(2)}) async-start(bf16[16,32,768]{2,1,0:T(8,128)(2,1)} %bitcast.31), calls=%async_computation.7 | async-start | bytes 1572864 | tf_op jit(solution)/shard_map/all_to_all | solution.py:586
  217.8 8.1 %collective-permute-start.6 = (bf16[128,768]{1,0:T(8,128)(2,1)S(1)}, bf16[128,768]{1,0:T(8,128)(2,1)S(1)}, u32[]{:S(2)}, u32[]{:S(2)}) collective-permute-start(bf16[128,768]{1,0:T(8,128)(2,1)S(1)} %combine_one.1.refs_2_), channel_id=1, source_target_pairs={{0,1},{1,2},{2,3},{3,0},{4,5},{5,6},{6,7},{7,4},{8,9},{9,10},{10,1... | collective-permute-start | bytes 589832 | tf_op jit(solution)/shard_map/ppermute | solution.py:742
  218.1 7.8 %collective-permute-start.7 = (bf16[128,768]{1,0:T(8,128)(2,1)S(1)}, bf16[128,768]{1,0:T(8,128)(2,1)S(1)}, u32[]{:S(2)}, u32[]{:S(2)}) collective-permute-start(bf16[128,768]{1,0:T(8,128)(2,1)S(1)} %combine_one.1.refs_2_), channel_id=1, source_target_pairs={{0,2},{1,3},{2,0},{3,1},{4,6},{5,7},{6,4},{7,5},{8,10},{9,11},{10,... | collective-permute-start | bytes 589832 | tf_op jit(solution)/shard_map/ppermute | solution.py:742
  219.3 7.2 %collective-permute-start.8 = (bf16[128,768]{1,0:T(8,128)(2,1)S(1)}, bf16[128,768]{1,0:T(8,128)(2,1)S(1)}, u32[]{:S(2)}, u32[]{:S(2)}) collective-permute-start(bf16[128,768]{1,0:T(8,128)(2,1)S(1)} %combine_one.1.refs_2_), channel_id=1, source_target_pairs={{0,3},{1,0},{2,1},{3,2},{4,7},{5,4},{6,5},{7,6},{8,11},{9,8},{10,9... | collective-permute-start | bytes 589832 | tf_op jit(solution)/shard_map/ppermute | solution.py:742
  221.3 17.7 %collective-permute-start.14 = (bf16[528,768]{1,0:T(8,128)(2,1)S(1)}, bf16[528,768]{1,0:T(8,128)(2,1)}, u32[]{:S(2)}, u32[]{:S(2)}) collective-permute-start(bf16[528,768]{1,0:T(8,128)(2,1)S(1)} %copy-done.3), channel_id=1, source_target_pairs={{0,64},{1,65},{2,66},{3,67},{4,68},{5,69},{6,70},{7,71},{8,72},{9,... | collective-permute-start | bytes 2433032 | tf_op jit(solution)/shard_map/ppermute | solution.py:51
  233.9 15.4 %all-to-all-start.8 = ((bf16[16,32,768]{2,1,0:T(8,128)(2,1)}), bf16[16,32,768]{2,1,0:T(8,128)(2,1)S(1)}, u32[]{:S(2)}, u32[]{:S(2)}) async-start(bf16[16,32,768]{2,1,0:T(8,128)(2,1)} %bitcast.33), calls=%async_computation.8 | async-start | bytes 1572864 | tf_op jit(solution)/shard_map/all_to_all | solution.py:586
  271.1 15.8 %collective-permute-start.15 = (bf16[528,768]{1,0:T(8,128)(2,1)S(1)}, bf16[528,768]{1,0:T(8,128)(2,1)S(1)}, u32[]{:S(2)}, u32[]{:S(2)}) collective-permute-start(bf16[528,768]{1,0:T(8,128)(2,1)S(1)} %attention_back_zero.1.refs_5_.refs_1_), channel_id=1, source_target_pairs={{64,0},{65,1},{66,2},{67,3},{68,4},{69,5},{70,6},{71,7},{72,8},{73... | collective-permute-start | bytes 2433032 | tf_op jit(solution)/shard_map/ppermute | solution.py:51
  290.8 17.0 %collective-permute-start.16 = (bf16[2,2,256,768]{3,2,1,0:T(8,128)(2,1)}, bf16[2,2,256,768]{3,2,1,0:T(8,128)(2,1)}, u32[]{:S(2)}, u32[]{:S(2)}) collective-permute-start(bf16[2,2,256,768]{3,2,1,0:T(8,128)(2,1)} %get-tuple-element.122.refs_1_), channel_id=1, source_target_pairs={{64,0},{65,1},{66,2},{67,3},{68,4},{69,5},{70,6},{71,7},{72,8},{73... | collective-permute-start | bytes 4718600 | tf_op jit(solution)/shard_map/ppermute | solution.py:51
  293.4 23.8 %all-to-all-start.9 = ((bf16[16,48,896]{2,1,0:T(8,128)(2,1)}), bf16[16,48,896]{2,1,0:T(8,128)(2,1)S(1)}, u32[]{:S(2)}, u32[]{:S(2)}) async-start(bf16[16,48,896]{2,1,0:T(8,128)(2,1)} %attention_grads.1), calls=%async_computation.9 | async-start | bytes 2752512 | tf_op jit(solution)/shard_map/all_to_all | solution.py:586
  297.2 4.3 %collective-permute-start.9 = (bf16[128,768]{1,0:T(8,128)(2,1)S(1)}, bf16[128,768]{1,0:T(8,128)(2,1)S(1)}, u32[]{:S(2)}, u32[]{:S(2)}) collective-permute-start(bf16[128,768]{1,0:T(8,128)(2,1)S(1)} %copy-done.4), channel_id=1, source_target_pairs={{64,0},{65,1},{66,2},{67,3},{68,4},{69,5},{70,6},{71,7},{72,8},{73... | collective-permute-start | bytes 589832 | tf_op jit(solution)/shard_map/ppermute | solution.py:51
  (13 other events, 128.2 us)
Sparse Core Ops, SparseCore 0:
  11.5 86.2 all-gather.6

commit v4 on v3

--- a/solution.py
+++ b/solution.py
@@ -161,8 +161,8 @@
         for i in range(count):
             pltpu.make_async_copy(other.at[i, :, lanes], buffer.at[i], sems.at[i]).start()
 
-    def arrived():
-        for i in range(count):
+    def arrived(start=0, stop=count):
+        for i in range(start, stop):
             pltpu.make_async_copy(own.at[i, :, lanes], buffer.at[i], sems.at[i]).wait()
 
     return arrived
@@ -310,8 +310,9 @@
     normed_out[...] = normed
     normed_out.start()
     attn = None
-    arrived()
     for part in range(4):
+        if part % 2 == 0:
+            arrived(part, part + 2)
         proj = dot(normed, weights[part, :, : 3 * SPLIT]).astype(bf16)
         proj_out[part] = proj
         proj_out.start(part)
@@ -358,26 +359,37 @@
         slope_in, arrived_grad, in_own, in_other, out_own, out_other, buf_out, behind = refs[:8]
     w_in, w_out, in_sems, out_sems = refs[-4:]
     here = ids[0] == layer
+    if mode != "forward":
+        backs = [rows_of(arrived_grad, e) for e in range(2)]
     if mode == "backward":
         out_arrived = fetch(here, out_own, out_other, w_out, out_sems)
         in_arrived = fetch(here, in_own, in_other, w_in, in_sems)
         slopes = [slope_in[e].astype(f32) for e in range(2)]
+        for e in range(2):
+            behind[1, e] = backs[e]
+        behind.start(1)
         out_arrived()
     else:
         in_arrived = fetch(here, in_own, in_other, w_in, in_sems)
         out_arrived = fetch(here, out_own, out_other, w_out, out_sems)
+        acts, slopes = [], []
+        for e in range(2):
+            ahead[0, e] = rows_of(received, e)
+        ahead.start(0)
+        if mode == "both":
+            for e in range(2):
+                behind[1, e] = backs[e]
+            behind.start(1)
         in_arrived()
-        acts, slopes = [], []
         for e in range(2):
             rows = rows_of(received, e)
             value, slope = gelu_both(dot(rows, w_in[e]))
             acts.append(value.astype(bf16))
             slopes.append(slope)
-            ahead[0, e] = rows
             ahead[1, e] = acts[e]
             if mode == "forward":
                 slope_out[e] = slope.astype(bf16)
-        ahead.start()
+        ahead.start(1)
         if mode == "forward":
             slope_out.start()
         out_arrived()
@@ -386,11 +398,9 @@
     if mode != "forward":
         pres = []
         for e in range(2):
-            back = rows_of(arrived_grad, e)
-            pres.append((dot_nt(back, w_out[e]) * slopes[e]).astype(bf16))
+            pres.append((dot_nt(backs[e], w_out[e]) * slopes[e]).astype(bf16))
             behind[0, e] = pres[e]
-            behind[1, e] = back
-        behind.start()
+        behind.start(0)
         if mode == "backward":
             in_arrived()
         for e in range(2):
@@ -448,8 +458,9 @@
     bundle[0:TOK] = normed_ref[...]
     bundle[TOK : 2 * TOK] = attn_low
     normed_grad = None
-    arrived()
     for part in range(4):
+        if part % 2 == 0:
+            arrived(part, part + 2)
         context_grad = dot(attn_low, weights[part, :, 512:WIDTH]).astype(bf16)
         proj = proj_ref[part]
         q_parts, k_parts, v_parts = [], [], []
@@ -478,8 +489,6 @@
     inner = jnp.mean(unit * gain_one * normed_grad, axis=-1, keepdims=True)
     low = (middle_grad + scale_one * (gain_one * normed_grad - unit * inner)).astype(bf16)
     bundle[3 * TOK : 4 * TOK] = low
-    if layer == 1:
-        sent_out[...] = dot_tn(gated[...], low).astype(bf16)
     bundle[2 * TOK : 3 * TOK] = jnp.concatenate([all_proj[device], context_ref[...]], axis=1)
     flip = jnp.where(iota((TOK, TOK), 0) + iota((TOK, TOK), 1) == TOK - 1, 1.0, 0.0).astype(bf16)
     for head in range(HEADS):
@@ -487,6 +496,9 @@
         lined = pltpu.roll(flipped, 1, 1, stride=1, stride_axis=0)
         small_out[2 + head : 3 + head, 0:TOK] = jnp.sum(lined, axis=0, keepdims=True)
     bundle[4 * TOK :] = small_out[...].astype(bf16)
+    if layer == 1:
+        bundle.start()
+        sent_out[...] = dot_tn(gated[...], low).astype(bf16)
 
 
 def weight_grad_kernel(ids, zero, zero_peer, one, one_peer, onehot, out, buffer, sems):
@@ -783,7 +795,8 @@
         name="experts_back_zero",
         limit=20,
     )
-    buf_back_zero = after(exchanged(buf_zero), back_one_peer)
+    state_zero_peer, state_one_peer = sent(state_zero, 1), sent(state_one, 0)
+    buf_back_zero = after(exchanged(buf_zero), back_one_peer, state_zero_peer, state_one_peer)
     buf_parts_zero = gathered_mp(combined(pick_zero, buf_back_zero, "combine_back_zero"))
     back_zero = call(
         functools.partial(backward_kernel, 0),
@@ -830,7 +843,7 @@
         [((2, TOK, WIDTH), bf16)] * 2,
         load=(1, 3, 4, 5, 6, 7, 8),
         args=(
-            ids, state_zero, state_one, sent(state_zero, 1), sent(state_one, 0), back_zero, back_one, back_zero_peer,
+            ids, state_zero, state_one, state_zero_peer, state_one_peer, back_zero, back_one, back_zero_peer,
             back_one_peer
         ),
         name="assemble",

time: 326 us -> 327 us (level)
  starting transfers between devices: 91.7 us -> 95.9 us
  waiting for transfers between devices: 45 us -> 41.5 us
    ppermute x9, starting transfers between devices: 32.8 us -> 37.4 us  [sent(): return lax.ppermute(x, 'section', [(source, 1 - source)])]
    all_to_all x9, waiting for transfers between devices: 24.3 us -> 20.9 us  [exchanged(): lax.all_to_all(x.reshape(16, -1, x.shape[-1]), 'dp', 0, 0, tiled=True)]
  transfers between devices with their start and end apart: 27 -> 27, of which waited for: 13 -> 12; matrix products, arithmetic and copies ran while one was open for 0% -> 0% of each run, Pallas kernels for 20% -> 19%
where the time goes in v4:
time: 327 us; the launch traced here: 325 us
  Pallas kernels  97.8 us (30%)
  starting transfers between devices  95.9 us (29%)
  blocking collectives  73.8 us (23%)
  waiting for transfers between devices  41.5 us (13%)
  between operations  14.6 us (4%)
    pallas_call x22, Pallas kernels, call(): pl.pallas_call(wrapped, out_shape=[pltpu.HBM(shape, dtype) if i in store...  90.6 us
    all_to_all x9, starting transfers between devices, exchanged(): lax.all_to_all(x.reshape(16, -1, x.shape[-1]), 'dp', 0, 0, tiled=True)  48.5 us
    all_gather x4, blocking collectives, gathered_mp(): return lax.all_gather(x, 'mp', axis=0)  48.4 us
    ppermute x9, starting transfers between devices, sent(): return lax.ppermute(x, 'section', [(source, 1 - source)])  37.4 us
    all_to_all x1, blocking collectives, exchanged(): lax.all_to_all(x.reshape(16, -1, x.shape[-1]), 'dp', 0, 0, tiled=True)  25.4 us
    all_to_all x9, waiting for transfers between devices, exchanged(): lax.all_to_all(x.reshape(16, -1, x.shape[-1]), 'dp', 0, 0, tiled=True)  20.9 us
    ppermute x5, waiting for transfers between devices, swapped(): return lax.ppermute(x, 'section', [(0, 1), (1, 0)])  8.25 us
    pallas_call x1, Pallas kernels, body(): pl.pallas_call(expert_grad_kernel, out_shape=[jax.ShapeDtypeStruct((2, WI...  7.19 us
  transfers between devices with their start and end apart: 27, of which 12 were waited for; matrix products, arithmetic and copies ran while one was open for 0% of the time, Pallas kernels for 19%

profile of v4, /device:TPU:1, one launch (start us, length us, event | category | flops | bytes accessed | tf_op | source)
XLA Modules:
  0.0 325.2 jit_solution(12971559980839878361)
XLA Ops:
  14.0 8.3 %all-to-all-start = ((bf16[16,48,512]{2,1,0:T(8,128)(2,1)}), bf16[16,48,512]{2,1,0:T(8,128)(2,1)S(1)}, u32[]{:S(2)}, u32[]{:S(2)}) async-start(bf16[16,48,512]{2,1,0:T(8,128)(2,1)} %spread.1), calls=%async_computation | async-start | bytes 1572864 | tf_op jit(solution)/shard_map/all_to_all | solution.py:598
  30.0 5.2 %all-to-all-done = bf16[16,48,512]{2,1,0:T(8,128)(2,1)S(1)} async-done(((bf16[16,48,512]{2,1,0:T(8,128)(2,1)}), bf16[16,48,512]{2,1,0:T(8,128)(2,1)S(1)}, u32[]{:S(2)}, u32[]{:S(2)}) %all-to-all-start) | async-done | bytes 786464 | tf_op jit(solution)/shard_map/all_to_all | solution.py:598
  46.0 14.5 %all-gather = bf16[512,768]{1,0:T(8,128)(2,1)S(1)} all-gather(bf16[128,768]{1,0:T(8,128)(2,1)S(1)} %get-tuple-element.73), channel_id=2, replica_groups=mesh['section'=2,'dp'=16,'mp'=4] {'mp'}, dimensions={0}, use_global_device_ids=true | all-gather | bytes 983040 | tf_op jit(solution)/shard_map/all_gather | solution.py:602
  63.0 25.4 %all_to_all.50 = bf16[16,32,768]{2,1,0:T(8,128)(2,1)S(1)} all-to-all(bf16[16,32,768]{2,1,0:T(8,128)(2,1)S(1)} %bitcast.63), channel_id=1, replica_groups=mesh['section'=2,'dp'=16,'mp'=4] {'dp'}, dimensions={0} | all-to-all | bytes 1572864 | tf_op jit(solution)/shard_map/all_to_all | solution.py:598
  88.5 6.6 %experts_zero.1 = (bf16[16,2,16,768]{3,2,1,0:T(8,128)(2,1)}, bf16[2,2,256,768]{3,2,1,0:T(8,128)(2,1)}, bf16[2,256,768]{2,1,0:T(8,128)(2,1)}) custom-call(s32[2]{0:T(128)S(1)} %pad_add_fusion.refs_0_.ids, bf16[16,2,16,768]{3,2,1,0:T(8,128)(2,1)S(1)} %bitcast.52, bf16[2,768,768]{2,1,0:T(8,128)(2,1)} %bitcast.73, ...), custom_call_target="tpu_custom_call" | custom-call | tf_op jit(solution)/shard_map/experts_zero/pallas_call | solution.py:134
  112.7 4.9 %all-to-all-done.3 = bf16[16,32,768]{2,1,0:T(8,128)(2,1)S(1)} async-done(((bf16[16,32,768]{2,1,0:T(8,128)(2,1)}), bf16[16,32,768]{2,1,0:T(8,128)(2,1)S(1)}, u32[]{:S(2)}, u32[]{:S(2)}) %all-to-all-start.3) | async-done | bytes 786464 | tf_op jit(solution)/shard_map/all_to_all | solution.py:598
  117.9 11.0 %all-gather.2 = bf16[512,768]{1,0:T(8,128)(2,1)S(1)} all-gather(bf16[128,768]{1,0:T(8,128)(2,1)S(1)} %combine_zero.1), channel_id=4, replica_groups=mesh['section'=2,'dp'=16,'mp'=4] {'mp'}, dimensions={0}, use_global_device_ids=true | all-gather | bytes 983040 | tf_op jit(solution)/shard_map/all_gather | solution.py:602
  128.9 9.6 %attention_one.1 = (bf16[128,768]{1,0:T(8,128)(2,1)}, bf16[512,768]{1,0:T(8,128)(2,1)}, f32[128,768]{1,0:T(8,128)}, bf16[128,768]{1,0:T(8,128)(2,1)}, bf16[4,128...) custom-call(s32[2]{0:T(128)S(1)} %pad_add_fusion.refs_0_.ids, ...), custom_call_target="tpu_custom_call" | custom-call | tf_op jit(solution)/shard_map/attention_one/pallas_call | solution.py:134
  146.7 6.7 %attention_zero.1 = (bf16[128,768]{1,0:T(8,128)(2,1)}, bf16[4,128,576]{2,1,0:T(8,128)(2,1)}, bf16[12,128,128]{2,1,0:T(8,128)(2,1)}, bf16[128,192]{1,0:T(8,128)(2,1)}) custom-call(s32[2]{0:T(128)S(1)} %pad_add_fusion.refs_0_.ids, bf16[2,128,768]{2,1,0:T(8,128)(2,1)} %refs_2_.3, bf16[4,768,896]{2,1,0:T(8,128)(2,1)} %bitcast.69, ...), custom_call_target="tpu_custom_call" | custom-call | tf_op jit(solution)/shard_map/attention_zero/pallas_call | solution.py:134
  153.4 8.1 %experts_one.1 = (bf16[16,2,16,768]{3,2,1,0:T(8,128)(2,1)}, bf16[16,2,16,768]{3,2,1,0:T(8,128)(2,1)}, bf16[2,2,256,768]{3,2,1,0:T(8,128)(2,1)}, bf16[2,2,256,768]{3,2,1,0:T(8,128)(2,1)}) custom-call(s32[2]{0:T(128)S(1)} %pad_add_fusion.refs_0_.ids, bf16[16,2,16,768]{3,2,1,0:T(8,128)(2,1)S(1)} %bitcast.62, bf16[16,2,16,768]{3,2,1,0:T(8,128)(2,1)S(1)} %bitcast.60, ...), custom_call_target="tpu_custom_call" | custom-call | tf_op jit(solution)/shard_map/experts_one/pallas_call | solution.py:134
  161.6 6.6 %all-to-all-start.5 = ((bf16[16,32,768]{2,1,0:T(8,128)(2,1)}), bf16[16,32,768]{2,1,0:T(8,128)(2,1)S(1)}, u32[]{:S(2)}, u32[]{:S(2)}) async-start(bf16[16,32,768]{2,1,0:T(8,128)(2,1)} %bitcast.26), calls=%async_computation.5 | async-start | bytes 1572864 | tf_op jit(solution)/shard_map/all_to_all | solution.py:598
  168.2 8.5 %collective-permute-start.11 = (bf16[2,2,256,768]{3,2,1,0:T(8,128)(2,1)}, bf16[2,2,256,768]{3,2,1,0:T(8,128)(2,1)}, u32[]{:S(2)}, u32[]{:S(2)}) collective-permute-start(bf16[2,2,256,768]{3,2,1,0:T(8,128)(2,1)} %get-tuple-element.110.refs_0_), channel_id=1, source_target_pairs={{64,0},{65,1},{66,2},{67,3},{68,4},{69,5},{70,6},{71,7},{72,8},{73... | collective-permute-start | bytes 4718600 | tf_op jit(solution)/shard_map/ppermute | solution.py:51
  179.2 6.9 %all-to-all-start.6 = ((bf16[16,32,768]{2,1,0:T(8,128)(2,1)}), bf16[16,32,768]{2,1,0:T(8,128)(2,1)S(1)}, u32[]{:S(2)}, u32[]{:S(2)}) async-start(bf16[16,32,768]{2,1,0:T(8,128)(2,1)} %bitcast.27), calls=%async_computation.6 | async-start | bytes 1572864 | tf_op jit(solution)/shard_map/all_to_all | solution.py:598
  186.5 11.8 %all-gather.3 = bf16[512,768]{1,0:T(8,128)(2,1)S(1)} all-gather(bf16[128,768]{1,0:T(8,128)(2,1)S(1)} %combine_back_one.1), channel_id=5, replica_groups=mesh['section'=2,'dp'=16,'mp'=4] {'mp'}, dimensions={0}, use_global_device_ids=true | all-gather | bytes 983040 | tf_op jit(solution)/shard_map/all_gather | solution.py:602
  198.5 12.6 %attention_back_one.1 = (bf16[512,768]{1,0:T(8,128)(2,1)}, bf16[528,768]{1,0:T(8,128)(2,1)}) custom-call(s32[2]{0:T(128)S(1)} %pad_add_fusion.refs_0_.ids, bf16[2,128,768]{2,1,0:T(8,128)(2,1)} %refs_1_.7, bf16[128,768]{1,0:T(8,128)(2,1)} %get-tuple-element.90.refs_2_.refs_1_, bf16[4,128,768]{2,1,0:T(8,128)(2,1)S(1)} %bitcast.55, ...), custom_call_target="tpu_custom_call" | custom-call | tf_op jit(solution)/shard_map/attention_back_one/pallas_call | solution.py:134
  211.1 6.1 %all-to-all-start.7 = ((bf16[16,32,768]{2,1,0:T(8,128)(2,1)}), bf16[16,32,768]{2,1,0:T(8,128)(2,1)S(1)}, u32[]{:S(2)}, u32[]{:S(2)}) async-start(bf16[16,32,768]{2,1,0:T(8,128)(2,1)} %bitcast.31), calls=%async_computation.7 | async-start | bytes 1572864 | tf_op jit(solution)/shard_map/all_to_all | solution.py:598
  227.6 5.5 %experts_back_zero.1 = (bf16[16,2,16,768]{3,2,1,0:T(8,128)(2,1)}, bf16[2,2,256,768]{3,2,1,0:T(8,128)(2,1)}) custom-call(s32[2]{0:T(128)S(1)} %pad_add_fusion.refs_0_.ids, bf16[2,256,768]{2,1,0:T(8,128)(2,1)} %get-tuple-element.107.refs_1_, bf16[16,2,16,768]{3,2,1,0:T(8,128)(2,1)S(1)} %bitcast.61, bf16[2,768,768]{2,1,0:T(8,128)(2,1)} %bitcast.75, ...), custom_call_target="tpu_custom_call" | custom-call | tf_op jit(solution)/shard_map/experts_back_zero/pallas_call | solution.py:134
  233.1 5.2 %all-to-all-start.8 = ((bf16[16,32,768]{2,1,0:T(8,128)(2,1)}), bf16[16,32,768]{2,1,0:T(8,128)(2,1)S(1)}, u32[]{:S(2)}, u32[]{:S(2)}) async-start(bf16[16,32,768]{2,1,0:T(8,128)(2,1)} %bitcast.33), calls=%async_computation.8 | async-start | bytes 1572864 | tf_op jit(solution)/shard_map/all_to_all | solution.py:598
  238.3 10.1 %collective-permute-start.9 = (bf16[128,768]{1,0:T(8,128)(2,1)S(1)}, bf16[128,768]{1,0:T(8,128)(2,1)S(1)}, u32[]{:S(2)}, u32[]{:S(2)}) collective-permute-start(bf16[128,768]{1,0:T(8,128)(2,1)S(1)} %copy-done.5), channel_id=1, source_target_pairs={{64,0},{65,1},{66,2},{67,3},{68,4},{69,5},{70,6},{71,7},{72,8},{73... | collective-permute-start | bytes 589832 | tf_op jit(solution)/shard_map/ppermute | solution.py:51
  254.4 11.0 %all-gather.4 = bf16[512,768]{1,0:T(8,128)(2,1)S(1)} all-gather(bf16[128,768]{1,0:T(8,128)(2,1)S(1)} %combine_back_zero.1), channel_id=6, replica_groups=mesh['section'=2,'dp'=16,'mp'=4] {'mp'}, dimensions={0}, use_global_device_ids=true | all-gather | bytes 983040 | tf_op jit(solution)/shard_map/all_gather | solution.py:602
  265.4 10.0 %attention_back_zero.1.refs_5_.refs_1_ = bf16[528,768]{1,0:T(8,128)(2,1)S(1)} custom-call(s32[2]{0:T(128)S(1)} %pad_add_fusion.refs_0_.ids, bf16[528,768]{1,0:T(8,128)(2,1)} %get-tuple-element.106.refs_1_.refs_6_.refs_3_, bf16[2,128,768]{2,1,0:T(8,128)(2,1)} %refs_2_.3, bf16[4,128,768]{2,1,0:T(8,128)(2,1)S(1)} %bitcast.49, ...), custom_call_target="tpu_custom_call" | custom-call | tf_op jit(solution)/shard_map/attention_back_zero/pallas_call | solution.py:134
  275.5 9.9 %collective-permute-start.15 = (bf16[528,768]{1,0:T(8,128)(2,1)S(1)}, bf16[528,768]{1,0:T(8,128)(2,1)S(1)}, u32[]{:S(2)}, u32[]{:S(2)}) collective-permute-start(bf16[528,768]{1,0:T(8,128)(2,1)S(1)} %attention_back_zero.1.refs_5_.refs_1_), channel_id=1, source_target_pairs={{64,0},{65,1},{66,2},{67,3},{68,4},{69,5},{70,6},{71,7},{72,8},{73... | collective-permute-start | bytes 2433032 | tf_op jit(solution)/shard_map/ppermute | solution.py:51
  301.1 7.2 %expert_grads.1 = (f32[2,768,768]{2,1,0:T(8,128)}, f32[2,768,768]{2,1,0:T(8,128)}) custom-call(s32[2]{0:T(128)S(1)} %pad_add_fusion.refs_0_.ids, bf16[2,2,256,768]{3,2,1,0:T(8,128)(2,1)} %get-tuple-element.110.refs_0_, bf16[2,2,256,768]{3,2,1,0:T(8,128)(2,1)} %get-tuple-element.122.refs_1_, bf16[2,2,256,768]{3,2,1,0:T(8,128)(2,1)} %collective-permute-done.11.refs_2_, ...), custom_call_target="tpu_custom_call" | custom-call | tf_op jit(solution)/shard_map/expert_grads/pallas_call | solution.py:825
  308.3 9.1 %all-to-all-done.9.refs_0_ = bf16[16,48,896]{2,1,0:T(8,128)(2,1)S(1)} async-done(((bf16[16,48,896]{2,1,0:T(8,128)(2,1)}), bf16[16,48,896]{2,1,0:T(8,128)(2,1)S(1)}, u32[]{:S(2)}, u32[]{:S(2)}) %all-to-all-start.9) | async-done | bytes 1376288 | tf_op jit(solution)/shard_map/all_to_all | solution.py:598
  (96 shorter events, 89.6 us)
Async XLA Ops:
  7.2 90.5 %all-gather.7.cloned.1.call-start = ((), (), s32[]{:S(2)}) async-start(), calls=%async_computation.10 | async-start | bytes 5591040 | tf_op jit(solution)/shard_map/all_gather | solution.py:621
  14.0 21.3 %all-to-all-start = ((bf16[16,48,512]{2,1,0:T(8,128)(2,1)}), bf16[16,48,512]{2,1,0:T(8,128)(2,1)S(1)}, u32[]{:S(2)}, u32[]{:S(2)}) async-start(bf16[16,48,512]{2,1,0:T(8,128)(2,1)} %spread.1), calls=%async_computation | async-start | bytes 1572864 | tf_op jit(solution)/shard_map/all_to_all | solution.py:598
  22.4 66.1 %collective-permute-start.3 = (bf16[2,768,768]{2,1,0:T(8,128)(2,1)}, bf16[2,768,768]{2,1,0:T(8,128)(2,1)}, u32[]{:S(2)}, u32[]{:S(2)}) collective-permute-start(bf16[2,768,768]{2,1,0:T(8,128)(2,1)} %bitcast.72), channel_id=1, source_target_pairs={{0,64},{64,0},{1,65},{65,1},{2,66},{66,2},{3,67},{67,3},{4,68},{68... | collective-permute-start | bytes 7077896 | tf_op jit(solution)/shard_map/ppermute | solution.py:47
  22.9 65.6 %collective-permute-start.4 = (bf16[2,768,768]{2,1,0:T(8,128)(2,1)}, bf16[2,768,768]{2,1,0:T(8,128)(2,1)}, u32[]{:S(2)}, u32[]{:S(2)}) collective-permute-start(bf16[2,768,768]{2,1,0:T(8,128)(2,1)} %bitcast.76), channel_id=1, source_target_pairs={{0,64},{64,0},{1,65},{65,1},{2,66},{66,2},{3,67},{67,3},{4,68},{68... | collective-permute-start | bytes 7077896 | tf_op jit(solution)/shard_map/ppermute | solution.py:47
  35.2 7.1 %collective-permute-start.2 = (bf16[768,512]{1,0:T(8,128)(2,1)S(1)}, bf16[768,512]{1,0:T(8,128)(2,1)S(1)}, u32[]{:S(2)}, u32[]{:S(2)}) collective-permute-start(bf16[768,512]{1,0:T(8,128)(2,1)S(1)} %bitcast.50), channel_id=1, source_target_pairs={{0,64},{64,0},{1,65},{65,1},{2,66},{66,2},{3,67},{67,3},{4,68},{68... | collective-permute-start | bytes 2359304 | tf_op jit(solution)/shard_map/ppermute | solution.py:47
  38.4 22.1 %all-to-all-start.1 = ((bf16[16,32,768]{2,1,0:T(8,128)(2,1)}), bf16[16,32,768]{2,1,0:T(8,128)(2,1)S(1)}, u32[]{:S(2)}, u32[]{:S(2)}) async-start(bf16[16,32,768]{2,1,0:T(8,128)(2,1)} %bitcast.14), calls=%async_computation.1 | async-start | bytes 1572864 | tf_op jit(solution)/shard_map/all_to_all | solution.py:598
  97.7 11.3 %collective-permute-start.5 = (bf16[4,768,896]{2,1,0:T(8,128)(2,1)}, bf16[4,768,896]{2,1,0:T(8,128)(2,1)}, u32[]{:S(2)}, u32[]{:S(2)}) collective-permute-start(bf16[4,768,896]{2,1,0:T(8,128)(2,1)} %bitcast.65), channel_id=1, source_target_pairs={{0,64},{64,0},{1,65},{65,1},{2,66},{66,2},{3,67},{67,3},{4,68},{68... | collective-permute-start | bytes 16515080 | tf_op jit(solution)/shard_map/ppermute | solution.py:47
  100.0 17.6 %all-to-all-start.3 = ((bf16[16,32,768]{2,1,0:T(8,128)(2,1)}), bf16[16,32,768]{2,1,0:T(8,128)(2,1)S(1)}, u32[]{:S(2)}, u32[]{:S(2)}) async-start(bf16[16,32,768]{2,1,0:T(8,128)(2,1)} %bitcast.20), calls=%async_computation.3 | async-start | bytes 1572864 | tf_op jit(solution)/shard_map/all_to_all | solution.py:598
  138.5 14.9 %all-to-all-start.4 = ((bf16[16,32,768]{2,1,0:T(8,128)(2,1)}), bf16[16,32,768]{2,1,0:T(8,128)(2,1)S(1)}, u32[]{:S(2)}, u32[]{:S(2)}) async-start(bf16[16,32,768]{2,1,0:T(8,128)(2,1)} %bitcast.24), calls=%async_computation.4 | async-start | bytes 1572864 | tf_op jit(solution)/shard_map/all_to_all | solution.py:598
  161.6 17.7 %all-to-all-start.5 = ((bf16[16,32,768]{2,1,0:T(8,128)(2,1)}), bf16[16,32,768]{2,1,0:T(8,128)(2,1)S(1)}, u32[]{:S(2)}, u32[]{:S(2)}) async-start(bf16[16,32,768]{2,1,0:T(8,128)(2,1)} %bitcast.26), calls=%async_computation.5 | async-start | bytes 1572864 | tf_op jit(solution)/shard_map/all_to_all | solution.py:598
  168.2 50.9 %collective-permute-start.11 = (bf16[2,2,256,768]{3,2,1,0:T(8,128)(2,1)}, bf16[2,2,256,768]{3,2,1,0:T(8,128)(2,1)}, u32[]{:S(2)}, u32[]{:S(2)}) collective-permute-start(bf16[2,2,256,768]{3,2,1,0:T(8,128)(2,1)} %get-tuple-element.110.refs_0_), channel_id=1, source_target_pairs={{64,0},{65,1},{66,2},{67,3},{68,4},{69,5},{70,6},{71,7},{72,8},{73... | collective-permute-start | bytes 4718600 | tf_op jit(solution)/shard_map/ppermute | solution.py:51
  176.6 44.3 %collective-permute-start.12 = (bf16[2,2,256,768]{3,2,1,0:T(8,128)(2,1)}, bf16[2,2,256,768]{3,2,1,0:T(8,128)(2,1)}, u32[]{:S(2)}, u32[]{:S(2)}) collective-permute-start(bf16[2,2,256,768]{3,2,1,0:T(8,128)(2,1)} %get-tuple-element.111.refs_4_), channel_id=1, source_target_pairs={{0,64},{1,65},{2,66},{3,67},{4,68},{5,69},{6,70},{7,71},{8,72},{9,... | collective-permute-start | bytes 4718600 | tf_op jit(solution)/shard_map/ppermute | solution.py:51
  177.9 44.3 %collective-permute-start.13 = (bf16[2,2,256,768]{3,2,1,0:T(8,128)(2,1)}, bf16[2,2,256,768]{3,2,1,0:T(8,128)(2,1)}, u32[]{:S(2)}, u32[]{:S(2)}) collective-permute-start(bf16[2,2,256,768]{3,2,1,0:T(8,128)(2,1)} %get-tuple-element.112.refs_5_), channel_id=1, source_target_pairs={{0,64},{1,65},{2,66},{3,67},{4,68},{5,69},{6,70},{7,71},{8,72},{9,... | collective-permute-start | bytes 4718600 | tf_op jit(solution)/shard_map/ppermute | solution.py:51
  179.2 19.0 %all-to-all-start.6 = ((bf16[16,32,768]{2,1,0:T(8,128)(2,1)}), bf16[16,32,768]{2,1,0:T(8,128)(2,1)S(1)}, u32[]{:S(2)}, u32[]{:S(2)}) async-start(bf16[16,32,768]{2,1,0:T(8,128)(2,1)} %bitcast.27), calls=%async_computation.6 | async-start | bytes 1572864 | tf_op jit(solution)/shard_map/all_to_all | solution.py:598
  211.1 16.5 %all-to-all-start.7 = ((bf16[16,32,768]{2,1,0:T(8,128)(2,1)}), bf16[16,32,768]{2,1,0:T(8,128)(2,1)S(1)}, u32[]{:S(2)}, u32[]{:S(2)}) async-start(bf16[16,32,768]{2,1,0:T(8,128)(2,1)} %bitcast.31), calls=%async_computation.7 | async-start | bytes 1572864 | tf_op jit(solution)/shard_map/all_to_all | solution.py:598
  217.2 8.1 %collective-permute-start.6 = (bf16[128,768]{1,0:T(8,128)(2,1)S(1)}, bf16[128,768]{1,0:T(8,128)(2,1)S(1)}, u32[]{:S(2)}, u32[]{:S(2)}) collective-permute-start(bf16[128,768]{1,0:T(8,128)(2,1)S(1)} %combine_one.1.refs_2_), channel_id=1, source_target_pairs={{0,1},{1,2},{2,3},{3,0},{4,5},{5,6},{6,7},{7,4},{8,9},{9,10},{10,1... | collective-permute-start | bytes 589832 | tf_op jit(solution)/shard_map/ppermute | solution.py:754
  217.5 7.8 %collective-permute-start.7 = (bf16[128,768]{1,0:T(8,128)(2,1)S(1)}, bf16[128,768]{1,0:T(8,128)(2,1)S(1)}, u32[]{:S(2)}, u32[]{:S(2)}) collective-permute-start(bf16[128,768]{1,0:T(8,128)(2,1)S(1)} %combine_one.1.refs_2_), channel_id=1, source_target_pairs={{0,2},{1,3},{2,0},{3,1},{4,6},{5,7},{6,4},{7,5},{8,10},{9,11},{10,... | collective-permute-start | bytes 589832 | tf_op jit(solution)/shard_map/ppermute | solution.py:754
  219.1 6.9 %collective-permute-start.8 = (bf16[128,768]{1,0:T(8,128)(2,1)S(1)}, bf16[128,768]{1,0:T(8,128)(2,1)S(1)}, u32[]{:S(2)}, u32[]{:S(2)}) collective-permute-start(bf16[128,768]{1,0:T(8,128)(2,1)S(1)} %combine_one.1.refs_2_), channel_id=1, source_target_pairs={{0,3},{1,0},{2,1},{3,2},{4,7},{5,4},{6,5},{7,6},{8,11},{9,8},{10,9... | collective-permute-start | bytes 589832 | tf_op jit(solution)/shard_map/ppermute | solution.py:754
  220.9 32.5 %collective-permute-start.14 = (bf16[528,768]{1,0:T(8,128)(2,1)S(1)}, bf16[528,768]{1,0:T(8,128)(2,1)}, u32[]{:S(2)}, u32[]{:S(2)}) collective-permute-start(bf16[528,768]{1,0:T(8,128)(2,1)S(1)} %copy-done.3), channel_id=1, source_target_pairs={{0,64},{1,65},{2,66},{3,67},{4,68},{5,69},{6,70},{7,71},{8,72},{9,... | collective-permute-start | bytes 2433032 | tf_op jit(solution)/shard_map/ppermute | solution.py:51
  233.1 20.4 %all-to-all-start.8 = ((bf16[16,32,768]{2,1,0:T(8,128)(2,1)}), bf16[16,32,768]{2,1,0:T(8,128)(2,1)S(1)}, u32[]{:S(2)}, u32[]{:S(2)}) async-start(bf16[16,32,768]{2,1,0:T(8,128)(2,1)} %bitcast.33), calls=%async_computation.8 | async-start | bytes 1572864 | tf_op jit(solution)/shard_map/all_to_all | solution.py:598
  238.3 13.1 %collective-permute-start.9 = (bf16[128,768]{1,0:T(8,128)(2,1)S(1)}, bf16[128,768]{1,0:T(8,128)(2,1)S(1)}, u32[]{:S(2)}, u32[]{:S(2)}) collective-permute-start(bf16[128,768]{1,0:T(8,128)(2,1)S(1)} %copy-done.5), channel_id=1, source_target_pairs={{64,0},{65,1},{66,2},{67,3},{68,4},{69,5},{70,6},{71,7},{72,8},{73... | collective-permute-start | bytes 589832 | tf_op jit(solution)/shard_map/ppermute | solution.py:51
  275.5 11.8 %collective-permute-start.15 = (bf16[528,768]{1,0:T(8,128)(2,1)S(1)}, bf16[528,768]{1,0:T(8,128)(2,1)S(1)}, u32[]{:S(2)}, u32[]{:S(2)}) collective-permute-start(bf16[528,768]{1,0:T(8,128)(2,1)S(1)} %attention_back_zero.1.refs_5_.refs_1_), channel_id=1, source_target_pairs={{64,0},{65,1},{66,2},{67,3},{68,4},{69,5},{70,6},{71,7},{72,8},{73... | collective-permute-start | bytes 2433032 | tf_op jit(solution)/shard_map/ppermute | solution.py:51
  291.2 9.9 %collective-permute-start.16 = (bf16[2,2,256,768]{3,2,1,0:T(8,128)(2,1)S(1)}, bf16[2,2,256,768]{3,2,1,0:T(8,128)(2,1)}, u32[]{:S(2)}, u32[]{:S(2)}) collective-permute-start(bf16[2,2,256,768]{3,2,1,0:T(8,128)(2,1)S(1)} %copy-done.4), channel_id=1, source_target_pairs={{64,0},{65,1},{66,2},{67,3},{68,4},{69,5},{70,6},{71,7},{72,8},{73... | collective-permute-start | bytes 4718600 | tf_op jit(solution)/shard_map/ppermute | solution.py:51
  293.7 23.7 %all-to-all-start.9 = ((bf16[16,48,896]{2,1,0:T(8,128)(2,1)}), bf16[16,48,896]{2,1,0:T(8,128)(2,1)S(1)}, u32[]{:S(2)}, u32[]{:S(2)}) async-start(bf16[16,48,896]{2,1,0:T(8,128)(2,1)} %attention_grads.1), calls=%async_computation.9 | async-start | bytes 2752512 | tf_op jit(solution)/shard_map/all_to_all | solution.py:598
  (14 other events, 138.4 us)
Sparse Core Ops, SparseCore 0:
  11.5 86.2 all-gather.6

commit v5 on v4

--- a/solution.py
+++ b/solution.py
@@ -796,7 +796,8 @@
         limit=20,
     )
     state_zero_peer, state_one_peer = sent(state_zero, 1), sent(state_one, 0)
-    buf_back_zero = after(exchanged(buf_zero), back_one_peer, state_zero_peer, state_one_peer)
+    behind_zero_peer = sent(after(behind_zero, state_one), 1)
+    buf_back_zero = after(exchanged(buf_zero), back_one_peer, state_zero_peer, state_one_peer, behind_zero_peer)
     buf_parts_zero = gathered_mp(combined(pick_zero, buf_back_zero, "combine_back_zero"))
     back_zero = call(
         functools.partial(backward_kernel, 0),
@@ -821,7 +822,6 @@
         name="attention_grads",
     )[0]
     shares = exchanged(packed)
-    behind_zero_peer = sent(after(behind_zero, packed), 1)
     in_grad, out_grad = pl.pallas_call(
         expert_grad_kernel,
         out_shape=[jax.ShapeDtypeStruct((2, WIDTH, WIDTH), f32)] * 2,

time: 327 us -> 339 us (1.037)
  waiting for transfers between devices: 41.5 us -> 56 us
  starting transfers between devices: 95.9 us -> 92.5 us
    ppermute x3, waiting for transfers between devices: 3.72 us -> 12.9 us  [body(): lax.ppermute(y_part_one, 'mp', [(i, (i + by) % 4) for i in range(4)])]
    all_to_all x9, waiting for transfers between devices: 20.9 us -> 26.2 us  [exchanged(): lax.all_to_all(x.reshape(16, -1, x.shape[-1]), 'dp', 0, 0, tiled=True)]
  transfers between devices with their start and end apart: 27 -> 27, of which waited for: 12 -> 12; matrix products, arithmetic and copies ran while one was open for 0% -> 0% of each run, Pallas kernels for 19% -> 17%
where the time goes in v5:
time: 339 us; the launch traced here: 338 us
  Pallas kernels  97.9 us (29%)
  starting transfers between devices  92.5 us (27%)
  blocking collectives  75 us (22%)
  waiting for transfers between devices  56 us (17%)
  between operations  14.6 us (4%)
    pallas_call x22, Pallas kernels, call(): pl.pallas_call(wrapped, out_shape=[pltpu.HBM(shape, dtype) if i in store...  90.8 us
    all_to_all x9, starting transfers between devices, exchanged(): lax.all_to_all(x.reshape(16, -1, x.shape[-1]), 'dp', 0, 0, tiled=True)  50.1 us
    all_gather x4, blocking collectives, gathered_mp(): return lax.all_gather(x, 'mp', axis=0)  49.6 us
    ppermute x9, starting transfers between devices, sent(): return lax.ppermute(x, 'section', [(source, 1 - source)])  34.4 us
    all_to_all x9, waiting for transfers between devices, exchanged(): lax.all_to_all(x.reshape(16, -1, x.shape[-1]), 'dp', 0, 0, tiled=True)  26.2 us
    all_to_all x1, blocking collectives, exchanged(): lax.all_to_all(x.reshape(16, -1, x.shape[-1]), 'dp', 0, 0, tiled=True)  25.4 us
    ppermute x3, waiting for transfers between devices, body(): lax.ppermute(y_part_one, 'mp', [(i, (i + by) % 4) for i in range(4)])  12.9 us
    ppermute x5, waiting for transfers between devices, swapped(): return lax.ppermute(x, 'section', [(0, 1), (1, 0)])  8.25 us
  transfers between devices with their start and end apart: 27, of which 12 were waited for; matrix products, arithmetic and copies ran while one was open for 0% of the time, Pallas kernels for 17%

profile of v5, /device:TPU:1, one launch (start us, length us, event | category | flops | bytes accessed | tf_op | source)
XLA Modules:
  0.0 337.7 jit_solution(12250141389127997781)
XLA Ops:
  14.0 8.3 %all-to-all-start = ((bf16[16,48,512]{2,1,0:T(8,128)(2,1)}), bf16[16,48,512]{2,1,0:T(8,128)(2,1)S(1)}, u32[]{:S(2)}, u32[]{:S(2)}) async-start(bf16[16,48,512]{2,1,0:T(8,128)(2,1)} %spread.1), calls=%async_computation | async-start | bytes 1572864 | tf_op jit(solution)/shard_map/all_to_all | solution.py:598
  46.0 14.5 %all-gather = bf16[512,768]{1,0:T(8,128)(2,1)S(1)} all-gather(bf16[128,768]{1,0:T(8,128)(2,1)S(1)} %get-tuple-element.73), channel_id=2, replica_groups=mesh['section'=2,'dp'=16,'mp'=4] {'mp'}, dimensions={0}, use_global_device_ids=true | all-gather | bytes 983040 | tf_op jit(solution)/shard_map/all_gather | solution.py:602
  63.0 25.4 %all_to_all.50 = bf16[16,32,768]{2,1,0:T(8,128)(2,1)S(1)} all-to-all(bf16[16,32,768]{2,1,0:T(8,128)(2,1)S(1)} %bitcast.63), channel_id=1, replica_groups=mesh['section'=2,'dp'=16,'mp'=4] {'dp'}, dimensions={0} | all-to-all | bytes 1572864 | tf_op jit(solution)/shard_map/all_to_all | solution.py:598
  88.5 6.6 %experts_zero.1 = (bf16[16,2,16,768]{3,2,1,0:T(8,128)(2,1)}, bf16[2,2,256,768]{3,2,1,0:T(8,128)(2,1)}, bf16[2,256,768]{2,1,0:T(8,128)(2,1)}) custom-call(s32[2]{0:T(128)S(1)} %pad_add_fusion.refs_0_.ids, bf16[16,2,16,768]{3,2,1,0:T(8,128)(2,1)S(1)} %bitcast.52, bf16[2,768,768]{2,1,0:T(8,128)(2,1)} %bitcast.73, ...), custom_call_target="tpu_custom_call" | custom-call | tf_op jit(solution)/shard_map/experts_zero/pallas_call | solution.py:134
  117.9 11.0 %all-gather.2 = bf16[512,768]{1,0:T(8,128)(2,1)S(1)} all-gather(bf16[128,768]{1,0:T(8,128)(2,1)S(1)} %combine_zero.1), channel_id=4, replica_groups=mesh['section'=2,'dp'=16,'mp'=4] {'mp'}, dimensions={0}, use_global_device_ids=true | all-gather | bytes 983040 | tf_op jit(solution)/shard_map/all_gather | solution.py:602
  128.9 9.6 %attention_one.1 = (bf16[128,768]{1,0:T(8,128)(2,1)}, bf16[512,768]{1,0:T(8,128)(2,1)}, f32[128,768]{1,0:T(8,128)}, bf16[128,768]{1,0:T(8,128)(2,1)}, bf16[4,128...) custom-call(s32[2]{0:T(128)S(1)} %pad_add_fusion.refs_0_.ids, ...), custom_call_target="tpu_custom_call" | custom-call | tf_op jit(solution)/shard_map/attention_one/pallas_call | solution.py:134
  146.7 6.8 %attention_zero.1 = (bf16[128,768]{1,0:T(8,128)(2,1)}, bf16[4,128,576]{2,1,0:T(8,128)(2,1)}, bf16[12,128,128]{2,1,0:T(8,128)(2,1)}, bf16[128,192]{1,0:T(8,128)(2,1)}) custom-call(s32[2]{0:T(128)S(1)} %pad_add_fusion.refs_0_.ids, bf16[2,128,768]{2,1,0:T(8,128)(2,1)} %refs_2_.3, bf16[4,768,896]{2,1,0:T(8,128)(2,1)} %bitcast.69, ...), custom_call_target="tpu_custom_call" | custom-call | tf_op jit(solution)/shard_map/attention_zero/pallas_call | solution.py:134
  153.5 8.1 %experts_one.1 = (bf16[16,2,16,768]{3,2,1,0:T(8,128)(2,1)}, bf16[16,2,16,768]{3,2,1,0:T(8,128)(2,1)}, bf16[2,2,256,768]{3,2,1,0:T(8,128)(2,1)}, bf16[2,2,256,768]{3,2,1,0:T(8,128)(2,1)}) custom-call(s32[2]{0:T(128)S(1)} %pad_add_fusion.refs_0_.ids, bf16[16,2,16,768]{3,2,1,0:T(8,128)(2,1)S(1)} %bitcast.62, bf16[16,2,16,768]{3,2,1,0:T(8,128)(2,1)S(1)} %bitcast.60, ...), custom_call_target="tpu_custom_call" | custom-call | tf_op jit(solution)/shard_map/experts_one/pallas_call | solution.py:134
  161.6 6.6 %all-to-all-start.5 = ((bf16[16,32,768]{2,1,0:T(8,128)(2,1)}), bf16[16,32,768]{2,1,0:T(8,128)(2,1)S(1)}, u32[]{:S(2)}, u32[]{:S(2)}) async-start(bf16[16,32,768]{2,1,0:T(8,128)(2,1)} %bitcast.26), calls=%async_computation.5 | async-start | bytes 1572864 | tf_op jit(solution)/shard_map/all_to_all | solution.py:598
  168.2 8.4 %collective-permute-start.11 = (bf16[2,2,256,768]{3,2,1,0:T(8,128)(2,1)}, bf16[2,2,256,768]{3,2,1,0:T(8,128)(2,1)}, u32[]{:S(2)}, u32[]{:S(2)}) collective-permute-start(bf16[2,2,256,768]{3,2,1,0:T(8,128)(2,1)} %get-tuple-element.110.refs_0_), channel_id=1, source_target_pairs={{64,0},{65,1},{66,2},{67,3},{68,4},{69,5},{70,6},{71,7},{72,8},{73... | collective-permute-start | bytes 4718600 | tf_op jit(solution)/shard_map/ppermute | solution.py:51
  179.3 6.9 %all-to-all-start.6 = ((bf16[16,32,768]{2,1,0:T(8,128)(2,1)}), bf16[16,32,768]{2,1,0:T(8,128)(2,1)S(1)}, u32[]{:S(2)}, u32[]{:S(2)}) async-start(bf16[16,32,768]{2,1,0:T(8,128)(2,1)} %bitcast.27), calls=%async_computation.6 | async-start | bytes 1572864 | tf_op jit(solution)/shard_map/all_to_all | solution.py:598
  186.5 11.7 %all-gather.3 = bf16[512,768]{1,0:T(8,128)(2,1)S(1)} all-gather(bf16[128,768]{1,0:T(8,128)(2,1)S(1)} %combine_back_one.1), channel_id=5, replica_groups=mesh['section'=2,'dp'=16,'mp'=4] {'mp'}, dimensions={0}, use_global_device_ids=true | all-gather | bytes 983040 | tf_op jit(solution)/shard_map/all_gather | solution.py:602
  198.5 12.5 %attention_back_one.1 = (bf16[512,768]{1,0:T(8,128)(2,1)}, bf16[528,768]{1,0:T(8,128)(2,1)}) custom-call(s32[2]{0:T(128)S(1)} %pad_add_fusion.refs_0_.ids, bf16[2,128,768]{2,1,0:T(8,128)(2,1)} %refs_1_.7, bf16[128,768]{1,0:T(8,128)(2,1)} %get-tuple-element.90.refs_2_.refs_1_, bf16[4,128,768]{2,1,0:T(8,128)(2,1)S(1)} %bitcast.55, ...), custom_call_target="tpu_custom_call" | custom-call | tf_op jit(solution)/shard_map/attention_back_one/pallas_call | solution.py:134
  211.1 6.2 %all-to-all-start.7 = ((bf16[16,32,768]{2,1,0:T(8,128)(2,1)}), bf16[16,32,768]{2,1,0:T(8,128)(2,1)S(1)}, u32[]{:S(2)}, u32[]{:S(2)}) async-start(bf16[16,32,768]{2,1,0:T(8,128)(2,1)} %bitcast.31), calls=%async_computation.7 | async-start | bytes 1572864 | tf_op jit(solution)/shard_map/all_to_all | solution.py:598
  219.0 6.4 %collective-permute-done.6.refs_3_ = bf16[128,768]{1,0:T(8,128)(2,1)S(1)} collective-permute-done((bf16[128,768]{1,0:T(8,128)(2,1)S(1)}, bf16[128,768]{1,0:T(8,128)(2,1)S(1)}, u32[]{:S(2)}, u32[]{:S(2)}) %collective-permute-start.6) | collective-permute-done | bytes 196640 | tf_op jit(solution)/shard_map/ppermute | solution.py:754
  225.4 6.5 %collective-permute-done.8.refs_5_ = bf16[128,768]{1,0:T(8,128)(2,1)S(1)} collective-permute-done((bf16[128,768]{1,0:T(8,128)(2,1)S(1)}, bf16[128,768]{1,0:T(8,128)(2,1)S(1)}, u32[]{:S(2)}, u32[]{:S(2)}) %collective-permute-start.8) | collective-permute-done | bytes 196640 | tf_op jit(solution)/shard_map/ppermute | solution.py:754
  233.6 5.5 %experts_back_zero.1 = (bf16[16,2,16,768]{3,2,1,0:T(8,128)(2,1)}, bf16[2,2,256,768]{3,2,1,0:T(8,128)(2,1)}) custom-call(s32[2]{0:T(128)S(1)} %pad_add_fusion.refs_0_.ids, bf16[2,256,768]{2,1,0:T(8,128)(2,1)} %get-tuple-element.107.refs_1_, bf16[16,2,16,768]{3,2,1,0:T(8,128)(2,1)S(1)} %bitcast.61, bf16[2,768,768]{2,1,0:T(8,128)(2,1)} %bitcast.75, ...), custom_call_target="tpu_custom_call" | custom-call | tf_op jit(solution)/shard_map/experts_back_zero/pallas_call | solution.py:134
  239.1 9.8 %collective-permute-start.15 = (bf16[2,2,256,768]{3,2,1,0:T(8,128)(2,1)}, bf16[2,2,256,768]{3,2,1,0:T(8,128)(2,1)}, u32[]{:S(2)}, u32[]{:S(2)}) collective-permute-start(bf16[2,2,256,768]{3,2,1,0:T(8,128)(2,1)} %get-tuple-element.116.refs_1_), channel_id=1, source_target_pairs={{64,0},{65,1},{66,2},{67,3},{68,4},{69,5},{70,6},{71,7},{72,8},{73... | collective-permute-start | bytes 4718600 | tf_op jit(solution)/shard_map/ppermute | solution.py:51
  250.2 6.7 %all-to-all-start.8 = ((bf16[16,32,768]{2,1,0:T(8,128)(2,1)}), bf16[16,32,768]{2,1,0:T(8,128)(2,1)S(1)}, u32[]{:S(2)}, u32[]{:S(2)}) async-start(bf16[16,32,768]{2,1,0:T(8,128)(2,1)} %bitcast.33), calls=%async_computation.8 | async-start | bytes 1572864 | tf_op jit(solution)/shard_map/all_to_all | solution.py:598
  269.9 12.3 %all-gather.4 = bf16[512,768]{1,0:T(8,128)(2,1)S(1)} all-gather(bf16[128,768]{1,0:T(8,128)(2,1)S(1)} %combine_back_zero.1), channel_id=6, replica_groups=mesh['section'=2,'dp'=16,'mp'=4] {'mp'}, dimensions={0}, use_global_device_ids=true | all-gather | bytes 983040 | tf_op jit(solution)/shard_map/all_gather | solution.py:602
  282.3 10.1 %attention_back_zero.1.refs_5_.refs_1_ = bf16[528,768]{1,0:T(8,128)(2,1)S(1)} custom-call(s32[2]{0:T(128)S(1)} %pad_add_fusion.refs_0_.ids, bf16[528,768]{1,0:T(8,128)(2,1)} %get-tuple-element.106.refs_1_.refs_6_.refs_3_, bf16[2,128,768]{2,1,0:T(8,128)(2,1)} %refs_2_.3, bf16[4,128,768]{2,1,0:T(8,128)(2,1)S(1)} %bitcast.49, ...), custom_call_target="tpu_custom_call" | custom-call | tf_op jit(solution)/shard_map/attention_back_zero/pallas_call | solution.py:134
  292.4 6.3 %collective-permute-start.16 = (bf16[528,768]{1,0:T(8,128)(2,1)S(1)}, bf16[528,768]{1,0:T(8,128)(2,1)S(1)}, u32[]{:S(2)}, u32[]{:S(2)}) collective-permute-start(bf16[528,768]{1,0:T(8,128)(2,1)S(1)} %attention_back_zero.1.refs_5_.refs_1_), channel_id=1, source_target_pairs={{64,0},{65,1},{66,2},{67,3},{68,4},{69,5},{70,6},{71,7},{72,8},{73... | collective-permute-start | bytes 2433032 | tf_op jit(solution)/shard_map/ppermute | solution.py:51
  308.3 7.2 %expert_grads.1 = (f32[2,768,768]{2,1,0:T(8,128)}, f32[2,768,768]{2,1,0:T(8,128)}) custom-call(s32[2]{0:T(128)S(1)} %pad_add_fusion.refs_0_.ids, bf16[2,2,256,768]{3,2,1,0:T(8,128)(2,1)} %get-tuple-element.110.refs_0_, bf16[2,2,256,768]{3,2,1,0:T(8,128)(2,1)} %get-tuple-element.116.refs_1_, bf16[2,2,256,768]{3,2,1,0:T(8,128)(2,1)} %collective-permute-done.11.refs_2_, ...), custom_call_target="tpu_custom_call" | custom-call | tf_op jit(solution)/shard_map/expert_grads/pallas_call | solution.py:825
  319.2 10.7 %all-to-all-done.9.refs_0_ = bf16[16,48,896]{2,1,0:T(8,128)(2,1)S(1)} async-done(((bf16[16,48,896]{2,1,0:T(8,128)(2,1)}), bf16[16,48,896]{2,1,0:T(8,128)(2,1)S(1)}, u32[]{:S(2)}, u32[]{:S(2)}) %all-to-all-start.9) | async-done | bytes 1376288 | tf_op jit(solution)/shard_map/all_to_all | solution.py:598
  (96 shorter events, 98.8 us)
Async XLA Ops:
  7.2 90.5 %all-gather.7.cloned.1.call-start = ((), (), s32[]{:S(2)}) async-start(), calls=%async_computation.10 | async-start | bytes 5591040 | tf_op jit(solution)/shard_map/all_gather | solution.py:621
  14.0 21.3 %all-to-all-start = ((bf16[16,48,512]{2,1,0:T(8,128)(2,1)}), bf16[16,48,512]{2,1,0:T(8,128)(2,1)S(1)}, u32[]{:S(2)}, u32[]{:S(2)}) async-start(bf16[16,48,512]{2,1,0:T(8,128)(2,1)} %spread.1), calls=%async_computation | async-start | bytes 1572864 | tf_op jit(solution)/shard_map/all_to_all | solution.py:598
  22.4 66.1 %collective-permute-start.3 = (bf16[2,768,768]{2,1,0:T(8,128)(2,1)}, bf16[2,768,768]{2,1,0:T(8,128)(2,1)}, u32[]{:S(2)}, u32[]{:S(2)}) collective-permute-start(bf16[2,768,768]{2,1,0:T(8,128)(2,1)} %bitcast.72), channel_id=1, source_target_pairs={{0,64},{64,0},{1,65},{65,1},{2,66},{66,2},{3,67},{67,3},{4,68},{68... | collective-permute-start | bytes 7077896 | tf_op jit(solution)/shard_map/ppermute | solution.py:47
  22.9 65.6 %collective-permute-start.4 = (bf16[2,768,768]{2,1,0:T(8,128)(2,1)}, bf16[2,768,768]{2,1,0:T(8,128)(2,1)}, u32[]{:S(2)}, u32[]{:S(2)}) collective-permute-start(bf16[2,768,768]{2,1,0:T(8,128)(2,1)} %bitcast.76), channel_id=1, source_target_pairs={{0,64},{64,0},{1,65},{65,1},{2,66},{66,2},{3,67},{67,3},{4,68},{68... | collective-permute-start | bytes 7077896 | tf_op jit(solution)/shard_map/ppermute | solution.py:47
  35.2 7.1 %collective-permute-start.2 = (bf16[768,512]{1,0:T(8,128)(2,1)S(1)}, bf16[768,512]{1,0:T(8,128)(2,1)S(1)}, u32[]{:S(2)}, u32[]{:S(2)}) collective-permute-start(bf16[768,512]{1,0:T(8,128)(2,1)S(1)} %bitcast.50), channel_id=1, source_target_pairs={{0,64},{64,0},{1,65},{65,1},{2,66},{66,2},{3,67},{67,3},{4,68},{68... | collective-permute-start | bytes 2359304 | tf_op jit(solution)/shard_map/ppermute | solution.py:47
  38.4 22.1 %all-to-all-start.1 = ((bf16[16,32,768]{2,1,0:T(8,128)(2,1)}), bf16[16,32,768]{2,1,0:T(8,128)(2,1)S(1)}, u32[]{:S(2)}, u32[]{:S(2)}) async-start(bf16[16,32,768]{2,1,0:T(8,128)(2,1)} %bitcast.14), calls=%async_computation.1 | async-start | bytes 1572864 | tf_op jit(solution)/shard_map/all_to_all | solution.py:598
  97.7 11.3 %collective-permute-start.5 = (bf16[4,768,896]{2,1,0:T(8,128)(2,1)}, bf16[4,768,896]{2,1,0:T(8,128)(2,1)}, u32[]{:S(2)}, u32[]{:S(2)}) collective-permute-start(bf16[4,768,896]{2,1,0:T(8,128)(2,1)} %bitcast.65), channel_id=1, source_target_pairs={{0,64},{64,0},{1,65},{65,1},{2,66},{66,2},{3,67},{67,3},{4,68},{68... | collective-permute-start | bytes 16515080 | tf_op jit(solution)/shard_map/ppermute | solution.py:47
  100.0 17.6 %all-to-all-start.3 = ((bf16[16,32,768]{2,1,0:T(8,128)(2,1)}), bf16[16,32,768]{2,1,0:T(8,128)(2,1)S(1)}, u32[]{:S(2)}, u32[]{:S(2)}) async-start(bf16[16,32,768]{2,1,0:T(8,128)(2,1)} %bitcast.20), calls=%async_computation.3 | async-start | bytes 1572864 | tf_op jit(solution)/shard_map/all_to_all | solution.py:598
  138.6 14.9 %all-to-all-start.4 = ((bf16[16,32,768]{2,1,0:T(8,128)(2,1)}), bf16[16,32,768]{2,1,0:T(8,128)(2,1)S(1)}, u32[]{:S(2)}, u32[]{:S(2)}) async-start(bf16[16,32,768]{2,1,0:T(8,128)(2,1)} %bitcast.24), calls=%async_computation.4 | async-start | bytes 1572864 | tf_op jit(solution)/shard_map/all_to_all | solution.py:598
  161.6 17.6 %all-to-all-start.5 = ((bf16[16,32,768]{2,1,0:T(8,128)(2,1)}), bf16[16,32,768]{2,1,0:T(8,128)(2,1)S(1)}, u32[]{:S(2)}, u32[]{:S(2)}) async-start(bf16[16,32,768]{2,1,0:T(8,128)(2,1)} %bitcast.26), calls=%async_computation.5 | async-start | bytes 1572864 | tf_op jit(solution)/shard_map/all_to_all | solution.py:598
  168.2 65.3 %collective-permute-start.11 = (bf16[2,2,256,768]{3,2,1,0:T(8,128)(2,1)}, bf16[2,2,256,768]{3,2,1,0:T(8,128)(2,1)}, u32[]{:S(2)}, u32[]{:S(2)}) collective-permute-start(bf16[2,2,256,768]{3,2,1,0:T(8,128)(2,1)} %get-tuple-element.110.refs_0_), channel_id=1, source_target_pairs={{64,0},{65,1},{66,2},{67,3},{68,4},{69,5},{70,6},{71,7},{72,8},{73... | collective-permute-start | bytes 4718600 | tf_op jit(solution)/shard_map/ppermute | solution.py:51
  176.7 56.9 %collective-permute-start.12 = (bf16[2,2,256,768]{3,2,1,0:T(8,128)(2,1)}, bf16[2,2,256,768]{3,2,1,0:T(8,128)(2,1)}, u32[]{:S(2)}, u32[]{:S(2)}) collective-permute-start(bf16[2,2,256,768]{3,2,1,0:T(8,128)(2,1)} %get-tuple-element.111.refs_4_), channel_id=1, source_target_pairs={{0,64},{1,65},{2,66},{3,67},{4,68},{5,69},{6,70},{7,71},{8,72},{9,... | collective-permute-start | bytes 4718600 | tf_op jit(solution)/shard_map/ppermute | solution.py:51
  178.0 55.6 %collective-permute-start.13 = (bf16[2,2,256,768]{3,2,1,0:T(8,128)(2,1)}, bf16[2,2,256,768]{3,2,1,0:T(8,128)(2,1)}, u32[]{:S(2)}, u32[]{:S(2)}) collective-permute-start(bf16[2,2,256,768]{3,2,1,0:T(8,128)(2,1)} %get-tuple-element.112.refs_5_), channel_id=1, source_target_pairs={{0,64},{1,65},{2,66},{3,67},{4,68},{5,69},{6,70},{7,71},{8,72},{9,... | collective-permute-start | bytes 4718600 | tf_op jit(solution)/shard_map/ppermute | solution.py:51
  179.3 18.9 %all-to-all-start.6 = ((bf16[16,32,768]{2,1,0:T(8,128)(2,1)}), bf16[16,32,768]{2,1,0:T(8,128)(2,1)S(1)}, u32[]{:S(2)}, u32[]{:S(2)}) async-start(bf16[16,32,768]{2,1,0:T(8,128)(2,1)} %bitcast.27), calls=%async_computation.6 | async-start | bytes 1572864 | tf_op jit(solution)/shard_map/all_to_all | solution.py:598
  211.1 22.5 %all-to-all-start.7 = ((bf16[16,32,768]{2,1,0:T(8,128)(2,1)}), bf16[16,32,768]{2,1,0:T(8,128)(2,1)S(1)}, u32[]{:S(2)}, u32[]{:S(2)}) async-start(bf16[16,32,768]{2,1,0:T(8,128)(2,1)} %bitcast.31), calls=%async_computation.7 | async-start | bytes 1572864 | tf_op jit(solution)/shard_map/all_to_all | solution.py:598
  217.2 8.1 %collective-permute-start.6 = (bf16[128,768]{1,0:T(8,128)(2,1)S(1)}, bf16[128,768]{1,0:T(8,128)(2,1)S(1)}, u32[]{:S(2)}, u32[]{:S(2)}) collective-permute-start(bf16[128,768]{1,0:T(8,128)(2,1)S(1)} %combine_one.1.refs_2_), channel_id=1, source_target_pairs={{0,1},{1,2},{2,3},{3,0},{4,5},{5,6},{6,7},{7,4},{8,9},{9,10},{10,1... | collective-permute-start | bytes 589832 | tf_op jit(solution)/shard_map/ppermute | solution.py:754
  217.5 7.8 %collective-permute-start.7 = (bf16[128,768]{1,0:T(8,128)(2,1)S(1)}, bf16[128,768]{1,0:T(8,128)(2,1)S(1)}, u32[]{:S(2)}, u32[]{:S(2)}) collective-permute-start(bf16[128,768]{1,0:T(8,128)(2,1)S(1)} %combine_one.1.refs_2_), channel_id=1, source_target_pairs={{0,2},{1,3},{2,0},{3,1},{4,6},{5,7},{6,4},{7,5},{8,10},{9,11},{10,... | collective-permute-start | bytes 589832 | tf_op jit(solution)/shard_map/ppermute | solution.py:754
  225.4 6.5 %collective-permute-start.8 = (bf16[128,768]{1,0:T(8,128)(2,1)S(1)}, bf16[128,768]{1,0:T(8,128)(2,1)S(1)}, u32[]{:S(2)}, u32[]{:S(2)}) collective-permute-start(bf16[128,768]{1,0:T(8,128)(2,1)S(1)} %combine_one.1.refs_2_), channel_id=1, source_target_pairs={{0,3},{1,0},{2,1},{3,2},{4,7},{5,4},{6,5},{7,6},{8,11},{9,8},{10,9... | collective-permute-start | bytes 589832 | tf_op jit(solution)/shard_map/ppermute | solution.py:754
  239.1 30.6 %collective-permute-start.15 = (bf16[2,2,256,768]{3,2,1,0:T(8,128)(2,1)}, bf16[2,2,256,768]{3,2,1,0:T(8,128)(2,1)}, u32[]{:S(2)}, u32[]{:S(2)}) collective-permute-start(bf16[2,2,256,768]{3,2,1,0:T(8,128)(2,1)} %get-tuple-element.116.refs_1_), channel_id=1, source_target_pairs={{64,0},{65,1},{66,2},{67,3},{68,4},{69,5},{70,6},{71,7},{72,8},{73... | collective-permute-start | bytes 4718600 | tf_op jit(solution)/shard_map/ppermute | solution.py:51
  248.9 15.4 %collective-permute-start.14 = (bf16[528,768]{1,0:T(8,128)(2,1)S(1)}, bf16[528,768]{1,0:T(8,128)(2,1)S(1)}, u32[]{:S(2)}, u32[]{:S(2)}) collective-permute-start(bf16[528,768]{1,0:T(8,128)(2,1)S(1)} %copy-done.3), channel_id=1, source_target_pairs={{0,64},{1,65},{2,66},{3,67},{4,68},{5,69},{6,70},{7,71},{8,72},{9,... | collective-permute-start | bytes 2433032 | tf_op jit(solution)/shard_map/ppermute | solution.py:51
  250.2 19.5 %all-to-all-start.8 = ((bf16[16,32,768]{2,1,0:T(8,128)(2,1)}), bf16[16,32,768]{2,1,0:T(8,128)(2,1)S(1)}, u32[]{:S(2)}, u32[]{:S(2)}) async-start(bf16[16,32,768]{2,1,0:T(8,128)(2,1)} %bitcast.33), calls=%async_computation.8 | async-start | bytes 1572864 | tf_op jit(solution)/shard_map/all_to_all | solution.py:598
  256.9 4.7 %collective-permute-start.9 = (bf16[128,768]{1,0:T(8,128)(2,1)S(1)}, bf16[128,768]{1,0:T(8,128)(2,1)S(1)}, u32[]{:S(2)}, u32[]{:S(2)}) collective-permute-start(bf16[128,768]{1,0:T(8,128)(2,1)S(1)} %copy-done.5), channel_id=1, source_target_pairs={{64,0},{65,1},{66,2},{67,3},{68,4},{69,5},{70,6},{71,7},{72,8},{73... | collective-permute-start | bytes 589832 | tf_op jit(solution)/shard_map/ppermute | solution.py:51
  292.4 8.2 %collective-permute-start.16 = (bf16[528,768]{1,0:T(8,128)(2,1)S(1)}, bf16[528,768]{1,0:T(8,128)(2,1)S(1)}, u32[]{:S(2)}, u32[]{:S(2)}) collective-permute-start(bf16[528,768]{1,0:T(8,128)(2,1)S(1)} %attention_back_zero.1.refs_5_.refs_1_), channel_id=1, source_target_pairs={{64,0},{65,1},{66,2},{67,3},{68,4},{69,5},{70,6},{71,7},{72,8},{73... | collective-permute-start | bytes 2433032 | tf_op jit(solution)/shard_map/ppermute | solution.py:51
  304.6 25.4 %all-to-all-start.9 = ((bf16[16,48,896]{2,1,0:T(8,128)(2,1)}), bf16[16,48,896]{2,1,0:T(8,128)(2,1)S(1)}, u32[]{:S(2)}, u32[]{:S(2)}) async-start(bf16[16,48,896]{2,1,0:T(8,128)(2,1)} %attention_grads.1), calls=%async_computation.9 | async-start | bytes 2752512 | tf_op jit(solution)/shard_map/all_to_all | solution.py:598
  (14 other events, 184.0 us)
Sparse Core Ops, SparseCore 0:
  11.5 86.2 all-gather.6
